TPU v7x, 128 devices: a whole 4x4x4 slice. The times are simulated.
128 devices in a mesh: space: 16 (over z_lo, y, core), vec: 8 (over x, z_hi).
Axes of the slice: x: 4, y: 4, z: 4 (z_hi: 2, z_lo: 2; z = z_hi * 2 + z_lo), core: 2. Of those that a mesh axis runs over, the one named last changes fastest.
Arguments:
- vectors: float32 [192, 3, 16, 4096], P('vec', None, 'space'), may hold values from -6 to 6
- labels: int32 [16, 4096], P('space'), may hold values from 0 to 3
- stiffness: float32 [4, 3, 3, 3], replicated, may hold values from -0.45 to 8, as said below
- mass: float32 [4], replicated, may hold values from 0.5 to 2
Outputs:
- refined: float32 [192, 3, 16, 4096], P('vec', None, 'space')
- rayleigh: float32 [2, 192, 192], P(None, 'vec')
Inputs may be any that keep to these rules, and one draw needn't show every extreme that they name: `stiffness`: each 3 x 3 coupling is symmetric, with diagonal entries larger than the sum of the magnitudes of the other entries of their row.
All inputs are finite; a program needn't handle non-finite values.
Results may differ from a plain program's by a relative error of at most 0.0001.
Values sent between devices are 32-bit elements; how exact they have to be, the bound alone decides.
No kernel may reach another device: no remote copies, remote signals or barrier semaphores. Data moves between devices by JAX's collectives and lax.ppermute only.
A program may use at most 128 MiB of HBM per device.

v0:
```python
import functools

import jax
import jax.numpy as jnp
from jax import lax
from jax.experimental import pallas as pl
from jax.experimental.pallas import tpu as pltpu
from jax.sharding import PartitionSpec as P

NX = 64
LANES = 128
SUB = 8
LEVELS = 4
BLOCK = 64
STEP = 8
ORDER = (0, 7, 5, 3, 4, 1, 6, 2)
ENTRIES = ((0, 0), (0, 1), (0, 2), (1, 1), (1, 2), (2, 2))
ENTRY_OF = {pair: i for i, pair in enumerate(ENTRIES)}
VMEM_LIMIT = 48 * 1024 * 1024
SPACE = (2, 4, 2)
VEC = (4, 2)
TILE = 64
PAIRS = ((0, 0), (1, 0), (1, 1), (2, 0), (2, 1), (2, 2))


def rows_of(device):
    x, far = device // VEC[1], device % VEC[1]
    return x + far * (2 * VEC[0] - 1 - 2 * x)


DEVICE_OF = sorted(range(VEC[0] * VEC[1]), key=rows_of)


def route(array, move):
    pairs = []
    for zl in range(SPACE[0]):
        for y in range(SPACE[1]):
            for core in range(SPACE[2]):
                for x in range(VEC[0]):
                    for zh in range(VEC[1]):
                        a, b, c, d, e = move(zl, y, core, x, zh)
                        here = (((zl * SPACE[1] + y) * SPACE[2] + core) * VEC[0] + x) * VEC[1] + zh
                        there = (((a * SPACE[1] + b) * SPACE[2] + c) * VEC[0] + d) * VEC[1] + e
                        pairs.append((here, there))
    return lax.ppermute(array, ("space", "vec"), pairs)


def step_along(array, axis, by):
    order = DEVICE_OF if axis == "vec" else range(lax.axis_size(axis))
    pairs = [(order[i], order[i + by]) for i in range(len(order)) if 0 <= i + by < len(order)]
    return lax.ppermute(array, axis, pairs)


def partner(place_ref, k):
    return jnp.bitwise_xor(place_ref[0], k)


def spread_kernel(place_ref, x_ref, *o_refs, tiles):
    per, comps, nvec = o_refs[0].shape[:3]
    stride = comps * tiles
    for k, o_ref in zip(ORDER, o_refs):
        first = rows_of(partner(place_ref, k)) * per
        for t in range(per):
            for c in range(comps):
                for v in range(0, nvec, SUB):
                    rows = pl.ds(first + (v * stride + c * tiles + t), SUB, stride)
                    o_ref[t, c, v : v + SUB, :] = x_ref[rows, :]


def collect_kernel(place_ref, *refs, tiles):
    x_refs, (o_ref, held, sems) = refs[:-3], refs[-3:]
    per, comps, nvec = x_refs[0].shape[:3]
    stride = comps * tiles
    stores = []
    for i, v in enumerate(range(0, nvec, SUB)):
        for k, x_ref in zip(ORDER, x_refs):
            first = rows_of(partner(place_ref, k)) * per
            for t in range(per):
                for c in range(comps):
                    rows = pl.ds(first + (v * stride + c * tiles + t), SUB, stride)
                    held[rows, :] = x_ref[t, c, v : v + SUB, :]
        rows = pl.ds(v * stride, SUB * stride)
        store = pltpu.make_async_copy(held.at[rows], o_ref.at[rows], sems.at[i])
        store.start()
        stores.append(store)
    for store in stores:
        store.wait()


def turn(a):
    return pltpu.roll(a, NX, 1)


def pack_edges(low, near, far, first_ref, last_ref, at):
    first_ref[at] = jnp.where(low, near[0], turn(far[0]))
    last_ref[at] = jnp.where(low, turn(near[1]), far[1])


def gather_kernel(place_ref, *refs):
    pieces, (o_ref, first_ref, last_ref) = refs[:-3], refs[-3:]
    groups, per, comps, nvec = o_ref.shape[:4]
    for k, x_ref in zip(ORDER, pieces):
        o_ref[partner(place_ref, k)] = x_ref[...]
    low = lax.broadcasted_iota(jnp.int32, (SUB, LANES), 1) < NX
    for q in range(groups // 2):
        for c in range(comps):
            for v in range(0, nvec, SUB):
                rows = slice(v, v + SUB)
                near, far = [[o_ref[g, t, c, rows, :] for t in (0, per - 1)] for g in (q, q + groups // 2)]
                pack_edges(low, near, far, first_ref, last_ref, (q, c, rows, slice(None)))


def stencil_kernel(stiff_ref, mass_ref, cls_ref, u_ref, yd_ref, yu_ref, za_ref, zb_ref, w_ref, *rest):
    edges, coef_ref = rest[:-1], rest[-1]
    groups, per, comps, nvec = u_ref.shape[:4]
    lane = lax.broadcasted_iota(jnp.int32, (SUB, LANES), 1)
    low = lane < NX

    def pick(cls, values):
        out = jnp.zeros((SUB, LANES), jnp.float32)
        for level in range(LEVELS):
            out = jnp.where(cls == level, values[level], out)
        return out

    for t in range(per):
        for face, direction in enumerate((0, 1, 1, 2, 2)):
            cls = jnp.broadcast_to(cls_ref[face, t : t + 1, :], (SUB, LANES))
            for i, (a, b) in enumerate(ENTRIES):
                spots = [((level * 3 + direction) * 3 + a) * 3 + b for level in range(LEVELS)]
                coef_ref[t, face * 6 + i] = pick(cls, [stiff_ref[s] for s in spots])
        cls = jnp.broadcast_to(cls_ref[5, t : t + 1, :], (SUB, LANES))
        coef_ref[t, 30] = pick(cls, [mass_ref[level] for level in range(LEVELS)])

    def mix(t, face, d):
        s = [coef_ref[t, face * 6 + i] for i in range(6)]
        return [
            s[ENTRY_OF[min(a, 0), max(a, 0)]] * d[0]
            + s[ENTRY_OF[min(a, 1), max(a, 1)]] * d[1]
            + s[ENTRY_OF[min(a, 2), max(a, 2)]] * d[2]
            for a in range(3)
        ]

    steps = nvec // SUB
    half = groups // 2

    def body(i, carry):
        q = i // steps
        rows = pl.ds(pl.multiple_of((i % steps) * SUB, SUB), SUB)
        ends = []
        for part in range(2):
            g = q + part * half
            tiles = [[u_ref[g, t, c, rows, :] for c in range(3)] for t in range(per)]
            below = [yd_ref[q, c, rows, :] for c in range(3)]
            above = [yu_ref[q, c, rows, :] for c in range(3)]
            if part == 0:
                above = [turn(a) for a in above]
            else:
                below = [turn(a) for a in below]
            swaps = [below] + [[turn(a) for a in line] for line in tiles] + [above]
            done = []
            for t in range(per):
                u = tiles[t]
                f = mix(t, 0, [pltpu.roll(u[c], LANES - 1, 1) - u[c] for c in range(3)])
                acc = [coef_ref[t, 30] * u[c] + (pltpu.roll(f[c], 1, 1) - f[c]) for c in range(3)]
                f = mix(t, 1, [jnp.where(low, swaps[t + 1][c], swaps[t + 2][c]) - u[c] for c in range(3)])
                acc = [acc[c] - f[c] for c in range(3)]
                f = mix(t, 2, [u[c] - jnp.where(low, swaps[t][c], swaps[t + 1][c]) for c in range(3)])
                acc = [acc[c] + f[c] for c in range(3)]
                f = mix(t, 3, [za_ref[g, t, c, rows, :] - u[c] for c in range(3)])
                acc = [acc[c] - f[c] for c in range(3)]
                f = mix(t, 4, [zb_ref[g, t, c, rows, :] - u[c] for c in range(3)])
                done.append([acc[c] - f[c] for c in range(3)])
                for c in range(3):
                    w_ref[g, t, c, rows, :] = done[t][c]
            ends.append((done[0], done[-1]))
        if edges:
            for c in range(3):
                near, far = [[end[c] for end in pair] for pair in ends]
                pack_edges(low, near, far, *edges, (q, c, rows, slice(None)))
        return carry

    lax.fori_loop(0, half * steps, body, 0)


def stacked(ref, t, c):
    groups = ref.shape[0]
    return jnp.concatenate([ref[g, t, c] for g in range(groups)], 0)


def wide(ref, k):
    comps = ref.shape[2]
    return jnp.concatenate([stacked(ref, (2 * k + j) // comps, (2 * k + j) % comps) for j in range(2)], 1)


def packed_products(b_ref, a_ref):
    chunks = a_ref.shape[1] * a_ref.shape[2] // 2
    total = None
    for k in range(chunks):
        a, b = wide(a_ref, k), wide(b_ref, k)
        both = [side[i : i + TILE] for i in range(0, a.shape[0], TILE) for side in (b, a)]
        part = dot(a, jnp.concatenate(both, 0), (1, 1))
        total = part if total is None else total + part
    return [total[i * TILE : (i + 1) * TILE, j * LANES : (j + 1) * LANES] for i, j in PAIRS]


def early_kernel(b_ref, a_ref, o_ref):
    for i, block in enumerate(packed_products(b_ref, a_ref)):
        o_ref[i * TILE : (i + 1) * TILE, :] = block


def late_kernel(place_ref, *refs):
    early_ref, w_ref, keep_ref, give_ref, coef_ref = refs[-5:]
    u_ref = refs[3]
    stencil_kernel(*refs[:-5], w_ref, coef_ref)
    even = place_ref[2] == 0
    for i, block in enumerate(packed_products(u_ref, w_ref)):
        rows = slice(i * TILE, (i + 1) * TILE)
        early = early_ref[rows, :]
        keep_ref[rows, :] = jnp.where(even, block, early)
        give_ref[rows, :] = jnp.where(even, early, block)


def eliminate(panels, cols):
    first, width = cols
    tile, lane0 = first // LANES, first % LANES
    lane = lax.broadcasted_iota(jnp.int32, (SUB, LANES), 1)
    sub = lax.broadcasted_iota(jnp.int32, (SUB, LANES), 0)
    strips = width // SUB
    states = []
    for panel in panels:
        state = [[panel[i * SUB : (i + 1) * SUB, a : a + LANES] for a in range(0, panel.shape[1], LANES)] for i in range(strips)]
        unit = [jnp.where(lane == lane0 + i * SUB + sub, 1.0, 0.0) for i in range(strips)]
        states.append([line + [u] for line, u in zip(state, unit)])
    scales = [[jnp.ones((SUB, LANES), jnp.float32) for _ in range(strips)] for _ in panels]

    def spread(row, like):
        return jnp.broadcast_to(row, (SUB, like.shape[1]))

    for j in range(0, width, STEP):
        strip, off = j // SUB, j % SUB
        for m, state in enumerate(states):
            columns = [
                [jnp.broadcast_to(state[i][tile][:, lane0 + j + s : lane0 + j + s + 1], (SUB, LANES)) for i in range(strip, strips)]
                for s in range(STEP)
            ]
            rows = [[spread(part[off + r : off + r + 1, :], part) for part in state[strip]] for r in range(STEP)]
            small = [[spread(columns[s][0][off + r : off + r + 1, :], columns[s][0]) for s in range(STEP)] for r in range(STEP)]
            inverse = []
            pivots = []
            for r in range(STEP):
                pivots.append(small[r][r])
                inverse.append(1.0 / small[r][r])
                for q in range(r + 1, STEP):
                    ratio = small[q][r] * inverse[r]
                    rows[q] = [a - ratio[:, : a.shape[1]] * b for a, b in zip(rows[q], rows[r])]
                    columns[q] = [a - ratio * b for a, b in zip(columns[q], columns[r])]
                    for p in range(q, STEP):
                        small[p][q] = small[p][q] - ratio * small[p][r]
            weights = [[a * inverse[s] for a in columns[s]] for s in range(STEP)]
            for i in range(strip, strips):
                line = []
                for n, part in enumerate(state[i]):
                    value = part
                    for s in range(STEP):
                        value = value - weights[s][i - strip][:, : part.shape[1]] * rows[s][n]
                    if i == strip:
                        at = sub[:, : part.shape[1]]
                        if off:
                            value = jnp.where(at < off, part, value)
                        for r in range(STEP):
                            value = jnp.where(at == off + r, rows[r][n], value)
                    line.append(value)
                state[i] = line
            for r in range(STEP):
                scales[m][strip] = jnp.where(sub == off + r, pivots[r], scales[m][strip])
    results = []
    for state, scale in zip(states, scales):
        inverse, reduced = [], []
        for line, pivot in zip(state, scale):
            root = lax.rsqrt(pivot)
            root = root * (1.5 - 0.5 * pivot * root * root)
            inverse.append(line[-1] * root)
            reduced.append(jnp.concatenate([part * root[:, : part.shape[1]] for part in line[:-1]], 1))
        results.append((jnp.concatenate(inverse, 0), jnp.concatenate(reduced, 0)))
    return results


def dot(a, b, dims):
    return lax.dot_general(
        a, b, ((dims[:1], dims[1:]), ((), ())), precision=lax.Precision.HIGHEST, preferred_element_type=jnp.float32
    )


def factor(scratch, total):
    count = scratch.shape[0]
    lane = lax.broadcasted_iota(jnp.int32, (1, total), 1)
    for first in range(0, total, BLOCK):
        last = first + BLOCK
        here = (lane >= first) & (lane < last)
        results = eliminate([scratch[m, first:last, :] for m in range(count)], (first, BLOCK))
        for m, (inverse, reduced) in enumerate(results):
            tile = first // LANES * LANES
            side = min(LANES, total - tile)
            parts = []
            if tile:
                parts.append(jnp.zeros((BLOCK, tile), jnp.float32))
            parts.append(inverse[:, :side])
            if tile + side < total:
                parts.append(jnp.zeros((BLOCK, total - tile - side), jnp.float32))
            inverse = jnp.concatenate(parts, 1)
            row = jnp.where(here, inverse, reduced)
            scratch[m, first:last, :] = jnp.where(lane < last, row, 0.0)
            if last < total:
                rest = scratch[m, last:, :]
                lower = dot(rest, inverse, (1, 1))
                scratch[m, last:, :] = jnp.where(here, 0.0, rest) - dot(lower, row, (1, 0))


def factor_kernel(place_ref, own_ref, o_ref, packed, scratch, *, cells):
    pieces, quarter = own_ref.shape[:2]
    total = o_ref.shape[1]
    for k in range(pieces):
        at = ((place_ref[1] + pieces - k) % pieces) * quarter
        packed[pl.ds(pl.multiple_of(at, SUB), quarter), :] = own_ref[k] * (1.0 / cells)
    for m, target in enumerate((o_ref.at[1], scratch.at[0])):
        for q, (i, j) in enumerate(PAIRS):
            block = packed[q * TILE : (q + 1) * TILE, m * TILE : (m + 1) * TILE]
            target[i * TILE : (i + 1) * TILE, j * TILE : (j + 1) * TILE] = block
            if i != j:
                target[j * TILE : (j + 1) * TILE, i * TILE : (i + 1) * TILE] = block.T
    factor(scratch, total)
    o_ref[0] = scratch[0]


def combine_kernel(place_ref, mine_ref, other_ref, w_ref, *o_refs):
    per, comps, nvec = w_ref.shape[1:4]
    groups = w_ref.shape[0]
    even = place_ref[2] == 0
    order = [pl.ds(pl.multiple_of(partner(place_ref, k) * nvec, SUB), nvec) for k in ORDER]
    inv = jnp.concatenate([jnp.where(even, mine_ref[0, rows, :], other_ref[0, rows, :]) for rows in order], 0)
    for n in range(per * comps // 2):
        out = dot(inv, wide(w_ref, n), (1, 0))
        for j in range(2):
            t, c = (2 * n + j) // comps, (2 * n + j) % comps
            for k in range(groups):
                o_refs[k][t, c] = out[k * nvec : (k + 1) * nvec, j * LANES : (j + 1) * LANES]


def rayleigh_kernel(place_ref, mine_ref, other_ref, ray_ref):
    nvec = ray_ref.shape[1]
    even = place_ref[2] == 0
    own = pl.ds(pl.multiple_of(place_ref[0] * nvec, SUB), nvec)
    ray_ref[0] = jnp.where(even, other_ref[1, own, :], mine_ref[1, own, :])
    rows = jnp.where(even, other_ref[0, own, :], mine_ref[0, own, :])
    rows = dot(rows, jnp.where(even, mine_ref[1], other_ref[1]), (1, 0))
    ray_ref[1] = dot(rows, jnp.where(even, other_ref[0], mine_ref[0]), (1, 1))


def call(kernel, outs, operands, scratch=(), smem=0, flops=0, far_out=False):
    inside, outside = pl.BlockSpec(memory_space=pltpu.VMEM), pl.BlockSpec(memory_space=pl.ANY)
    specs = [pl.BlockSpec(memory_space=pltpu.SMEM)] * smem
    specs += [inside] * (len(operands) - smem)
    size = sum(a.size * 4 for a in operands) + 4
    return pl.pallas_call(
        kernel,
        out_shape=[jax.ShapeDtypeStruct(dims, jnp.float32) for dims in outs],
        in_specs=specs,
        out_specs=[outside if far_out else inside] * len(outs),
        scratch_shapes=list(scratch),
        compiler_params=pltpu.CompilerParams(vmem_limit_bytes=VMEM_LIMIT),
        cost_estimate=pl.CostEstimate(flops=flops, bytes_accessed=size, transcendentals=0),
    )(*operands)


def to_core(zl, y, core, x, zh):
    return (zl, y, 1 - core, x, zh)


def total_over_all(keep, give):
    y = (lax.axis_index("space") // 2) % 4
    quarter = keep.shape[0] // 4
    mine = keep + route(give, to_core)

    def chunk(k):
        return lax.dynamic_slice_in_dim(mine, ((y + k) % 4) * quarter, quarter, 0)

    def along_y(k):
        return lambda zl, y, c, x, zh: (zl, (y + k) % 4, c, x, zh)

    def along_x(k):
        return lambda zl, y, c, x, zh: (zl, y, c, (x + k) % 4, zh)

    def along_z(k):
        def move(zl, y, c, x, zh):
            z = (zh * 2 + zl + k) % 4
            return (z % 2, y, c, x, z // 2)

        return move

    got = [route(chunk(k), along_y(k)) for k in (1, 2, 3)]
    mine = (chunk(0) + got[1]) + (got[0] + got[2])
    for along in (along_x, along_z):
        got = [route(mine, along(k)) for k in (1, 2, 3)]
        mine = (mine + got[1]) + (got[0] + got[2])
    return jnp.stack([mine] + [route(mine, along_y(k)) for k in (1, 2, 3)])


def local(vectors, labels, stiffness, mass):
    nvec, comps, _, plane = vectors.shape
    groups = lax.axis_size("vec")
    total = nvec * groups
    nz = lax.axis_size("space")
    cells = 3.0 * nz * plane
    tiles = plane // LANES
    per = tiles // groups
    z = lax.axis_index("space")
    h = lax.axis_index("vec")

    below = step_along(labels, "space", 1)
    lab = labels.reshape(plane // NX, NX)
    row = lax.broadcasted_iota(jnp.int32, lab.shape, 0)
    col = lax.broadcasted_iota(jnp.int32, lab.shape, 1)
    none = LEVELS
    upper = jnp.concatenate([jnp.full((1, NX), none, jnp.int32), lab[:-1]], 0)
    over = jnp.where(z == nz - 1, none, lab)
    under = jnp.where(z == 0, none, below.reshape(lab.shape))
    core = z % 2
    faces = jnp.stack(
        [
            jnp.where(col == NX - 1, none, lab),
            jnp.where(row == lab.shape[0] - 1, none, lab),
            upper,
            jnp.where(core == 0, under, over),
            jnp.where(core == 0, over, under),
            lab,
        ]
    )
    faces = faces.reshape(6, tiles, LANES)
    faces = lax.dynamic_slice_in_dim(faces, rows_of(h) * per, per, 1)
    stiff = stiffness.reshape(-1)

    piece = (per, comps, nvec, LANES)
    shape = (groups,) + piece
    edge = (groups // 2, comps, nvec, LANES)

    def exchange(pieces):
        got = [lax.ppermute(a, "vec", [(i, i ^ k) for i in range(groups)]) for k, a in zip(ORDER[1:], pieces[1:])]
        return [pieces[0]] + got

    def halo(u, first, last):
        yd = step_along(last, "vec", 1)
        yu = step_along(first, "vec", -1)
        za = lax.ppermute(u, "space", [(i, i + (1 if i % 2 else -1)) for i in range(1, nz - 1)])
        zb = lax.ppermute(u, "space", [(i, i ^ 1) for i in range(nz)])
        return u, yd, yu, za, zb

    coefs = [pltpu.VMEM((per, 31, SUB, LANES), jnp.float32)]
    moving = [pltpu.VMEM((nvec * comps * tiles, LANES), jnp.float32), pltpu.SemaphoreType.DMA((nvec // SUB,))]
    place = jnp.stack([h, (z // 2) % 4, core]).astype(jnp.int32)
    work = total * total * per * comps * LANES
    packed = len(PAIRS) * TILE
    pieces = call(
        functools.partial(spread_kernel, tiles=tiles),
        [piece] * groups,
        (place, vectors.reshape(nvec * comps * tiles, LANES)),
        smem=1,
    )
    v, first, last = call(gather_kernel, [shape, edge, edge], [place] + exchange(pieces), smem=1)
    w1, first, last = call(
        stencil_kernel,
        [shape, edge, edge],
        (stiff, mass, faces, *halo(v, first, last)),
        scratch=coefs,
        smem=2,
        flops=20_000_000,
    )
    (early,) = call(early_kernel, [(packed, LANES)], (v, w1), flops=24 * work)
    w2, keep, give = call(
        late_kernel,
        [shape, (packed, LANES), (packed, LANES)],
        (place, stiff, mass, faces, *halo(w1, first, last), early),
        scratch=coefs,
        smem=3,
        flops=24 * work,
    )
    (mine,) = call(
        functools.partial(factor_kernel, cells=cells),
        [(2, total, total)],
        (place, total_over_all(keep, give)),
        scratch=[pltpu.VMEM((packed, LANES), jnp.float32), pltpu.VMEM((1, total, total), jnp.float32)],
        smem=1,
        flops=2 * work,
    )
    other = route(mine, to_core)
    pieces = call(combine_kernel, [piece] * groups, (place, mine, other, w2), smem=1, flops=12 * work)
    *pieces, mine, other = lax.optimization_barrier((*pieces, mine, other))
    (rayleigh,) = call(rayleigh_kernel, [(2, nvec, total)], (place, mine, other), smem=1, flops=2 * work)
    (refined,) = call(
        functools.partial(collect_kernel, tiles=tiles),
        [(nvec * comps * tiles, LANES)],
        [place] + exchange(pieces),
        scratch=moving,
        smem=1,
        far_out=True,
    )
    return refined.reshape(vectors.shape), rayleigh


def solution(mesh):
    return jax.shard_map(
        local,
        mesh=mesh,
        in_specs=(P("vec", None, "space", None), P("space", None), P(), P()),
        out_specs=(P("vec", None, "space", None), P(None, "vec", None)),
        check_vma=False,
    )
```

profile of v0, /device:TPU:8, one launch (start us, length us, event | category | flops | bytes accessed | tf_op | source)
XLA Modules:
  0.0 143.9 jit_solution(5859123634796028244)
XLA Ops:
  0.8 1.3 copy-done
  2.0 1.3 shard_map.59
  3.3 6.2 %collective-permute-start.1 = (f32[4,3,24,128]{3,2,1,0:T(8,128)S(1)}, f32[4,3,24,128]{3,2,1,0:T(8,128)S(1)}, u32[]{:S(2)}, u32[]{:S(2)}) collective-permute-start(f32[4,3,24,128]{3,2,1,0:T(8,128)S(1)} %get-tuple-element.38), channel_id=1, source_target_pairs={{0,7},{1,6},{2,5},{3,4},{4,3},{5,2},{6,1},{7,0},{8,15},{9,14},{10,... | collective-permute-start | bytes 442376 | tf_op jit(solution)/shard_map/ppermute | solution.py:447
  9.5 0.4 collective-permute-start.2
  9.8 3.4 %collective-permute-start.3 = (f32[4,3,24,128]{3,2,1,0:T(8,128)S(1)}, f32[4,3,24,128]{3,2,1,0:T(8,128)S(1)}, u32[]{:S(2)}, u32[]{:S(2)}) collective-permute-start(f32[4,3,24,128]{3,2,1,0:T(8,128)S(1)} %get-tuple-element.40), channel_id=1, source_target_pairs={{0,3},{1,2},{2,1},{3,0},{4,7},{5,6},{6,5},{7,4},{8,11},{9,10},{10,... | collective-permute-start | bytes 442376 | tf_op jit(solution)/shard_map/ppermute | solution.py:447
  13.2 3.0 %collective-permute-start.4 = (f32[4,3,24,128]{3,2,1,0:T(8,128)S(1)}, f32[4,3,24,128]{3,2,1,0:T(8,128)S(1)}, u32[]{:S(2)}, u32[]{:S(2)}) collective-permute-start(f32[4,3,24,128]{3,2,1,0:T(8,128)S(1)} %get-tuple-element.41), channel_id=1, source_target_pairs={{0,4},{1,5},{2,6},{3,7},{4,0},{5,1},{6,2},{7,3},{8,12},{9,13},{10,... | collective-permute-start | bytes 442376 | tf_op jit(solution)/shard_map/ppermute | solution.py:447
  16.6 1.3 collective-permute-start.6
  17.9 3.3 %collective-permute-done.2.refs_2_ = f32[4,3,24,128]{3,2,1,0:T(8,128)S(1)} collective-permute-done((f32[4,3,24,128]{3,2,1,0:T(8,128)S(1)}, f32[4,3,24,128]{3,2,1,0:T(8,128)S(1)}, u32[]{:S(2)}, u32[]{:S(2)}) %collective-permute-start.2) | collective-permute-done | bytes 147488 | tf_op jit(solution)/shard_map/ppermute | solution.py:447
  21.4 0.3 collective-permute-done.3.refs_3_
  21.7 1.9 %collective-permute-start = (s32[1,4096]{1,0:T(1,128)S(1)}, s32[1,4096]{1,0:T(1,128)S(1)}, u32[]{:S(2)}, u32[]{:S(2)}) collective-permute-start(s32[1,4096]{1,0:T(1,128)S(1)} %copy-done.2), channel_id=1, source_target_pairs={{0,8},{8,16},{16,24},{24,32},{32,40},{40,48},{48,56},{56,64},{64,7... | collective-permute-start | bytes 49160 | tf_op jit(solution)/shard_map/ppermute | solution.py:51
  23.7 0.1 reshape.126.stiff_ref.refs_0_
  23.8 1.5 %collective-permute-done.4.refs_4_ = f32[4,3,24,128]{3,2,1,0:T(8,128)S(1)} collective-permute-done((f32[4,3,24,128]{3,2,1,0:T(8,128)S(1)}, f32[4,3,24,128]{3,2,1,0:T(8,128)S(1)}, u32[]{:S(2)}, u32[]{:S(2)}) %collective-permute-start.4) | collective-permute-done | bytes 147488 | tf_op jit(solution)/shard_map/ppermute | solution.py:447
  25.4 1.0 collective-permute-done.7.refs_7_
  26.3 0.8 shard_map.60
  27.1 1.9 %collective-permute-start.10 = (f32[8,4,3,24,128]{4,3,2,1,0:T(8,128)S(1)}, f32[8,4,3,24,128]{4,3,2,1,0:T(8,128)S(1)}, u32[]{:S(2)}, u32[]{:S(2)}) collective-permute-start(f32[8,4,3,24,128]{4,3,2,1,0:T(8,128)S(1)} %get-tuple-element.45.u_ref.b_ref), channel_id=1, source_target_pairs={{8,16},{16,8},{24,32},{32,24},{40,48},{48,40},{56,64},{64,56},{72,... | collective-permute-start | bytes 3538952 | tf_op jit(solution)/shard_map/ppermute | solution.py:453
  29.0 1.8 %collective-permute-start.11 = (f32[8,4,3,24,128]{4,3,2,1,0:T(8,128)S(1)}, f32[8,4,3,24,128]{4,3,2,1,0:T(8,128)S(1)}, u32[]{:S(2)}, u32[]{:S(2)}) collective-permute-start(f32[8,4,3,24,128]{4,3,2,1,0:T(8,128)S(1)} %get-tuple-element.45.u_ref.b_ref), channel_id=1, source_target_pairs={{0,8},{8,0},{16,24},{24,16},{32,40},{40,32},{48,56},{56,48},{64,72... | collective-permute-start | bytes 3538952 | tf_op jit(solution)/shard_map/ppermute | solution.py:454
  30.8 1.9 %collective-permute-start.8 = (f32[4,3,24,128]{3,2,1,0:T(8,128)S(1)}, f32[4,3,24,128]{3,2,1,0:T(8,128)S(1)}, u32[]{:S(2)}, u32[]{:S(2)}) collective-permute-start(f32[4,3,24,128]{3,2,1,0:T(8,128)S(1)} %get-tuple-element.46), channel_id=1, source_target_pairs={{0,2},{2,4},{4,6},{6,7},{7,5},{5,3},{3,1},{8,10},{10,12},{12,14},{... | collective-permute-start | bytes 442376 | tf_op jit(solution)/shard_map/ppermute | solution.py:51
  32.8 1.3 collective-permute-start.9
  34.1 1.9 %collective-permute-done.8.yd_ref = f32[4,3,24,128]{3,2,1,0:T(8,128)S(1)} collective-permute-done((f32[4,3,24,128]{3,2,1,0:T(8,128)S(1)}, f32[4,3,24,128]{3,2,1,0:T(8,128)S(1)}, u32[]{:S(2)}, u32[]{:S(2)}) %collective-permute-start.8) | collective-permute-done | bytes 147488 | tf_op jit(solution)/shard_map/ppermute | solution.py:51
  36.0 4.1 %collective-permute-done.9.yu_ref = f32[4,3,24,128]{3,2,1,0:T(8,128)S(1)} collective-permute-done((f32[4,3,24,128]{3,2,1,0:T(8,128)S(1)}, f32[4,3,24,128]{3,2,1,0:T(8,128)S(1)}, u32[]{:S(2)}, u32[]{:S(2)}) %collective-permute-start.9) | collective-permute-done | bytes 147488 | tf_op jit(solution)/shard_map/ppermute | solution.py:51
  40.2 4.5 %collective-permute-done.10.za_ref = f32[8,4,3,24,128]{4,3,2,1,0:T(8,128)S(1)} collective-permute-done((f32[8,4,3,24,128]{4,3,2,1,0:T(8,128)S(1)}, f32[8,4,3,24,128]{4,3,2,1,0:T(8,128)S(1)}, u32[]{:S(2)}, u32[]{:S(2)}) %collective-permute-start.10) | collective-permute-done | bytes 1179680 | tf_op jit(solution)/shard_map/ppermute | solution.py:453
  44.6 3.7 %shard_map.61 = (f32[8,4,3,24,128]{4,3,2,1,0:T(8,128)S(1)}, f32[4,3,24,128]{3,2,1,0:T(8,128)S(1)}, f32[4,3,24,128]{3,2,1,0:T(8,128)S(1)}) custom-call(f32[108]{0:T(128)S(1)} %reshape.126.stiff_ref.refs_0_, f32[4]{0:T(128)S(1)} %copy-done.1, s32[6,4,128]{2,1,0:T(4,128)S(1)} %constant_dynamic-slice_fusion.3.cls_ref.refs_2_, ...), custom_call_target="tpu_custom_call" | custom-call | flops 20000000 | bytes 3846596 | tf_op jit(solution)/shard_map/pallas_call | solution.py:364
  48.4 1.9 %collective-permute-start.14 = (f32[8,4,3,24,128]{4,3,2,1,0:T(8,128)S(1)}, f32[8,4,3,24,128]{4,3,2,1,0:T(8,128)S(1)}, u32[]{:S(2)}, u32[]{:S(2)}) collective-permute-start(f32[8,4,3,24,128]{4,3,2,1,0:T(8,128)S(1)} %get-tuple-element.48.a_ref.refs_3_), channel_id=1, source_target_pairs={{8,16},{16,8},{24,32},{32,24},{40,48},{48,40},{56,64},{64,56},{72,... | collective-permute-start | bytes 3538952 | tf_op jit(solution)/shard_map/ppermute | solution.py:453
  50.3 1.8 %collective-permute-start.15 = (f32[8,4,3,24,128]{4,3,2,1,0:T(8,128)S(1)}, f32[8,4,3,24,128]{4,3,2,1,0:T(8,128)S(1)}, u32[]{:S(2)}, u32[]{:S(2)}) collective-permute-start(f32[8,4,3,24,128]{4,3,2,1,0:T(8,128)S(1)} %get-tuple-element.48.a_ref.refs_3_), channel_id=1, source_target_pairs={{0,8},{8,0},{16,24},{24,16},{32,40},{40,32},{48,56},{56,48},{64,72... | collective-permute-start | bytes 3538952 | tf_op jit(solution)/shard_map/ppermute | solution.py:454
  52.1 1.9 %collective-permute-start.12 = (f32[4,3,24,128]{3,2,1,0:T(8,128)S(1)}, f32[4,3,24,128]{3,2,1,0:T(8,128)S(1)}, u32[]{:S(2)}, u32[]{:S(2)}) collective-permute-start(f32[4,3,24,128]{3,2,1,0:T(8,128)S(1)} %get-tuple-element.49), channel_id=1, source_target_pairs={{0,2},{2,4},{4,6},{6,7},{7,5},{5,3},{3,1},{8,10},{10,12},{12,14},{... | collective-permute-start | bytes 442376 | tf_op jit(solution)/shard_map/ppermute | solution.py:51
  54.0 1.3 collective-permute-start.13
  55.3 2.4 %shard_map.62.refs_8_ = f32[384,128]{1,0:T(8,128)S(1)} custom-call(f32[8,4,3,24,128]{4,3,2,1,0:T(8,128)S(1)} %get-tuple-element.45.u_ref.b_ref, f32[8,4,3,24,128]{4,3,2,1,0:T(8,128)S(1)} %get-tuple-element.48.a_ref.refs_3_), custom_call_target="tpu_custom_call" | custom-call | flops 1358954496 | bytes 2359300 | tf_op jit(solution)/shard_map/pallas_call | solution.py:364
  57.7 3.6 %collective-permute-done.13.refs_5_ = f32[4,3,24,128]{3,2,1,0:T(8,128)S(1)} collective-permute-done((f32[4,3,24,128]{3,2,1,0:T(8,128)S(1)}, f32[4,3,24,128]{3,2,1,0:T(8,128)S(1)}, u32[]{:S(2)}, u32[]{:S(2)}) %collective-permute-start.13) | collective-permute-done | bytes 147488 | tf_op jit(solution)/shard_map/ppermute | solution.py:51
  61.4 4.5 %collective-permute-done.14.refs_6_ = f32[8,4,3,24,128]{4,3,2,1,0:T(8,128)S(1)} collective-permute-done((f32[8,4,3,24,128]{4,3,2,1,0:T(8,128)S(1)}, f32[8,4,3,24,128]{4,3,2,1,0:T(8,128)S(1)}, u32[]{:S(2)}, u32[]{:S(2)}) %collective-permute-start.14) | collective-permute-done | bytes 1179680 | tf_op jit(solution)/shard_map/ppermute | solution.py:453
  65.9 5.7 %shard_map.63 = (f32[8,4,3,24,128]{4,3,2,1,0:T(8,128)S(1)}, f32[384,128]{1,0:T(8,128)S(1)}, f32[384,128]{1,0:T(8,128)S(1)}) custom-call(s32[3]{0:T(128)S(1)} %pad_add_fusion.place_ref, f32[108]{0:T(128)S(1)} %reshape.126.stiff_ref.refs_0_, f32[4]{0:T(128)S(1)} %copy-done.1, s32[6,4,128]{2,1,0:T(4,128)S(1)} %constant_dynamic-slice_fusion.3.cls_ref.refs_2_, ...), custom_call_target="tpu_custom_call" | custom-call | flops 1358954496 | bytes 4043216 | tf_op jit(solution)/shard_map/pallas_call | solution.py:364
  71.6 0.2 collective-permute-start.16
  71.8 1.3 collective-permute-done.16
  73.2 4.7 %collective-permute-start.17 = (f32[96,128]{1,0:T(8,128)S(1)}, f32[96,128]{1,0:T(8,128)S(1)}, u32[]{:S(2)}, u32[]{:S(2)}) collective-permute-start(f32[96,128]{1,0:T(8,128)S(1)} %get-tuple-element.76), channel_id=1, source_target_pairs={{0,32},{1,33},{2,34},{3,35},{4,36},{5,37},{6,38},{7,39},{8,40},{9,... | collective-permute-start | bytes 147464 | tf_op jit(solution)/shard_map/ppermute | solution.py:45
  77.9 2.0 %collective-permute-start.19 = (f32[96,128]{1,0:T(8,128)S(1)}, f32[96,128]{1,0:T(8,128)S(1)}, u32[]{:S(2)}, u32[]{:S(2)}) collective-permute-start(f32[96,128]{1,0:T(8,128)S(1)} %get-tuple-element.77), channel_id=1, source_target_pairs={{0,48},{1,49},{2,50},{3,51},{4,52},{5,53},{6,54},{7,55},{8,56},{9,... | collective-permute-start | bytes 147464 | tf_op jit(solution)/shard_map/ppermute | solution.py:45
  79.9 0.2 collective-permute-done.17
  80.1 1.8 %collective-permute-done.18 = f32[96,128]{1,0:T(8,128)S(1)} collective-permute-done((f32[96,128]{1,0:T(8,128)S(1)}, f32[96,128]{1,0:T(8,128)S(1)}, u32[]{:S(2)}, u32[]{:S(2)}) %collective-permute-start.18) | collective-permute-done | bytes 49184 | tf_op jit(solution)/shard_map/ppermute | solution.py:45
  82.0 2.8 %collective-permute-start.20 = (f32[96,128]{1,0:T(8,128)S(1)}, f32[96,128]{1,0:T(8,128)S(1)}, u32[]{:S(2)}, u32[]{:S(2)}) collective-permute-start(f32[96,128]{1,0:T(8,128)S(1)} %add_add_fusion.2), channel_id=1, source_target_pairs={{0,4},{1,5},{2,6},{3,7},{4,0},{5,1},{6,2},{7,3},{8,12},{9,13},{10,... | collective-permute-start | bytes 147464 | tf_op jit(solution)/shard_map/ppermute | solution.py:45
  84.8 6.9 %collective-permute-start.21 = (f32[96,128]{1,0:T(8,128)S(1)}, f32[96,128]{1,0:T(8,128)S(1)}, u32[]{:S(2)}, u32[]{:S(2)}) collective-permute-start(f32[96,128]{1,0:T(8,128)S(1)} %add_add_fusion.2), channel_id=1, source_target_pairs={{0,2},{1,3},{2,4},{3,5},{4,6},{5,7},{6,0},{7,1},{8,10},{9,11},{10,... | collective-permute-start | bytes 147464 | tf_op jit(solution)/shard_map/ppermute | solution.py:45
  91.7 1.7 %collective-permute-done.21 = f32[96,128]{1,0:T(8,128)S(1)} collective-permute-done((f32[96,128]{1,0:T(8,128)S(1)}, f32[96,128]{1,0:T(8,128)S(1)}, u32[]{:S(2)}, u32[]{:S(2)}) %collective-permute-start.21) | collective-permute-done | bytes 49184 | tf_op jit(solution)/shard_map/ppermute | solution.py:45
  93.5 2.3 %collective-permute-done.22 = f32[96,128]{1,0:T(8,128)S(1)} collective-permute-done((f32[96,128]{1,0:T(8,128)S(1)}, f32[96,128]{1,0:T(8,128)S(1)}, u32[]{:S(2)}, u32[]{:S(2)}) %collective-permute-start.22) | collective-permute-done | bytes 49184 | tf_op jit(solution)/shard_map/ppermute | solution.py:45
  95.8 0.3 collective-permute-start.23
  96.1 0.4 collective-permute-start.24
  96.5 2.8 %collective-permute-start.25 = (f32[96,128]{1,0:T(8,128)S(1)}, f32[96,128]{1,0:T(8,128)S(1)}, u32[]{:S(2)}, u32[]{:S(2)}) collective-permute-start(f32[96,128]{1,0:T(8,128)S(1)} %add_add_fusion.1), channel_id=1, source_target_pairs={{0,65},{1,64},{2,67},{3,66},{4,69},{5,68},{6,71},{7,70},{8,73},{9,... | collective-permute-start | bytes 147464 | tf_op jit(solution)/shard_map/ppermute | solution.py:45
  99.3 2.3 %collective-permute-done.23 = f32[96,128]{1,0:T(8,128)S(1)} collective-permute-done((f32[96,128]{1,0:T(8,128)S(1)}, f32[96,128]{1,0:T(8,128)S(1)}, u32[]{:S(2)}, u32[]{:S(2)}) %collective-permute-start.23) | collective-permute-done | bytes 49184 | tf_op jit(solution)/shard_map/ppermute | solution.py:45
  101.6 0.3 collective-permute-done.24
  102.0 2.8 %collective-permute-start.27 = (f32[96,128]{1,0:T(8,128)S(1)}, f32[96,128]{1,0:T(8,128)S(1)}, u32[]{:S(2)}, u32[]{:S(2)}) collective-permute-start(f32[96,128]{1,0:T(8,128)S(1)} %add_add_fusion), channel_id=1, source_target_pairs={{0,32},{1,33},{2,34},{3,35},{4,36},{5,37},{6,38},{7,39},{8,40},{9,... | collective-permute-start | bytes 147464 | tf_op jit(solution)/shard_map/ppermute | solution.py:45
  104.8 1.8 %collective-permute-start.28 = (f32[96,128]{1,0:T(8,128)S(1)}, f32[96,128]{1,0:T(8,128)S(1)}, u32[]{:S(2)}, u32[]{:S(2)}) collective-permute-start(f32[96,128]{1,0:T(8,128)S(1)} %add_add_fusion), channel_id=1, source_target_pairs={{0,48},{1,49},{2,50},{3,51},{4,52},{5,53},{6,54},{7,55},{8,56},{9,... | collective-permute-start | bytes 147464 | tf_op jit(solution)/shard_map/ppermute | solution.py:45
  106.5 1.2 collective-permute-done.27
  107.7 1.2 collective-permute-done.28
  108.9 7.8 %shard_map.64.mine_ref = f32[2,192,192]{2,1,0:T(8,128)S(1)} custom-call(s32[3]{0:T(128)S(1)} %pad_add_fusion.place_ref, f32[4,96,128]{2,1,0:T(8,128)S(1)} %pad_maximum_fusion.own_ref), custom_call_target="tpu_custom_call" | custom-call | flops 113246208 | bytes 196624 | tf_op jit(solution)/shard_map/pallas_call | solution.py:364
  116.8 1.7 %collective-permute-done.29.other_ref = f32[2,192,192]{2,1,0:T(8,128)S(1)} collective-permute-done((f32[2,192,192]{2,1,0:T(8,128)S(1)}, f32[2,192,192]{2,1,0:T(8,128)S(1)}, u32[]{:S(2)}, u32[]{:S(2)}) %collective-permute-start.29) | collective-permute-done | bytes 294944 | tf_op jit(solution)/shard_map/ppermute | solution.py:45
  118.5 1.7 %shard_map.65 = (f32[4,3,24,128]{3,2,1,0:T(8,128)S(1)}, f32[4,3,24,128]{3,2,1,0:T(8,128)S(1)}, f32[4,3,24,128]{3,2,1,0:T(8,128)S(1)}, f32[4,3,24,128]{3,2,1,0:T(...) custom-call(s32[3]{0:T(128)S(1)} %pad_add_fusion.place_ref, ...), custom_call_target="tpu_custom_call" | custom-call | flops 679477248 | bytes 1769488 | tf_op jit(solution)/shard_map/pallas_call | solution.py:364
  120.2 3.4 %collective-permute-start.30 = (f32[4,3,24,128]{3,2,1,0:T(8,128)S(1)}, f32[4,3,24,128]{3,2,1,0:T(8,128)S(1)}, u32[]{:S(2)}, u32[]{:S(2)}) collective-permute-start(f32[4,3,24,128]{3,2,1,0:T(8,128)S(1)} %get-tuple-element.63), channel_id=1, source_target_pairs={{0,7},{1,6},{2,5},{3,4},{4,3},{5,2},{6,1},{7,0},{8,15},{9,14},{10,... | collective-permute-start | bytes 442376 | tf_op jit(solution)/shard_map/ppermute | solution.py:447
  123.5 1.2 collective-permute-start.31
  124.7 4.1 %collective-permute-start.32 = (f32[4,3,24,128]{3,2,1,0:T(8,128)S(1)}, f32[4,3,24,128]{3,2,1,0:T(8,128)S(1)}, u32[]{:S(2)}, u32[]{:S(2)}) collective-permute-start(f32[4,3,24,128]{3,2,1,0:T(8,128)S(1)} %get-tuple-element.65), channel_id=1, source_target_pairs={{0,3},{1,2},{2,1},{3,0},{4,7},{5,6},{6,5},{7,4},{8,11},{9,10},{10,... | collective-permute-start | bytes 442376 | tf_op jit(solution)/shard_map/ppermute | solution.py:447
  128.8 0.9 collective-permute-start.33
  129.7 0.9 collective-permute-start.34
  130.6 2.0 %collective-permute-start.35 = (f32[4,3,24,128]{3,2,1,0:T(8,128)S(1)}, f32[4,3,24,128]{3,2,1,0:T(8,128)S(1)}, u32[]{:S(2)}, u32[]{:S(2)}) collective-permute-start(f32[4,3,24,128]{3,2,1,0:T(8,128)S(1)} %get-tuple-element.68), channel_id=1, source_target_pairs={{0,6},{1,7},{2,4},{3,5},{4,2},{5,3},{6,0},{7,1},{8,14},{9,15},{10,... | collective-permute-start | bytes 442376 | tf_op jit(solution)/shard_map/ppermute | solution.py:447
  132.6 2.4 %collective-permute-done.31.refs_2_ = f32[4,3,24,128]{3,2,1,0:T(8,128)S(1)} collective-permute-done((f32[4,3,24,128]{3,2,1,0:T(8,128)S(1)}, f32[4,3,24,128]{3,2,1,0:T(8,128)S(1)}, u32[]{:S(2)}, u32[]{:S(2)}) %collective-permute-start.31) | collective-permute-done | bytes 147488 | tf_op jit(solution)/shard_map/ppermute | solution.py:447
  134.9 1.8 %shard_map.67 = f32[2,24,192]{2,1,0:T(8,128)} custom-call(s32[3]{0:T(128)S(1)} %pad_add_fusion.place_ref, f32[2,192,192]{2,1,0:T(8,128)S(1)} %shard_map.64.mine_ref, f32[2,192,192]{2,1,0:T(8,128)S(1)} %collective-permute-done.29.other_ref), custom_call_target="tpu_custom_call" | custom-call | flops 113246208 | bytes 589840 | tf_op jit(solution)/shard_map/pallas_call | solution.py:364
  136.7 0.3 collective-permute-done.32.refs_3_
  137.0 3.0 %collective-permute-done.33.refs_4_ = f32[4,3,24,128]{3,2,1,0:T(8,128)S(1)} collective-permute-done((f32[4,3,24,128]{3,2,1,0:T(8,128)S(1)}, f32[4,3,24,128]{3,2,1,0:T(8,128)S(1)}, u32[]{:S(2)}, u32[]{:S(2)}) %collective-permute-start.33) | collective-permute-done | bytes 147488 | tf_op jit(solution)/shard_map/ppermute | solution.py:447
  140.0 1.4 collective-permute-done.36.refs_7_
  141.4 2.4 %shard_map.66 = f32[2304,128]{1,0:T(8,128)} custom-call(s32[3]{0:T(128)S(1)} %pad_add_fusion.place_ref, f32[4,3,24,128]{3,2,1,0:T(8,128)S(1)} %get-tuple-element.62.refs_0_, f32[4,3,24,128]{3,2,1,0:T(8,128)S(1)} %collective-permute-done.30.refs_1_, f32[4,3,24,128]{3,2,1,0:T(8,128)S(1)} %collective-permute-done.31.refs_2_, ...), custom_call_target="tpu_custom_call" | custom-call | bytes 1179664 | tf_op jit(solution)/shard_map/pallas_call | solution.py:364
  (53 shorter events, 0.9 us)
Async XLA Ops:
  0.6 15.9 %copy-start.2 = (s32[1,4096]{1,0:T(1,128)S(1)}, s32[1,4096]{1,0:T(1,128)}, u32[]{:S(2)}) copy-start(s32[1,4096]{1,0:T(1,128)} %param.5) | copy-start | bytes 49156
  0.6 23.0 %copy-start.3 = (f32[4,3,3,3]{3,0,2,1:T(4,128)S(1)}, f32[4,3,3,3]{3,0,2,1:T(4,128)}, u32[]{:S(2)}) copy-start(f32[4,3,3,3]{3,0,2,1:T(4,128)} %param.6) | copy-start | bytes 1300
  0.8 1.3 copy-start
  3.3 41.3 %copy-start.1 = (f32[4]{0:T(128)S(1)}, f32[4]{0:T(128)}, u32[]{:S(2)}) copy-start(f32[4]{0:T(128)} %refs_1_.1) | copy-start | bytes 52
  3.3 13.2 %collective-permute-start.1 = (f32[4,3,24,128]{3,2,1,0:T(8,128)S(1)}, f32[4,3,24,128]{3,2,1,0:T(8,128)S(1)}, u32[]{:S(2)}, u32[]{:S(2)}) collective-permute-start(f32[4,3,24,128]{3,2,1,0:T(8,128)S(1)} %get-tuple-element.38), channel_id=1, source_target_pairs={{0,7},{1,6},{2,5},{3,4},{4,3},{5,2},{6,1},{7,0},{8,15},{9,14},{10,... | collective-permute-start | bytes 442376 | tf_op jit(solution)/shard_map/ppermute | solution.py:447
  9.5 11.7 %collective-permute-start.2 = (f32[4,3,24,128]{3,2,1,0:T(8,128)S(1)}, f32[4,3,24,128]{3,2,1,0:T(8,128)S(1)}, u32[]{:S(2)}, u32[]{:S(2)}) collective-permute-start(f32[4,3,24,128]{3,2,1,0:T(8,128)S(1)} %get-tuple-element.39), channel_id=1, source_target_pairs={{0,5},{1,4},{2,7},{3,6},{4,1},{5,0},{6,3},{7,2},{8,13},{9,12},{10,... | collective-permute-start | bytes 442376 | tf_op jit(solution)/shard_map/ppermute | solution.py:447
  9.8 11.9 %collective-permute-start.3 = (f32[4,3,24,128]{3,2,1,0:T(8,128)S(1)}, f32[4,3,24,128]{3,2,1,0:T(8,128)S(1)}, u32[]{:S(2)}, u32[]{:S(2)}) collective-permute-start(f32[4,3,24,128]{3,2,1,0:T(8,128)S(1)} %get-tuple-element.40), channel_id=1, source_target_pairs={{0,3},{1,2},{2,1},{3,0},{4,7},{5,6},{6,5},{7,4},{8,11},{9,10},{10,... | collective-permute-start | bytes 442376 | tf_op jit(solution)/shard_map/ppermute | solution.py:447
  13.2 12.1 %collective-permute-start.4 = (f32[4,3,24,128]{3,2,1,0:T(8,128)S(1)}, f32[4,3,24,128]{3,2,1,0:T(8,128)S(1)}, u32[]{:S(2)}, u32[]{:S(2)}) collective-permute-start(f32[4,3,24,128]{3,2,1,0:T(8,128)S(1)} %get-tuple-element.41), channel_id=1, source_target_pairs={{0,4},{1,5},{2,6},{3,7},{4,0},{5,1},{6,2},{7,3},{8,12},{9,13},{10,... | collective-permute-start | bytes 442376 | tf_op jit(solution)/shard_map/ppermute | solution.py:447
  16.3 9.1 %collective-permute-start.5 = (f32[4,3,24,128]{3,2,1,0:T(8,128)S(1)}, f32[4,3,24,128]{3,2,1,0:T(8,128)S(1)}, u32[]{:S(2)}, u32[]{:S(2)}) collective-permute-start(f32[4,3,24,128]{3,2,1,0:T(8,128)S(1)} %get-tuple-element.42), channel_id=1, source_target_pairs={{0,1},{1,0},{2,3},{3,2},{4,5},{5,4},{6,7},{7,6},{8,9},{9,8},{10,11... | collective-permute-start | bytes 442376 | tf_op jit(solution)/shard_map/ppermute | solution.py:447
  16.6 8.8 %collective-permute-start.6 = (f32[4,3,24,128]{3,2,1,0:T(8,128)S(1)}, f32[4,3,24,128]{3,2,1,0:T(8,128)S(1)}, u32[]{:S(2)}, u32[]{:S(2)}) collective-permute-start(f32[4,3,24,128]{3,2,1,0:T(8,128)S(1)} %get-tuple-element.43), channel_id=1, source_target_pairs={{0,6},{1,7},{2,4},{3,5},{4,2},{5,3},{6,0},{7,1},{8,14},{9,15},{10,... | collective-permute-start | bytes 442376 | tf_op jit(solution)/shard_map/ppermute | solution.py:447
  21.2 5.1 %collective-permute-start.7 = (f32[4,3,24,128]{3,2,1,0:T(8,128)S(1)}, f32[4,3,24,128]{3,2,1,0:T(8,128)S(1)}, u32[]{:S(2)}, u32[]{:S(2)}) collective-permute-start(f32[4,3,24,128]{3,2,1,0:T(8,128)S(1)} %get-tuple-element.44), channel_id=1, source_target_pairs={{0,2},{1,3},{2,0},{3,1},{4,6},{5,7},{6,4},{7,5},{8,10},{9,11},{10,... | collective-permute-start | bytes 442376 | tf_op jit(solution)/shard_map/ppermute | solution.py:447
  21.7 9.1 %collective-permute-start = (s32[1,4096]{1,0:T(1,128)S(1)}, s32[1,4096]{1,0:T(1,128)S(1)}, u32[]{:S(2)}, u32[]{:S(2)}) collective-permute-start(s32[1,4096]{1,0:T(1,128)S(1)} %copy-done.2), channel_id=1, source_target_pairs={{0,8},{8,16},{16,24},{24,32},{32,40},{40,48},{48,56},{56,64},{64,7... | collective-permute-start | bytes 49160 | tf_op jit(solution)/shard_map/ppermute | solution.py:51
  27.1 17.5 %collective-permute-start.10 = (f32[8,4,3,24,128]{4,3,2,1,0:T(8,128)S(1)}, f32[8,4,3,24,128]{4,3,2,1,0:T(8,128)S(1)}, u32[]{:S(2)}, u32[]{:S(2)}) collective-permute-start(f32[8,4,3,24,128]{4,3,2,1,0:T(8,128)S(1)} %get-tuple-element.45.u_ref.b_ref), channel_id=1, source_target_pairs={{8,16},{16,8},{24,32},{32,24},{40,48},{48,40},{56,64},{64,56},{72,... | collective-permute-start | bytes 3538952 | tf_op jit(solution)/shard_map/ppermute | solution.py:453
  29.0 15.6 %collective-permute-start.11 = (f32[8,4,3,24,128]{4,3,2,1,0:T(8,128)S(1)}, f32[8,4,3,24,128]{4,3,2,1,0:T(8,128)S(1)}, u32[]{:S(2)}, u32[]{:S(2)}) collective-permute-start(f32[8,4,3,24,128]{4,3,2,1,0:T(8,128)S(1)} %get-tuple-element.45.u_ref.b_ref), channel_id=1, source_target_pairs={{0,8},{8,0},{16,24},{24,16},{32,40},{40,32},{48,56},{56,48},{64,72... | collective-permute-start | bytes 3538952 | tf_op jit(solution)/shard_map/ppermute | solution.py:454
  30.8 5.2 %collective-permute-start.8 = (f32[4,3,24,128]{3,2,1,0:T(8,128)S(1)}, f32[4,3,24,128]{3,2,1,0:T(8,128)S(1)}, u32[]{:S(2)}, u32[]{:S(2)}) collective-permute-start(f32[4,3,24,128]{3,2,1,0:T(8,128)S(1)} %get-tuple-element.46), channel_id=1, source_target_pairs={{0,2},{2,4},{4,6},{6,7},{7,5},{5,3},{3,1},{8,10},{10,12},{12,14},{... | collective-permute-start | bytes 442376 | tf_op jit(solution)/shard_map/ppermute | solution.py:51
  32.8 7.4 %collective-permute-start.9 = (f32[4,3,24,128]{3,2,1,0:T(8,128)S(1)}, f32[4,3,24,128]{3,2,1,0:T(8,128)S(1)}, u32[]{:S(2)}, u32[]{:S(2)}) collective-permute-start(f32[4,3,24,128]{3,2,1,0:T(8,128)S(1)} %get-tuple-element.47), channel_id=1, source_target_pairs={{2,0},{4,2},{6,4},{7,6},{5,7},{3,5},{1,3},{10,8},{12,10},{14,12},{... | collective-permute-start | bytes 442376 | tf_op jit(solution)/shard_map/ppermute | solution.py:51
  48.4 17.5 %collective-permute-start.14 = (f32[8,4,3,24,128]{4,3,2,1,0:T(8,128)S(1)}, f32[8,4,3,24,128]{4,3,2,1,0:T(8,128)S(1)}, u32[]{:S(2)}, u32[]{:S(2)}) collective-permute-start(f32[8,4,3,24,128]{4,3,2,1,0:T(8,128)S(1)} %get-tuple-element.48.a_ref.refs_3_), channel_id=1, source_target_pairs={{8,16},{16,8},{24,32},{32,24},{40,48},{48,40},{56,64},{64,56},{72,... | collective-permute-start | bytes 3538952 | tf_op jit(solution)/shard_map/ppermute | solution.py:453
  50.3 15.6 %collective-permute-start.15 = (f32[8,4,3,24,128]{4,3,2,1,0:T(8,128)S(1)}, f32[8,4,3,24,128]{4,3,2,1,0:T(8,128)S(1)}, u32[]{:S(2)}, u32[]{:S(2)}) collective-permute-start(f32[8,4,3,24,128]{4,3,2,1,0:T(8,128)S(1)} %get-tuple-element.48.a_ref.refs_3_), channel_id=1, source_target_pairs={{0,8},{8,0},{16,24},{24,16},{32,40},{40,32},{48,56},{56,48},{64,72... | collective-permute-start | bytes 3538952 | tf_op jit(solution)/shard_map/ppermute | solution.py:454
  52.1 5.7 %collective-permute-start.12 = (f32[4,3,24,128]{3,2,1,0:T(8,128)S(1)}, f32[4,3,24,128]{3,2,1,0:T(8,128)S(1)}, u32[]{:S(2)}, u32[]{:S(2)}) collective-permute-start(f32[4,3,24,128]{3,2,1,0:T(8,128)S(1)} %get-tuple-element.49), channel_id=1, source_target_pairs={{0,2},{2,4},{4,6},{6,7},{7,5},{5,3},{3,1},{8,10},{10,12},{12,14},{... | collective-permute-start | bytes 442376 | tf_op jit(solution)/shard_map/ppermute | solution.py:51
  54.0 7.4 %collective-permute-start.13 = (f32[4,3,24,128]{3,2,1,0:T(8,128)S(1)}, f32[4,3,24,128]{3,2,1,0:T(8,128)S(1)}, u32[]{:S(2)}, u32[]{:S(2)}) collective-permute-start(f32[4,3,24,128]{3,2,1,0:T(8,128)S(1)} %get-tuple-element.50), channel_id=1, source_target_pairs={{2,0},{4,2},{6,4},{7,6},{5,7},{3,5},{1,3},{10,8},{12,10},{14,12},{... | collective-permute-start | bytes 442376 | tf_op jit(solution)/shard_map/ppermute | solution.py:51
  71.6 1.5 %collective-permute-start.16 = (f32[384,128]{1,0:T(8,128)S(1)}, f32[384,128]{1,0:T(8,128)S(1)}, u32[]{:S(2)}, u32[]{:S(2)}) collective-permute-start(f32[384,128]{1,0:T(8,128)S(1)} %get-tuple-element.52), channel_id=1, source_target_pairs={{0,8},{1,9},{2,10},{3,11},{4,12},{5,13},{6,14},{7,15},{8,0},{9,1},... | collective-permute-start | bytes 589832 | tf_op jit(solution)/shard_map/ppermute | solution.py:45
  73.2 7.0 %collective-permute-start.17 = (f32[96,128]{1,0:T(8,128)S(1)}, f32[96,128]{1,0:T(8,128)S(1)}, u32[]{:S(2)}, u32[]{:S(2)}) collective-permute-start(f32[96,128]{1,0:T(8,128)S(1)} %get-tuple-element.76), channel_id=1, source_target_pairs={{0,32},{1,33},{2,34},{3,35},{4,36},{5,37},{6,38},{7,39},{8,40},{9,... | collective-permute-start | bytes 147464 | tf_op jit(solution)/shard_map/ppermute | solution.py:45
  77.9 4.1 %collective-permute-start.18 = (f32[96,128]{1,0:T(8,128)S(1)}, f32[96,128]{1,0:T(8,128)S(1)}, u32[]{:S(2)}, u32[]{:S(2)}) collective-permute-start(f32[96,128]{1,0:T(8,128)S(1)} %get-tuple-element.78), channel_id=1, source_target_pairs={{0,16},{1,17},{2,18},{3,19},{4,20},{5,21},{6,22},{7,23},{8,24},{9,... | collective-permute-start | bytes 147464 | tf_op jit(solution)/shard_map/ppermute | solution.py:45
  77.9 4.1 %collective-permute-start.19 = (f32[96,128]{1,0:T(8,128)S(1)}, f32[96,128]{1,0:T(8,128)S(1)}, u32[]{:S(2)}, u32[]{:S(2)}) collective-permute-start(f32[96,128]{1,0:T(8,128)S(1)} %get-tuple-element.77), channel_id=1, source_target_pairs={{0,48},{1,49},{2,50},{3,51},{4,52},{5,53},{6,54},{7,55},{8,56},{9,... | collective-permute-start | bytes 147464 | tf_op jit(solution)/shard_map/ppermute | solution.py:45
  82.0 9.7 %collective-permute-start.20 = (f32[96,128]{1,0:T(8,128)S(1)}, f32[96,128]{1,0:T(8,128)S(1)}, u32[]{:S(2)}, u32[]{:S(2)}) collective-permute-start(f32[96,128]{1,0:T(8,128)S(1)} %add_add_fusion.2), channel_id=1, source_target_pairs={{0,4},{1,5},{2,6},{3,7},{4,0},{5,1},{6,2},{7,3},{8,12},{9,13},{10,... | collective-permute-start | bytes 147464 | tf_op jit(solution)/shard_map/ppermute | solution.py:45
  84.8 8.7 %collective-permute-start.21 = (f32[96,128]{1,0:T(8,128)S(1)}, f32[96,128]{1,0:T(8,128)S(1)}, u32[]{:S(2)}, u32[]{:S(2)}) collective-permute-start(f32[96,128]{1,0:T(8,128)S(1)} %add_add_fusion.2), channel_id=1, source_target_pairs={{0,2},{1,3},{2,4},{3,5},{4,6},{5,7},{6,0},{7,1},{8,10},{9,11},{10,... | collective-permute-start | bytes 147464 | tf_op jit(solution)/shard_map/ppermute | solution.py:45
  91.7 4.1 %collective-permute-start.22 = (f32[96,128]{1,0:T(8,128)S(1)}, f32[96,128]{1,0:T(8,128)S(1)}, u32[]{:S(2)}, u32[]{:S(2)}) collective-permute-start(f32[96,128]{1,0:T(8,128)S(1)} %add_add_fusion.2), channel_id=1, source_target_pairs={{0,6},{1,7},{2,0},{3,1},{4,2},{5,3},{6,4},{7,5},{8,14},{9,15},{10,... | collective-permute-start | bytes 147464 | tf_op jit(solution)/shard_map/ppermute | solution.py:45
  95.8 5.8 %collective-permute-start.23 = (f32[96,128]{1,0:T(8,128)S(1)}, f32[96,128]{1,0:T(8,128)S(1)}, u32[]{:S(2)}, u32[]{:S(2)}) collective-permute-start(f32[96,128]{1,0:T(8,128)S(1)} %add_add_fusion.1), channel_id=1, source_target_pairs={{0,1},{1,0},{2,3},{3,2},{4,5},{5,4},{6,7},{7,6},{8,9},{9,8},{10,11... | collective-permute-start | bytes 147464 | tf_op jit(solution)/shard_map/ppermute | solution.py:45
  96.1 5.8 %collective-permute-start.24 = (f32[96,128]{1,0:T(8,128)S(1)}, f32[96,128]{1,0:T(8,128)S(1)}, u32[]{:S(2)}, u32[]{:S(2)}) collective-permute-start(f32[96,128]{1,0:T(8,128)S(1)} %add_add_fusion.1), channel_id=1, source_target_pairs={{0,64},{1,65},{2,66},{3,67},{4,68},{5,69},{6,70},{7,71},{8,72},{9,... | collective-permute-start | bytes 147464 | tf_op jit(solution)/shard_map/ppermute | solution.py:45
  96.5 5.4 %collective-permute-start.25 = (f32[96,128]{1,0:T(8,128)S(1)}, f32[96,128]{1,0:T(8,128)S(1)}, u32[]{:S(2)}, u32[]{:S(2)}) collective-permute-start(f32[96,128]{1,0:T(8,128)S(1)} %add_add_fusion.1), channel_id=1, source_target_pairs={{0,65},{1,64},{2,67},{3,66},{4,69},{5,68},{6,71},{7,70},{8,73},{9,... | collective-permute-start | bytes 147464 | tf_op jit(solution)/shard_map/ppermute | solution.py:45
  101.9 4.6 %collective-permute-start.26 = (f32[96,128]{1,0:T(8,128)S(1)}, f32[96,128]{1,0:T(8,128)S(1)}, u32[]{:S(2)}, u32[]{:S(2)}) collective-permute-start(f32[96,128]{1,0:T(8,128)S(1)} %add_add_fusion), channel_id=1, source_target_pairs={{0,16},{1,17},{2,18},{3,19},{4,20},{5,21},{6,22},{7,23},{8,24},{9,... | collective-permute-start | bytes 147464 | tf_op jit(solution)/shard_map/ppermute | solution.py:45
  102.0 5.7 %collective-permute-start.27 = (f32[96,128]{1,0:T(8,128)S(1)}, f32[96,128]{1,0:T(8,128)S(1)}, u32[]{:S(2)}, u32[]{:S(2)}) collective-permute-start(f32[96,128]{1,0:T(8,128)S(1)} %add_add_fusion), channel_id=1, source_target_pairs={{0,32},{1,33},{2,34},{3,35},{4,36},{5,37},{6,38},{7,39},{8,40},{9,... | collective-permute-start | bytes 147464 | tf_op jit(solution)/shard_map/ppermute | solution.py:45
  104.8 4.1 %collective-permute-start.28 = (f32[96,128]{1,0:T(8,128)S(1)}, f32[96,128]{1,0:T(8,128)S(1)}, u32[]{:S(2)}, u32[]{:S(2)}) collective-permute-start(f32[96,128]{1,0:T(8,128)S(1)} %add_add_fusion), channel_id=1, source_target_pairs={{0,48},{1,49},{2,50},{3,51},{4,52},{5,53},{6,54},{7,55},{8,56},{9,... | collective-permute-start | bytes 147464 | tf_op jit(solution)/shard_map/ppermute | solution.py:45
  116.7 1.8 %collective-permute-start.29 = (f32[2,192,192]{2,1,0:T(8,128)S(1)}, f32[2,192,192]{2,1,0:T(8,128)S(1)}, u32[]{:S(2)}, u32[]{:S(2)}) collective-permute-start(f32[2,192,192]{2,1,0:T(8,128)S(1)} %shard_map.64.mine_ref), channel_id=1, source_target_pairs={{0,8},{1,9},{2,10},{3,11},{4,12},{5,13},{6,14},{7,15},{8,0},{9,1},... | collective-permute-start | bytes 884744 | tf_op jit(solution)/shard_map/ppermute | solution.py:45
  120.2 10.4 %collective-permute-start.30 = (f32[4,3,24,128]{3,2,1,0:T(8,128)S(1)}, f32[4,3,24,128]{3,2,1,0:T(8,128)S(1)}, u32[]{:S(2)}, u32[]{:S(2)}) collective-permute-start(f32[4,3,24,128]{3,2,1,0:T(8,128)S(1)} %get-tuple-element.63), channel_id=1, source_target_pairs={{0,7},{1,6},{2,5},{3,4},{4,3},{5,2},{6,1},{7,0},{8,15},{9,14},{10,... | collective-permute-start | bytes 442376 | tf_op jit(solution)/shard_map/ppermute | solution.py:447
  123.5 11.4 %collective-permute-start.31 = (f32[4,3,24,128]{3,2,1,0:T(8,128)S(1)}, f32[4,3,24,128]{3,2,1,0:T(8,128)S(1)}, u32[]{:S(2)}, u32[]{:S(2)}) collective-permute-start(f32[4,3,24,128]{3,2,1,0:T(8,128)S(1)} %get-tuple-element.64), channel_id=1, source_target_pairs={{0,5},{1,4},{2,7},{3,6},{4,1},{5,0},{6,3},{7,2},{8,13},{9,12},{10,... | collective-permute-start | bytes 442376 | tf_op jit(solution)/shard_map/ppermute | solution.py:447
  124.7 12.3 %collective-permute-start.32 = (f32[4,3,24,128]{3,2,1,0:T(8,128)S(1)}, f32[4,3,24,128]{3,2,1,0:T(8,128)S(1)}, u32[]{:S(2)}, u32[]{:S(2)}) collective-permute-start(f32[4,3,24,128]{3,2,1,0:T(8,128)S(1)} %get-tuple-element.65), channel_id=1, source_target_pairs={{0,3},{1,2},{2,1},{3,0},{4,7},{5,6},{6,5},{7,4},{8,11},{9,10},{10,... | collective-permute-start | bytes 442376 | tf_op jit(solution)/shard_map/ppermute | solution.py:447
  128.8 11.2 %collective-permute-start.33 = (f32[4,3,24,128]{3,2,1,0:T(8,128)S(1)}, f32[4,3,24,128]{3,2,1,0:T(8,128)S(1)}, u32[]{:S(2)}, u32[]{:S(2)}) collective-permute-start(f32[4,3,24,128]{3,2,1,0:T(8,128)S(1)} %get-tuple-element.66), channel_id=1, source_target_pairs={{0,4},{1,5},{2,6},{3,7},{4,0},{5,1},{6,2},{7,3},{8,12},{9,13},{10,... | collective-permute-start | bytes 442376 | tf_op jit(solution)/shard_map/ppermute | solution.py:447
  129.7 10.3 %collective-permute-start.34 = (f32[4,3,24,128]{3,2,1,0:T(8,128)S(1)}, f32[4,3,24,128]{3,2,1,0:T(8,128)S(1)}, u32[]{:S(2)}, u32[]{:S(2)}) collective-permute-start(f32[4,3,24,128]{3,2,1,0:T(8,128)S(1)} %get-tuple-element.67), channel_id=1, source_target_pairs={{0,1},{1,0},{2,3},{3,2},{4,5},{5,4},{6,7},{7,6},{8,9},{9,8},{10,11... | collective-permute-start | bytes 442376 | tf_op jit(solution)/shard_map/ppermute | solution.py:447
  130.6 9.4 %collective-permute-start.35 = (f32[4,3,24,128]{3,2,1,0:T(8,128)S(1)}, f32[4,3,24,128]{3,2,1,0:T(8,128)S(1)}, u32[]{:S(2)}, u32[]{:S(2)}) collective-permute-start(f32[4,3,24,128]{3,2,1,0:T(8,128)S(1)} %get-tuple-element.68), channel_id=1, source_target_pairs={{0,6},{1,7},{2,4},{3,5},{4,2},{5,3},{6,0},{7,1},{8,14},{9,15},{10,... | collective-permute-start | bytes 442376 | tf_op jit(solution)/shard_map/ppermute | solution.py:447
  134.9 6.5 %collective-permute-start.36 = (f32[4,3,24,128]{3,2,1,0:T(8,128)S(1)}, f32[4,3,24,128]{3,2,1,0:T(8,128)S(1)}, u32[]{:S(2)}, u32[]{:S(2)}) collective-permute-start(f32[4,3,24,128]{3,2,1,0:T(8,128)S(1)} %get-tuple-element.69), channel_id=1, source_target_pairs={{0,2},{1,3},{2,0},{3,1},{4,6},{5,7},{6,4},{7,5},{8,10},{9,11},{10,... | collective-permute-start | bytes 442376 | tf_op jit(solution)/shard_map/ppermute | solution.py:447
where the time goes:
time: 145 us; the launch traced here: 144 us
  starting transfers between devices  67.1 us (46%)
  waiting for transfers between devices  46 us (32%)
  Pallas kernels  27.6 us (19%)
  local copies, waits for them, and re-layouts  1.9 us (1%)
    pallas_call x9, Pallas kernels, call(): pl.pallas_call(kernel, out_shape=[jax.ShapeDtypeStruct(dims, jnp.float32)...  27.6 us
    ppermute x14, starting transfers between devices, exchange(): lax.ppermute(a, 'vec', [(i, i ^ k) for i in range(groups)])  26.6 us
    ppermute x14, starting transfers between devices, route(): return lax.ppermute(array, ('space', 'vec'), pairs)  24.8 us
    ppermute x14, waiting for transfers between devices, route(): return lax.ppermute(array, ('space', 'vec'), pairs)  14.1 us
    ppermute x14, waiting for transfers between devices, exchange(): lax.ppermute(a, 'vec', [(i, i ^ k) for i in range(groups)])  13.2 us
    ppermute x5, waiting for transfers between devices, step_along(): return lax.ppermute(array, axis, pairs)  9.7 us
    ppermute x2, waiting for transfers between devices, halo(): lax.ppermute(u, 'space', [(i, i + (1 if i % 2 else -1)) for i in range(1,...  8.99 us
    ppermute x5, starting transfers between devices, step_along(): return lax.ppermute(array, axis, pairs)  8.32 us
  transfers between devices with their start and end apart: 37, of which 23 were waited for; matrix products, arithmetic and copies ran while one was open for 0% of the time, Pallas kernels for 3%

commit v1 on v0

--- a/solution.py
+++ b/solution.py
@@ -377,12 +377,12 @@
 
 
 def total_over_all(keep, give):
-    y = (lax.axis_index("space") // 2) % 4
+    x = lax.axis_index("vec") // 2
     quarter = keep.shape[0] // 4
     mine = keep + route(give, to_core)
 
     def chunk(k):
-        return lax.dynamic_slice_in_dim(mine, ((y + k) % 4) * quarter, quarter, 0)
+        return lax.dynamic_slice_in_dim(mine, ((x + k) % 4) * quarter, quarter, 0)
 
     def along_y(k):
         return lambda zl, y, c, x, zh: (zl, (y + k) % 4, c, x, zh)
@@ -397,12 +397,12 @@
 
         return move
 
-    got = [route(chunk(k), along_y(k)) for k in (1, 2, 3)]
+    got = [route(chunk(k), along_x(k)) for k in (1, 2, 3)]
     mine = (chunk(0) + got[1]) + (got[0] + got[2])
-    for along in (along_x, along_z):
+    for along in (along_y, along_z):
         got = [route(mine, along(k)) for k in (1, 2, 3)]
         mine = (mine + got[1]) + (got[0] + got[2])
-    return jnp.stack([mine] + [route(mine, along_y(k)) for k in (1, 2, 3)])
+    return jnp.stack([mine] + [route(mine, along_x(k)) for k in (1, 2, 3)])
 
 
 def local(vectors, labels, stiffness, mass):
@@ -456,7 +456,7 @@
 
     coefs = [pltpu.VMEM((per, 31, SUB, LANES), jnp.float32)]
     moving = [pltpu.VMEM((nvec * comps * tiles, LANES), jnp.float32), pltpu.SemaphoreType.DMA((nvec // SUB,))]
-    place = jnp.stack([h, (z // 2) % 4, core]).astype(jnp.int32)
+    place = jnp.stack([h, h // 2, core]).astype(jnp.int32)
     work = total * total * per * comps * LANES
     packed = len(PAIRS) * TILE
     pieces = call(

time: 145 us -> 145 us (level)
    ppermute x14, starting transfers between devices: 26.6 us -> 30.9 us  [exchange(): lax.ppermute(a, 'vec', [(i, i ^ k) for i in range(groups)])]
    ppermute x14, waiting for transfers between devices: 13.2 us -> 9.51 us  [exchange(): lax.ppermute(a, 'vec', [(i, i ^ k) for i in range(groups)])]
    ppermute x14, waiting for transfers between devices: 14.1 us -> 17.4 us  [route(): return lax.ppermute(array, ('space', 'vec'), pairs)]
    ppermute x14, starting transfers between devices: 24.8 us -> 21.6 us  [route(): return lax.ppermute(array, ('space', 'vec'), pairs)]
  transfers between devices with their start and end apart: 37 -> 37, of which waited for: 23 -> 22; matrix products, arithmetic and copies ran while one was open for 0% -> 0% of each run, Pallas kernels for 3% -> 3%
where the time goes in v1:
time: 145 us
  starting transfers between devices  68.1 us (47%)
  waiting for transfers between devices  45.6 us (31%)
  Pallas kernels  27.6 us (19%)
  local copies, waits for them, and re-layouts  1.9 us (1%)
    ppermute x14, starting transfers between devices, exchange(): lax.ppermute(a, 'vec', [(i, i ^ k) for i in range(groups)])  30.9 us
    pallas_call x9, Pallas kernels, call(): pl.pallas_call(kernel, out_shape=[jax.ShapeDtypeStruct(dims, jnp.float32)...  27.6 us
    ppermute x14, starting transfers between devices, route(): return lax.ppermute(array, ('space', 'vec'), pairs)  21.6 us
    ppermute x14, waiting for transfers between devices, route(): return lax.ppermute(array, ('space', 'vec'), pairs)  17.4 us
    ppermute x5, waiting for transfers between devices, step_along(): return lax.ppermute(array, axis, pairs)  9.7 us
    ppermute x14, waiting for transfers between devices, exchange(): lax.ppermute(a, 'vec', [(i, i ^ k) for i in range(groups)])  9.51 us
    ppermute x2, waiting for transfers between devices, halo(): lax.ppermute(u, 'space', [(i, i + (1 if i % 2 else -1)) for i in range(1,...  8.99 us
    ppermute x5, starting transfers between devices, step_along(): return lax.ppermute(array, axis, pairs)  8.32 us
  transfers between devices with their start and end apart: 37, of which 22 were waited for; matrix products, arithmetic and copies ran while one was open for 0% of the time, Pallas kernels for 3%

profile of v1, /device:TPU:8, one launch (start us, length us, event | category | flops | bytes accessed | tf_op | source)
XLA Modules:
  0.0 144.6 jit_solution(5726947009548479556)
XLA Ops:
  0.8 1.3 copy-done
  2.0 1.3 shard_map.59
  3.3 6.2 %collective-permute-start.1 = (f32[4,3,24,128]{3,2,1,0:T(8,128)S(1)}, f32[4,3,24,128]{3,2,1,0:T(8,128)S(1)}, u32[]{:S(2)}, u32[]{:S(2)}) collective-permute-start(f32[4,3,24,128]{3,2,1,0:T(8,128)S(1)} %get-tuple-element.38), channel_id=1, source_target_pairs={{0,7},{1,6},{2,5},{3,4},{4,3},{5,2},{6,1},{7,0},{8,15},{9,14},{10,... | collective-permute-start | bytes 442376 | tf_op jit(solution)/shard_map/ppermute | solution.py:447
  9.5 0.4 collective-permute-start.2
  9.8 3.4 %collective-permute-start.3 = (f32[4,3,24,128]{3,2,1,0:T(8,128)S(1)}, f32[4,3,24,128]{3,2,1,0:T(8,128)S(1)}, u32[]{:S(2)}, u32[]{:S(2)}) collective-permute-start(f32[4,3,24,128]{3,2,1,0:T(8,128)S(1)} %get-tuple-element.40), channel_id=1, source_target_pairs={{0,3},{1,2},{2,1},{3,0},{4,7},{5,6},{6,5},{7,4},{8,11},{9,10},{10,... | collective-permute-start | bytes 442376 | tf_op jit(solution)/shard_map/ppermute | solution.py:447
  13.2 3.0 %collective-permute-start.4 = (f32[4,3,24,128]{3,2,1,0:T(8,128)S(1)}, f32[4,3,24,128]{3,2,1,0:T(8,128)S(1)}, u32[]{:S(2)}, u32[]{:S(2)}) collective-permute-start(f32[4,3,24,128]{3,2,1,0:T(8,128)S(1)} %get-tuple-element.41), channel_id=1, source_target_pairs={{0,4},{1,5},{2,6},{3,7},{4,0},{5,1},{6,2},{7,3},{8,12},{9,13},{10,... | collective-permute-start | bytes 442376 | tf_op jit(solution)/shard_map/ppermute | solution.py:447
  16.3 0.1 iota.20
  16.4 0.1 iota.23
  16.6 1.3 collective-permute-start.6
  17.9 3.3 %collective-permute-done.2.refs_2_ = f32[4,3,24,128]{3,2,1,0:T(8,128)S(1)} collective-permute-done((f32[4,3,24,128]{3,2,1,0:T(8,128)S(1)}, f32[4,3,24,128]{3,2,1,0:T(8,128)S(1)}, u32[]{:S(2)}, u32[]{:S(2)}) %collective-permute-start.2) | collective-permute-done | bytes 147488 | tf_op jit(solution)/shard_map/ppermute | solution.py:447
  21.4 0.3 collective-permute-done.3.refs_3_
  21.7 1.9 %collective-permute-start = (s32[1,4096]{1,0:T(1,128)S(1)}, s32[1,4096]{1,0:T(1,128)S(1)}, u32[]{:S(2)}, u32[]{:S(2)}) collective-permute-start(s32[1,4096]{1,0:T(1,128)S(1)} %copy-done.2), channel_id=1, source_target_pairs={{0,8},{8,16},{16,24},{24,32},{32,40},{40,48},{48,56},{56,64},{64,7... | collective-permute-start | bytes 49160 | tf_op jit(solution)/shard_map/ppermute | solution.py:51
  23.7 0.1 reshape.126.stiff_ref.refs_0_
  23.8 1.5 %collective-permute-done.4.refs_4_ = f32[4,3,24,128]{3,2,1,0:T(8,128)S(1)} collective-permute-done((f32[4,3,24,128]{3,2,1,0:T(8,128)S(1)}, f32[4,3,24,128]{3,2,1,0:T(8,128)S(1)}, u32[]{:S(2)}, u32[]{:S(2)}) %collective-permute-start.4) | collective-permute-done | bytes 147488 | tf_op jit(solution)/shard_map/ppermute | solution.py:447
  25.4 1.0 collective-permute-done.7.refs_7_
  26.3 0.8 shard_map.60
  27.1 1.9 %collective-permute-start.10 = (f32[8,4,3,24,128]{4,3,2,1,0:T(8,128)S(1)}, f32[8,4,3,24,128]{4,3,2,1,0:T(8,128)S(1)}, u32[]{:S(2)}, u32[]{:S(2)}) collective-permute-start(f32[8,4,3,24,128]{4,3,2,1,0:T(8,128)S(1)} %get-tuple-element.45.u_ref.b_ref), channel_id=1, source_target_pairs={{8,16},{16,8},{24,32},{32,24},{40,48},{48,40},{56,64},{64,56},{72,... | collective-permute-start | bytes 3538952 | tf_op jit(solution)/shard_map/ppermute | solution.py:453
  29.0 1.8 %collective-permute-start.11 = (f32[8,4,3,24,128]{4,3,2,1,0:T(8,128)S(1)}, f32[8,4,3,24,128]{4,3,2,1,0:T(8,128)S(1)}, u32[]{:S(2)}, u32[]{:S(2)}) collective-permute-start(f32[8,4,3,24,128]{4,3,2,1,0:T(8,128)S(1)} %get-tuple-element.45.u_ref.b_ref), channel_id=1, source_target_pairs={{0,8},{8,0},{16,24},{24,16},{32,40},{40,32},{48,56},{56,48},{64,72... | collective-permute-start | bytes 3538952 | tf_op jit(solution)/shard_map/ppermute | solution.py:454
  30.8 1.9 %collective-permute-start.8 = (f32[4,3,24,128]{3,2,1,0:T(8,128)S(1)}, f32[4,3,24,128]{3,2,1,0:T(8,128)S(1)}, u32[]{:S(2)}, u32[]{:S(2)}) collective-permute-start(f32[4,3,24,128]{3,2,1,0:T(8,128)S(1)} %get-tuple-element.46), channel_id=1, source_target_pairs={{0,2},{2,4},{4,6},{6,7},{7,5},{5,3},{3,1},{8,10},{10,12},{12,14},{... | collective-permute-start | bytes 442376 | tf_op jit(solution)/shard_map/ppermute | solution.py:51
  32.8 1.3 collective-permute-start.9
  34.1 1.9 %collective-permute-done.8.yd_ref = f32[4,3,24,128]{3,2,1,0:T(8,128)S(1)} collective-permute-done((f32[4,3,24,128]{3,2,1,0:T(8,128)S(1)}, f32[4,3,24,128]{3,2,1,0:T(8,128)S(1)}, u32[]{:S(2)}, u32[]{:S(2)}) %collective-permute-start.8) | collective-permute-done | bytes 147488 | tf_op jit(solution)/shard_map/ppermute | solution.py:51
  36.0 4.1 %collective-permute-done.9.yu_ref = f32[4,3,24,128]{3,2,1,0:T(8,128)S(1)} collective-permute-done((f32[4,3,24,128]{3,2,1,0:T(8,128)S(1)}, f32[4,3,24,128]{3,2,1,0:T(8,128)S(1)}, u32[]{:S(2)}, u32[]{:S(2)}) %collective-permute-start.9) | collective-permute-done | bytes 147488 | tf_op jit(solution)/shard_map/ppermute | solution.py:51
  40.2 4.5 %collective-permute-done.10.za_ref = f32[8,4,3,24,128]{4,3,2,1,0:T(8,128)S(1)} collective-permute-done((f32[8,4,3,24,128]{4,3,2,1,0:T(8,128)S(1)}, f32[8,4,3,24,128]{4,3,2,1,0:T(8,128)S(1)}, u32[]{:S(2)}, u32[]{:S(2)}) %collective-permute-start.10) | collective-permute-done | bytes 1179680 | tf_op jit(solution)/shard_map/ppermute | solution.py:453
  44.6 3.7 %shard_map.61 = (f32[8,4,3,24,128]{4,3,2,1,0:T(8,128)S(1)}, f32[4,3,24,128]{3,2,1,0:T(8,128)S(1)}, f32[4,3,24,128]{3,2,1,0:T(8,128)S(1)}) custom-call(f32[108]{0:T(128)S(1)} %reshape.126.stiff_ref.refs_0_, f32[4]{0:T(128)S(1)} %copy-done.1, s32[6,4,128]{2,1,0:T(4,128)S(1)} %constant_dynamic-slice_fusion.3.cls_ref.refs_2_, ...), custom_call_target="tpu_custom_call" | custom-call | flops 20000000 | bytes 3846596 | tf_op jit(solution)/shard_map/pallas_call | solution.py:364
  48.4 1.9 %collective-permute-start.14 = (f32[8,4,3,24,128]{4,3,2,1,0:T(8,128)S(1)}, f32[8,4,3,24,128]{4,3,2,1,0:T(8,128)S(1)}, u32[]{:S(2)}, u32[]{:S(2)}) collective-permute-start(f32[8,4,3,24,128]{4,3,2,1,0:T(8,128)S(1)} %get-tuple-element.48.a_ref.refs_3_), channel_id=1, source_target_pairs={{8,16},{16,8},{24,32},{32,24},{40,48},{48,40},{56,64},{64,56},{72,... | collective-permute-start | bytes 3538952 | tf_op jit(solution)/shard_map/ppermute | solution.py:453
  50.3 1.8 %collective-permute-start.15 = (f32[8,4,3,24,128]{4,3,2,1,0:T(8,128)S(1)}, f32[8,4,3,24,128]{4,3,2,1,0:T(8,128)S(1)}, u32[]{:S(2)}, u32[]{:S(2)}) collective-permute-start(f32[8,4,3,24,128]{4,3,2,1,0:T(8,128)S(1)} %get-tuple-element.48.a_ref.refs_3_), channel_id=1, source_target_pairs={{0,8},{8,0},{16,24},{24,16},{32,40},{40,32},{48,56},{56,48},{64,72... | collective-permute-start | bytes 3538952 | tf_op jit(solution)/shard_map/ppermute | solution.py:454
  52.0 1.9 %collective-permute-start.12 = (f32[4,3,24,128]{3,2,1,0:T(8,128)S(1)}, f32[4,3,24,128]{3,2,1,0:T(8,128)S(1)}, u32[]{:S(2)}, u32[]{:S(2)}) collective-permute-start(f32[4,3,24,128]{3,2,1,0:T(8,128)S(1)} %get-tuple-element.49), channel_id=1, source_target_pairs={{0,2},{2,4},{4,6},{6,7},{7,5},{5,3},{3,1},{8,10},{10,12},{12,14},{... | collective-permute-start | bytes 442376 | tf_op jit(solution)/shard_map/ppermute | solution.py:51
  54.0 1.3 collective-permute-start.13
  55.3 2.4 %shard_map.62.refs_8_ = f32[384,128]{1,0:T(8,128)S(1)} custom-call(f32[8,4,3,24,128]{4,3,2,1,0:T(8,128)S(1)} %get-tuple-element.45.u_ref.b_ref, f32[8,4,3,24,128]{4,3,2,1,0:T(8,128)S(1)} %get-tuple-element.48.a_ref.refs_3_), custom_call_target="tpu_custom_call" | custom-call | flops 1358954496 | bytes 2359300 | tf_op jit(solution)/shard_map/pallas_call | solution.py:364
  57.7 3.6 %collective-permute-done.13.refs_5_ = f32[4,3,24,128]{3,2,1,0:T(8,128)S(1)} collective-permute-done((f32[4,3,24,128]{3,2,1,0:T(8,128)S(1)}, f32[4,3,24,128]{3,2,1,0:T(8,128)S(1)}, u32[]{:S(2)}, u32[]{:S(2)}) %collective-permute-start.13) | collective-permute-done | bytes 147488 | tf_op jit(solution)/shard_map/ppermute | solution.py:51
  61.3 4.5 %collective-permute-done.14.refs_6_ = f32[8,4,3,24,128]{4,3,2,1,0:T(8,128)S(1)} collective-permute-done((f32[8,4,3,24,128]{4,3,2,1,0:T(8,128)S(1)}, f32[8,4,3,24,128]{4,3,2,1,0:T(8,128)S(1)}, u32[]{:S(2)}, u32[]{:S(2)}) %collective-permute-start.14) | collective-permute-done | bytes 1179680 | tf_op jit(solution)/shard_map/ppermute | solution.py:453
  65.9 5.7 %shard_map.63 = (f32[8,4,3,24,128]{4,3,2,1,0:T(8,128)S(1)}, f32[384,128]{1,0:T(8,128)S(1)}, f32[384,128]{1,0:T(8,128)S(1)}) custom-call(s32[3]{0:T(128)S(1)} %pad_add_fusion.place_ref, f32[108]{0:T(128)S(1)} %reshape.126.stiff_ref.refs_0_, f32[4]{0:T(128)S(1)} %copy-done.1, s32[6,4,128]{2,1,0:T(4,128)S(1)} %constant_dynamic-slice_fusion.3.cls_ref.refs_2_, ...), custom_call_target="tpu_custom_call" | custom-call | flops 1358954496 | bytes 4043216 | tf_op jit(solution)/shard_map/pallas_call | solution.py:364
  71.6 0.2 collective-permute-start.16
  71.8 1.3 collective-permute-done.16
  73.2 5.2 %collective-permute-start.17 = (f32[96,128]{1,0:T(8,128)S(1)}, f32[96,128]{1,0:T(8,128)S(1)}, u32[]{:S(2)}, u32[]{:S(2)}) collective-permute-start(f32[96,128]{1,0:T(8,128)S(1)} %get-tuple-element.76), channel_id=1, source_target_pairs={{0,4},{1,5},{2,6},{3,7},{4,0},{5,1},{6,2},{7,3},{8,12},{9,13},{10,... | collective-permute-start | bytes 147464 | tf_op jit(solution)/shard_map/ppermute | solution.py:45
  78.3 3.4 %collective-permute-start.18 = (f32[96,128]{1,0:T(8,128)S(1)}, f32[96,128]{1,0:T(8,128)S(1)}, u32[]{:S(2)}, u32[]{:S(2)}) collective-permute-start(f32[96,128]{1,0:T(8,128)S(1)} %get-tuple-element.78), channel_id=1, source_target_pairs={{0,2},{1,3},{2,4},{3,5},{4,6},{5,7},{6,0},{7,1},{8,10},{9,11},{10,... | collective-permute-start | bytes 147464 | tf_op jit(solution)/shard_map/ppermute | solution.py:45
  81.8 1.9 %collective-permute-done.18 = f32[96,128]{1,0:T(8,128)S(1)} collective-permute-done((f32[96,128]{1,0:T(8,128)S(1)}, f32[96,128]{1,0:T(8,128)S(1)}, u32[]{:S(2)}, u32[]{:S(2)}) %collective-permute-start.18) | collective-permute-done | bytes 49184 | tf_op jit(solution)/shard_map/ppermute | solution.py:45
  83.6 2.2 %collective-permute-done.19 = f32[96,128]{1,0:T(8,128)S(1)} collective-permute-done((f32[96,128]{1,0:T(8,128)S(1)}, f32[96,128]{1,0:T(8,128)S(1)}, u32[]{:S(2)}, u32[]{:S(2)}) %collective-permute-start.19) | collective-permute-done | bytes 49184 | tf_op jit(solution)/shard_map/ppermute | solution.py:45
  85.9 5.8 %collective-permute-start.21 = (f32[96,128]{1,0:T(8,128)S(1)}, f32[96,128]{1,0:T(8,128)S(1)}, u32[]{:S(2)}, u32[]{:S(2)}) collective-permute-start(f32[96,128]{1,0:T(8,128)S(1)} %add_add_fusion.2), channel_id=1, source_target_pairs={{0,16},{1,17},{2,18},{3,19},{4,20},{5,21},{6,22},{7,23},{8,24},{9,... | collective-permute-start | bytes 147464 | tf_op jit(solution)/shard_map/ppermute | solution.py:45
  91.7 1.7 %collective-permute-done.21 = f32[96,128]{1,0:T(8,128)S(1)} collective-permute-done((f32[96,128]{1,0:T(8,128)S(1)}, f32[96,128]{1,0:T(8,128)S(1)}, u32[]{:S(2)}, u32[]{:S(2)}) %collective-permute-start.21) | collective-permute-done | bytes 49184 | tf_op jit(solution)/shard_map/ppermute | solution.py:45
  93.5 2.3 %collective-permute-done.22 = f32[96,128]{1,0:T(8,128)S(1)} collective-permute-done((f32[96,128]{1,0:T(8,128)S(1)}, f32[96,128]{1,0:T(8,128)S(1)}, u32[]{:S(2)}, u32[]{:S(2)}) %collective-permute-start.22) | collective-permute-done | bytes 49184 | tf_op jit(solution)/shard_map/ppermute | solution.py:45
  95.8 0.2 collective-permute-start.23
  96.1 0.4 collective-permute-start.24
  96.5 2.8 %collective-permute-start.25 = (f32[96,128]{1,0:T(8,128)S(1)}, f32[96,128]{1,0:T(8,128)S(1)}, u32[]{:S(2)}, u32[]{:S(2)}) collective-permute-start(f32[96,128]{1,0:T(8,128)S(1)} %add_add_fusion.1), channel_id=1, source_target_pairs={{0,65},{1,64},{2,67},{3,66},{4,69},{5,68},{6,71},{7,70},{8,73},{9,... | collective-permute-start | bytes 147464 | tf_op jit(solution)/shard_map/ppermute | solution.py:45
  99.3 2.3 %collective-permute-done.23 = f32[96,128]{1,0:T(8,128)S(1)} collective-permute-done((f32[96,128]{1,0:T(8,128)S(1)}, f32[96,128]{1,0:T(8,128)S(1)}, u32[]{:S(2)}, u32[]{:S(2)}) %collective-permute-start.23) | collective-permute-done | bytes 49184 | tf_op jit(solution)/shard_map/ppermute | solution.py:45
  101.6 0.3 collective-permute-done.24
  102.0 2.8 %collective-permute-start.27 = (f32[96,128]{1,0:T(8,128)S(1)}, f32[96,128]{1,0:T(8,128)S(1)}, u32[]{:S(2)}, u32[]{:S(2)}) collective-permute-start(f32[96,128]{1,0:T(8,128)S(1)} %add_add_fusion), channel_id=1, source_target_pairs={{0,4},{1,5},{2,6},{3,7},{4,0},{5,1},{6,2},{7,3},{8,12},{9,13},{10,... | collective-permute-start | bytes 147464 | tf_op jit(solution)/shard_map/ppermute | solution.py:45
  104.8 0.5 collective-permute-start.28
  105.3 2.5 %collective-permute-done.26 = f32[96,128]{1,0:T(8,128)S(1)} collective-permute-done((f32[96,128]{1,0:T(8,128)S(1)}, f32[96,128]{1,0:T(8,128)S(1)}, u32[]{:S(2)}, u32[]{:S(2)}) %collective-permute-start.26) | collective-permute-done | bytes 49184 | tf_op jit(solution)/shard_map/ppermute | solution.py:45
  107.8 1.1 collective-permute-done.28
  108.9 7.8 %shard_map.64.mine_ref = f32[2,192,192]{2,1,0:T(8,128)S(1)} custom-call(s32[3]{0:T(128)S(1)} %pad_add_fusion.place_ref, f32[4,96,128]{2,1,0:T(8,128)S(1)} %pad_maximum_fusion.own_ref), custom_call_target="tpu_custom_call" | custom-call | flops 113246208 | bytes 196624 | tf_op jit(solution)/shard_map/pallas_call | solution.py:364
  116.9 1.7 %collective-permute-done.29.other_ref = f32[2,192,192]{2,1,0:T(8,128)S(1)} collective-permute-done((f32[2,192,192]{2,1,0:T(8,128)S(1)}, f32[2,192,192]{2,1,0:T(8,128)S(1)}, u32[]{:S(2)}, u32[]{:S(2)}) %collective-permute-start.29) | collective-permute-done | bytes 294944 | tf_op jit(solution)/shard_map/ppermute | solution.py:45
  118.6 1.7 %shard_map.65 = (f32[4,3,24,128]{3,2,1,0:T(8,128)S(1)}, f32[4,3,24,128]{3,2,1,0:T(8,128)S(1)}, f32[4,3,24,128]{3,2,1,0:T(8,128)S(1)}, f32[4,3,24,128]{3,2,1,0:T(...) custom-call(s32[3]{0:T(128)S(1)} %pad_add_fusion.place_ref, ...), custom_call_target="tpu_custom_call" | custom-call | flops 679477248 | bytes 1769488 | tf_op jit(solution)/shard_map/pallas_call | solution.py:364
  120.3 3.3 %collective-permute-start.30 = (f32[4,3,24,128]{3,2,1,0:T(8,128)S(1)}, f32[4,3,24,128]{3,2,1,0:T(8,128)S(1)}, u32[]{:S(2)}, u32[]{:S(2)}) collective-permute-start(f32[4,3,24,128]{3,2,1,0:T(8,128)S(1)} %get-tuple-element.63), channel_id=1, source_target_pairs={{0,7},{1,6},{2,5},{3,4},{4,3},{5,2},{6,1},{7,0},{8,15},{9,14},{10,... | collective-permute-start | bytes 442376 | tf_op jit(solution)/shard_map/ppermute | solution.py:447
  123.6 2.4 %collective-permute-start.31 = (f32[4,3,24,128]{3,2,1,0:T(8,128)S(1)}, f32[4,3,24,128]{3,2,1,0:T(8,128)S(1)}, u32[]{:S(2)}, u32[]{:S(2)}) collective-permute-start(f32[4,3,24,128]{3,2,1,0:T(8,128)S(1)} %get-tuple-element.64), channel_id=1, source_target_pairs={{0,5},{1,4},{2,7},{3,6},{4,1},{5,0},{6,3},{7,2},{8,13},{9,12},{10,... | collective-permute-start | bytes 442376 | tf_op jit(solution)/shard_map/ppermute | solution.py:447
  126.1 1.9 %collective-permute-start.32 = (f32[4,3,24,128]{3,2,1,0:T(8,128)S(1)}, f32[4,3,24,128]{3,2,1,0:T(8,128)S(1)}, u32[]{:S(2)}, u32[]{:S(2)}) collective-permute-start(f32[4,3,24,128]{3,2,1,0:T(8,128)S(1)} %get-tuple-element.65), channel_id=1, source_target_pairs={{0,3},{1,2},{2,1},{3,0},{4,7},{5,6},{6,5},{7,4},{8,11},{9,10},{10,... | collective-permute-start | bytes 442376 | tf_op jit(solution)/shard_map/ppermute | solution.py:447
  127.9 1.5 %collective-permute-start.33 = (f32[4,3,24,128]{3,2,1,0:T(8,128)S(1)}, f32[4,3,24,128]{3,2,1,0:T(8,128)S(1)}, u32[]{:S(2)}, u32[]{:S(2)}) collective-permute-start(f32[4,3,24,128]{3,2,1,0:T(8,128)S(1)} %get-tuple-element.66), channel_id=1, source_target_pairs={{0,4},{1,5},{2,6},{3,7},{4,0},{5,1},{6,2},{7,3},{8,12},{9,13},{10,... | collective-permute-start | bytes 442376 | tf_op jit(solution)/shard_map/ppermute | solution.py:447
  129.4 1.9 %collective-permute-start.34 = (f32[4,3,24,128]{3,2,1,0:T(8,128)S(1)}, f32[4,3,24,128]{3,2,1,0:T(8,128)S(1)}, u32[]{:S(2)}, u32[]{:S(2)}) collective-permute-start(f32[4,3,24,128]{3,2,1,0:T(8,128)S(1)} %get-tuple-element.67), channel_id=1, source_target_pairs={{0,1},{1,0},{2,3},{3,2},{4,5},{5,4},{6,7},{7,6},{8,9},{9,8},{10,11... | collective-permute-start | bytes 442376 | tf_op jit(solution)/shard_map/ppermute | solution.py:447
  131.3 5.6 %collective-permute-start.35 = (f32[4,3,24,128]{3,2,1,0:T(8,128)S(1)}, f32[4,3,24,128]{3,2,1,0:T(8,128)S(1)}, u32[]{:S(2)}, u32[]{:S(2)}) collective-permute-start(f32[4,3,24,128]{3,2,1,0:T(8,128)S(1)} %get-tuple-element.68), channel_id=1, source_target_pairs={{0,6},{1,7},{2,4},{3,5},{4,2},{5,3},{6,0},{7,1},{8,14},{9,15},{10,... | collective-permute-start | bytes 442376 | tf_op jit(solution)/shard_map/ppermute | solution.py:447
  136.9 1.8 %shard_map.67 = f32[2,24,192]{2,1,0:T(8,128)} custom-call(s32[3]{0:T(128)S(1)} %pad_add_fusion.place_ref, f32[2,192,192]{2,1,0:T(8,128)S(1)} %shard_map.64.mine_ref, f32[2,192,192]{2,1,0:T(8,128)S(1)} %collective-permute-done.29.other_ref), custom_call_target="tpu_custom_call" | custom-call | flops 113246208 | bytes 589840 | tf_op jit(solution)/shard_map/pallas_call | solution.py:364
  138.7 1.8 %collective-permute-done.33.refs_4_ = f32[4,3,24,128]{3,2,1,0:T(8,128)S(1)} collective-permute-done((f32[4,3,24,128]{3,2,1,0:T(8,128)S(1)}, f32[4,3,24,128]{3,2,1,0:T(8,128)S(1)}, u32[]{:S(2)}, u32[]{:S(2)}) %collective-permute-start.33) | collective-permute-done | bytes 147488 | tf_op jit(solution)/shard_map/ppermute | solution.py:447
  140.5 0.8 collective-permute-done.35.refs_6_
  141.3 0.8 collective-permute-done.36.refs_7_
  142.0 2.4 %shard_map.66 = f32[2304,128]{1,0:T(8,128)} custom-call(s32[3]{0:T(128)S(1)} %pad_add_fusion.place_ref, f32[4,3,24,128]{3,2,1,0:T(8,128)S(1)} %get-tuple-element.62.refs_0_, f32[4,3,24,128]{3,2,1,0:T(8,128)S(1)} %collective-permute-done.30.refs_1_, f32[4,3,24,128]{3,2,1,0:T(8,128)S(1)} %collective-permute-done.31.refs_2_, ...), custom_call_target="tpu_custom_call" | custom-call | bytes 1179664 | tf_op jit(solution)/shard_map/pallas_call | solution.py:364
  (53 shorter events, 0.8 us)
Async XLA Ops:
  0.6 15.9 %copy-start.2 = (s32[1,4096]{1,0:T(1,128)S(1)}, s32[1,4096]{1,0:T(1,128)}, u32[]{:S(2)}) copy-start(s32[1,4096]{1,0:T(1,128)} %param.5) | copy-start | bytes 49156
  0.6 23.0 %copy-start.3 = (f32[4,3,3,3]{3,0,2,1:T(4,128)S(1)}, f32[4,3,3,3]{3,0,2,1:T(4,128)}, u32[]{:S(2)}) copy-start(f32[4,3,3,3]{3,0,2,1:T(4,128)} %param.6) | copy-start | bytes 1300
  0.7 1.3 copy-start
  3.3 41.3 %copy-start.1 = (f32[4]{0:T(128)S(1)}, f32[4]{0:T(128)}, u32[]{:S(2)}) copy-start(f32[4]{0:T(128)} %refs_1_.1) | copy-start | bytes 52
  3.3 13.2 %collective-permute-start.1 = (f32[4,3,24,128]{3,2,1,0:T(8,128)S(1)}, f32[4,3,24,128]{3,2,1,0:T(8,128)S(1)}, u32[]{:S(2)}, u32[]{:S(2)}) collective-permute-start(f32[4,3,24,128]{3,2,1,0:T(8,128)S(1)} %get-tuple-element.38), channel_id=1, source_target_pairs={{0,7},{1,6},{2,5},{3,4},{4,3},{5,2},{6,1},{7,0},{8,15},{9,14},{10,... | collective-permute-start | bytes 442376 | tf_op jit(solution)/shard_map/ppermute | solution.py:447
  9.5 11.7 %collective-permute-start.2 = (f32[4,3,24,128]{3,2,1,0:T(8,128)S(1)}, f32[4,3,24,128]{3,2,1,0:T(8,128)S(1)}, u32[]{:S(2)}, u32[]{:S(2)}) collective-permute-start(f32[4,3,24,128]{3,2,1,0:T(8,128)S(1)} %get-tuple-element.39), channel_id=1, source_target_pairs={{0,5},{1,4},{2,7},{3,6},{4,1},{5,0},{6,3},{7,2},{8,13},{9,12},{10,... | collective-permute-start | bytes 442376 | tf_op jit(solution)/shard_map/ppermute | solution.py:447
  9.8 11.9 %collective-permute-start.3 = (f32[4,3,24,128]{3,2,1,0:T(8,128)S(1)}, f32[4,3,24,128]{3,2,1,0:T(8,128)S(1)}, u32[]{:S(2)}, u32[]{:S(2)}) collective-permute-start(f32[4,3,24,128]{3,2,1,0:T(8,128)S(1)} %get-tuple-element.40), channel_id=1, source_target_pairs={{0,3},{1,2},{2,1},{3,0},{4,7},{5,6},{6,5},{7,4},{8,11},{9,10},{10,... | collective-permute-start | bytes 442376 | tf_op jit(solution)/shard_map/ppermute | solution.py:447
  13.2 12.1 %collective-permute-start.4 = (f32[4,3,24,128]{3,2,1,0:T(8,128)S(1)}, f32[4,3,24,128]{3,2,1,0:T(8,128)S(1)}, u32[]{:S(2)}, u32[]{:S(2)}) collective-permute-start(f32[4,3,24,128]{3,2,1,0:T(8,128)S(1)} %get-tuple-element.41), channel_id=1, source_target_pairs={{0,4},{1,5},{2,6},{3,7},{4,0},{5,1},{6,2},{7,3},{8,12},{9,13},{10,... | collective-permute-start | bytes 442376 | tf_op jit(solution)/shard_map/ppermute | solution.py:447
  16.2 9.1 %collective-permute-start.5 = (f32[4,3,24,128]{3,2,1,0:T(8,128)S(1)}, f32[4,3,24,128]{3,2,1,0:T(8,128)S(1)}, u32[]{:S(2)}, u32[]{:S(2)}) collective-permute-start(f32[4,3,24,128]{3,2,1,0:T(8,128)S(1)} %get-tuple-element.42), channel_id=1, source_target_pairs={{0,1},{1,0},{2,3},{3,2},{4,5},{5,4},{6,7},{7,6},{8,9},{9,8},{10,11... | collective-permute-start | bytes 442376 | tf_op jit(solution)/shard_map/ppermute | solution.py:447
  16.6 8.8 %collective-permute-start.6 = (f32[4,3,24,128]{3,2,1,0:T(8,128)S(1)}, f32[4,3,24,128]{3,2,1,0:T(8,128)S(1)}, u32[]{:S(2)}, u32[]{:S(2)}) collective-permute-start(f32[4,3,24,128]{3,2,1,0:T(8,128)S(1)} %get-tuple-element.43), channel_id=1, source_target_pairs={{0,6},{1,7},{2,4},{3,5},{4,2},{5,3},{6,0},{7,1},{8,14},{9,15},{10,... | collective-permute-start | bytes 442376 | tf_op jit(solution)/shard_map/ppermute | solution.py:447
  21.2 5.1 %collective-permute-start.7 = (f32[4,3,24,128]{3,2,1,0:T(8,128)S(1)}, f32[4,3,24,128]{3,2,1,0:T(8,128)S(1)}, u32[]{:S(2)}, u32[]{:S(2)}) collective-permute-start(f32[4,3,24,128]{3,2,1,0:T(8,128)S(1)} %get-tuple-element.44), channel_id=1, source_target_pairs={{0,2},{1,3},{2,0},{3,1},{4,6},{5,7},{6,4},{7,5},{8,10},{9,11},{10,... | collective-permute-start | bytes 442376 | tf_op jit(solution)/shard_map/ppermute | solution.py:447
  21.7 9.1 %collective-permute-start = (s32[1,4096]{1,0:T(1,128)S(1)}, s32[1,4096]{1,0:T(1,128)S(1)}, u32[]{:S(2)}, u32[]{:S(2)}) collective-permute-start(s32[1,4096]{1,0:T(1,128)S(1)} %copy-done.2), channel_id=1, source_target_pairs={{0,8},{8,16},{16,24},{24,32},{32,40},{40,48},{48,56},{56,64},{64,7... | collective-permute-start | bytes 49160 | tf_op jit(solution)/shard_map/ppermute | solution.py:51
  27.1 17.5 %collective-permute-start.10 = (f32[8,4,3,24,128]{4,3,2,1,0:T(8,128)S(1)}, f32[8,4,3,24,128]{4,3,2,1,0:T(8,128)S(1)}, u32[]{:S(2)}, u32[]{:S(2)}) collective-permute-start(f32[8,4,3,24,128]{4,3,2,1,0:T(8,128)S(1)} %get-tuple-element.45.u_ref.b_ref), channel_id=1, source_target_pairs={{8,16},{16,8},{24,32},{32,24},{40,48},{48,40},{56,64},{64,56},{72,... | collective-permute-start | bytes 3538952 | tf_op jit(solution)/shard_map/ppermute | solution.py:453
  29.0 15.6 %collective-permute-start.11 = (f32[8,4,3,24,128]{4,3,2,1,0:T(8,128)S(1)}, f32[8,4,3,24,128]{4,3,2,1,0:T(8,128)S(1)}, u32[]{:S(2)}, u32[]{:S(2)}) collective-permute-start(f32[8,4,3,24,128]{4,3,2,1,0:T(8,128)S(1)} %get-tuple-element.45.u_ref.b_ref), channel_id=1, source_target_pairs={{0,8},{8,0},{16,24},{24,16},{32,40},{40,32},{48,56},{56,48},{64,72... | collective-permute-start | bytes 3538952 | tf_op jit(solution)/shard_map/ppermute | solution.py:454
  30.8 5.2 %collective-permute-start.8 = (f32[4,3,24,128]{3,2,1,0:T(8,128)S(1)}, f32[4,3,24,128]{3,2,1,0:T(8,128)S(1)}, u32[]{:S(2)}, u32[]{:S(2)}) collective-permute-start(f32[4,3,24,128]{3,2,1,0:T(8,128)S(1)} %get-tuple-element.46), channel_id=1, source_target_pairs={{0,2},{2,4},{4,6},{6,7},{7,5},{5,3},{3,1},{8,10},{10,12},{12,14},{... | collective-permute-start | bytes 442376 | tf_op jit(solution)/shard_map/ppermute | solution.py:51
  32.8 7.4 %collective-permute-start.9 = (f32[4,3,24,128]{3,2,1,0:T(8,128)S(1)}, f32[4,3,24,128]{3,2,1,0:T(8,128)S(1)}, u32[]{:S(2)}, u32[]{:S(2)}) collective-permute-start(f32[4,3,24,128]{3,2,1,0:T(8,128)S(1)} %get-tuple-element.47), channel_id=1, source_target_pairs={{2,0},{4,2},{6,4},{7,6},{5,7},{3,5},{1,3},{10,8},{12,10},{14,12},{... | collective-permute-start | bytes 442376 | tf_op jit(solution)/shard_map/ppermute | solution.py:51
  48.4 17.5 %collective-permute-start.14 = (f32[8,4,3,24,128]{4,3,2,1,0:T(8,128)S(1)}, f32[8,4,3,24,128]{4,3,2,1,0:T(8,128)S(1)}, u32[]{:S(2)}, u32[]{:S(2)}) collective-permute-start(f32[8,4,3,24,128]{4,3,2,1,0:T(8,128)S(1)} %get-tuple-element.48.a_ref.refs_3_), channel_id=1, source_target_pairs={{8,16},{16,8},{24,32},{32,24},{40,48},{48,40},{56,64},{64,56},{72,... | collective-permute-start | bytes 3538952 | tf_op jit(solution)/shard_map/ppermute | solution.py:453
  50.3 15.6 %collective-permute-start.15 = (f32[8,4,3,24,128]{4,3,2,1,0:T(8,128)S(1)}, f32[8,4,3,24,128]{4,3,2,1,0:T(8,128)S(1)}, u32[]{:S(2)}, u32[]{:S(2)}) collective-permute-start(f32[8,4,3,24,128]{4,3,2,1,0:T(8,128)S(1)} %get-tuple-element.48.a_ref.refs_3_), channel_id=1, source_target_pairs={{0,8},{8,0},{16,24},{24,16},{32,40},{40,32},{48,56},{56,48},{64,72... | collective-permute-start | bytes 3538952 | tf_op jit(solution)/shard_map/ppermute | solution.py:454
  52.0 5.7 %collective-permute-start.12 = (f32[4,3,24,128]{3,2,1,0:T(8,128)S(1)}, f32[4,3,24,128]{3,2,1,0:T(8,128)S(1)}, u32[]{:S(2)}, u32[]{:S(2)}) collective-permute-start(f32[4,3,24,128]{3,2,1,0:T(8,128)S(1)} %get-tuple-element.49), channel_id=1, source_target_pairs={{0,2},{2,4},{4,6},{6,7},{7,5},{5,3},{3,1},{8,10},{10,12},{12,14},{... | collective-permute-start | bytes 442376 | tf_op jit(solution)/shard_map/ppermute | solution.py:51
  54.0 7.4 %collective-permute-start.13 = (f32[4,3,24,128]{3,2,1,0:T(8,128)S(1)}, f32[4,3,24,128]{3,2,1,0:T(8,128)S(1)}, u32[]{:S(2)}, u32[]{:S(2)}) collective-permute-start(f32[4,3,24,128]{3,2,1,0:T(8,128)S(1)} %get-tuple-element.50), channel_id=1, source_target_pairs={{2,0},{4,2},{6,4},{7,6},{5,7},{3,5},{1,3},{10,8},{12,10},{14,12},{... | collective-permute-start | bytes 442376 | tf_op jit(solution)/shard_map/ppermute | solution.py:51
  71.6 1.5 %collective-permute-start.16 = (f32[384,128]{1,0:T(8,128)S(1)}, f32[384,128]{1,0:T(8,128)S(1)}, u32[]{:S(2)}, u32[]{:S(2)}) collective-permute-start(f32[384,128]{1,0:T(8,128)S(1)} %get-tuple-element.52), channel_id=1, source_target_pairs={{0,8},{1,9},{2,10},{3,11},{4,12},{5,13},{6,14},{7,15},{8,0},{9,1},... | collective-permute-start | bytes 589832 | tf_op jit(solution)/shard_map/ppermute | solution.py:45
  73.2 8.6 %collective-permute-start.17 = (f32[96,128]{1,0:T(8,128)S(1)}, f32[96,128]{1,0:T(8,128)S(1)}, u32[]{:S(2)}, u32[]{:S(2)}) collective-permute-start(f32[96,128]{1,0:T(8,128)S(1)} %get-tuple-element.76), channel_id=1, source_target_pairs={{0,4},{1,5},{2,6},{3,7},{4,0},{5,1},{6,2},{7,3},{8,12},{9,13},{10,... | collective-permute-start | bytes 147464 | tf_op jit(solution)/shard_map/ppermute | solution.py:45
  78.3 5.3 %collective-permute-start.18 = (f32[96,128]{1,0:T(8,128)S(1)}, f32[96,128]{1,0:T(8,128)S(1)}, u32[]{:S(2)}, u32[]{:S(2)}) collective-permute-start(f32[96,128]{1,0:T(8,128)S(1)} %get-tuple-element.78), channel_id=1, source_target_pairs={{0,2},{1,3},{2,4},{3,5},{4,6},{5,7},{6,0},{7,1},{8,10},{9,11},{10,... | collective-permute-start | bytes 147464 | tf_op jit(solution)/shard_map/ppermute | solution.py:45
  81.7 4.1 %collective-permute-start.19 = (f32[96,128]{1,0:T(8,128)S(1)}, f32[96,128]{1,0:T(8,128)S(1)}, u32[]{:S(2)}, u32[]{:S(2)}) collective-permute-start(f32[96,128]{1,0:T(8,128)S(1)} %get-tuple-element.77), channel_id=1, source_target_pairs={{0,6},{1,7},{2,0},{3,1},{4,2},{5,3},{6,4},{7,5},{8,14},{9,15},{10,... | collective-permute-start | bytes 147464 | tf_op jit(solution)/shard_map/ppermute | solution.py:45
  85.9 5.9 %collective-permute-start.20 = (f32[96,128]{1,0:T(8,128)S(1)}, f32[96,128]{1,0:T(8,128)S(1)}, u32[]{:S(2)}, u32[]{:S(2)}) collective-permute-start(f32[96,128]{1,0:T(8,128)S(1)} %add_add_fusion.2), channel_id=1, source_target_pairs={{0,32},{1,33},{2,34},{3,35},{4,36},{5,37},{6,38},{7,39},{8,40},{9,... | collective-permute-start | bytes 147464 | tf_op jit(solution)/shard_map/ppermute | solution.py:45
  85.9 7.5 %collective-permute-start.21 = (f32[96,128]{1,0:T(8,128)S(1)}, f32[96,128]{1,0:T(8,128)S(1)}, u32[]{:S(2)}, u32[]{:S(2)}) collective-permute-start(f32[96,128]{1,0:T(8,128)S(1)} %add_add_fusion.2), channel_id=1, source_target_pairs={{0,16},{1,17},{2,18},{3,19},{4,20},{5,21},{6,22},{7,23},{8,24},{9,... | collective-permute-start | bytes 147464 | tf_op jit(solution)/shard_map/ppermute | solution.py:45
  91.7 4.1 %collective-permute-start.22 = (f32[96,128]{1,0:T(8,128)S(1)}, f32[96,128]{1,0:T(8,128)S(1)}, u32[]{:S(2)}, u32[]{:S(2)}) collective-permute-start(f32[96,128]{1,0:T(8,128)S(1)} %add_add_fusion.2), channel_id=1, source_target_pairs={{0,48},{1,49},{2,50},{3,51},{4,52},{5,53},{6,54},{7,55},{8,56},{9,... | collective-permute-start | bytes 147464 | tf_op jit(solution)/shard_map/ppermute | solution.py:45
  95.8 5.8 %collective-permute-start.23 = (f32[96,128]{1,0:T(8,128)S(1)}, f32[96,128]{1,0:T(8,128)S(1)}, u32[]{:S(2)}, u32[]{:S(2)}) collective-permute-start(f32[96,128]{1,0:T(8,128)S(1)} %add_add_fusion.1), channel_id=1, source_target_pairs={{0,1},{1,0},{2,3},{3,2},{4,5},{5,4},{6,7},{7,6},{8,9},{9,8},{10,11... | collective-permute-start | bytes 147464 | tf_op jit(solution)/shard_map/ppermute | solution.py:45
  96.1 5.8 %collective-permute-start.24 = (f32[96,128]{1,0:T(8,128)S(1)}, f32[96,128]{1,0:T(8,128)S(1)}, u32[]{:S(2)}, u32[]{:S(2)}) collective-permute-start(f32[96,128]{1,0:T(8,128)S(1)} %add_add_fusion.1), channel_id=1, source_target_pairs={{0,64},{1,65},{2,66},{3,67},{4,68},{5,69},{6,70},{7,71},{8,72},{9,... | collective-permute-start | bytes 147464 | tf_op jit(solution)/shard_map/ppermute | solution.py:45
  96.5 5.4 %collective-permute-start.25 = (f32[96,128]{1,0:T(8,128)S(1)}, f32[96,128]{1,0:T(8,128)S(1)}, u32[]{:S(2)}, u32[]{:S(2)}) collective-permute-start(f32[96,128]{1,0:T(8,128)S(1)} %add_add_fusion.1), channel_id=1, source_target_pairs={{0,65},{1,64},{2,67},{3,66},{4,69},{5,68},{6,71},{7,70},{8,73},{9,... | collective-permute-start | bytes 147464 | tf_op jit(solution)/shard_map/ppermute | solution.py:45
  101.9 5.9 %collective-permute-start.26 = (f32[96,128]{1,0:T(8,128)S(1)}, f32[96,128]{1,0:T(8,128)S(1)}, u32[]{:S(2)}, u32[]{:S(2)}) collective-permute-start(f32[96,128]{1,0:T(8,128)S(1)} %add_add_fusion), channel_id=1, source_target_pairs={{0,2},{1,3},{2,4},{3,5},{4,6},{5,7},{6,0},{7,1},{8,10},{9,11},{10,... | collective-permute-start | bytes 147464 | tf_op jit(solution)/shard_map/ppermute | solution.py:45
  102.0 5.8 %collective-permute-start.27 = (f32[96,128]{1,0:T(8,128)S(1)}, f32[96,128]{1,0:T(8,128)S(1)}, u32[]{:S(2)}, u32[]{:S(2)}) collective-permute-start(f32[96,128]{1,0:T(8,128)S(1)} %add_add_fusion), channel_id=1, source_target_pairs={{0,4},{1,5},{2,6},{3,7},{4,0},{5,1},{6,2},{7,3},{8,12},{9,13},{10,... | collective-permute-start | bytes 147464 | tf_op jit(solution)/shard_map/ppermute | solution.py:45
  104.8 4.1 %collective-permute-start.28 = (f32[96,128]{1,0:T(8,128)S(1)}, f32[96,128]{1,0:T(8,128)S(1)}, u32[]{:S(2)}, u32[]{:S(2)}) collective-permute-start(f32[96,128]{1,0:T(8,128)S(1)} %add_add_fusion), channel_id=1, source_target_pairs={{0,6},{1,7},{2,0},{3,1},{4,2},{5,3},{6,4},{7,5},{8,14},{9,15},{10,... | collective-permute-start | bytes 147464 | tf_op jit(solution)/shard_map/ppermute | solution.py:45
  116.8 1.8 %collective-permute-start.29 = (f32[2,192,192]{2,1,0:T(8,128)S(1)}, f32[2,192,192]{2,1,0:T(8,128)S(1)}, u32[]{:S(2)}, u32[]{:S(2)}) collective-permute-start(f32[2,192,192]{2,1,0:T(8,128)S(1)} %shard_map.64.mine_ref), channel_id=1, source_target_pairs={{0,8},{1,9},{2,10},{3,11},{4,12},{5,13},{6,14},{7,15},{8,0},{9,1},... | collective-permute-start | bytes 884744 | tf_op jit(solution)/shard_map/ppermute | solution.py:45
  120.3 11.1 %collective-permute-start.30 = (f32[4,3,24,128]{3,2,1,0:T(8,128)S(1)}, f32[4,3,24,128]{3,2,1,0:T(8,128)S(1)}, u32[]{:S(2)}, u32[]{:S(2)}) collective-permute-start(f32[4,3,24,128]{3,2,1,0:T(8,128)S(1)} %get-tuple-element.63), channel_id=1, source_target_pairs={{0,7},{1,6},{2,5},{3,4},{4,3},{5,2},{6,1},{7,0},{8,15},{9,14},{10,... | collective-permute-start | bytes 442376 | tf_op jit(solution)/shard_map/ppermute | solution.py:447
  123.6 13.3 %collective-permute-start.31 = (f32[4,3,24,128]{3,2,1,0:T(8,128)S(1)}, f32[4,3,24,128]{3,2,1,0:T(8,128)S(1)}, u32[]{:S(2)}, u32[]{:S(2)}) collective-permute-start(f32[4,3,24,128]{3,2,1,0:T(8,128)S(1)} %get-tuple-element.64), channel_id=1, source_target_pairs={{0,5},{1,4},{2,7},{3,6},{4,1},{5,0},{6,3},{7,2},{8,13},{9,12},{10,... | collective-permute-start | bytes 442376 | tf_op jit(solution)/shard_map/ppermute | solution.py:447
  126.1 12.6 %collective-permute-start.32 = (f32[4,3,24,128]{3,2,1,0:T(8,128)S(1)}, f32[4,3,24,128]{3,2,1,0:T(8,128)S(1)}, u32[]{:S(2)}, u32[]{:S(2)}) collective-permute-start(f32[4,3,24,128]{3,2,1,0:T(8,128)S(1)} %get-tuple-element.65), channel_id=1, source_target_pairs={{0,3},{1,2},{2,1},{3,0},{4,7},{5,6},{6,5},{7,4},{8,11},{9,10},{10,... | collective-permute-start | bytes 442376 | tf_op jit(solution)/shard_map/ppermute | solution.py:447
  127.9 12.6 %collective-permute-start.33 = (f32[4,3,24,128]{3,2,1,0:T(8,128)S(1)}, f32[4,3,24,128]{3,2,1,0:T(8,128)S(1)}, u32[]{:S(2)}, u32[]{:S(2)}) collective-permute-start(f32[4,3,24,128]{3,2,1,0:T(8,128)S(1)} %get-tuple-element.66), channel_id=1, source_target_pairs={{0,4},{1,5},{2,6},{3,7},{4,0},{5,1},{6,2},{7,3},{8,12},{9,13},{10,... | collective-permute-start | bytes 442376 | tf_op jit(solution)/shard_map/ppermute | solution.py:447
  129.4 11.1 %collective-permute-start.34 = (f32[4,3,24,128]{3,2,1,0:T(8,128)S(1)}, f32[4,3,24,128]{3,2,1,0:T(8,128)S(1)}, u32[]{:S(2)}, u32[]{:S(2)}) collective-permute-start(f32[4,3,24,128]{3,2,1,0:T(8,128)S(1)} %get-tuple-element.67), channel_id=1, source_target_pairs={{0,1},{1,0},{2,3},{3,2},{4,5},{5,4},{6,7},{7,6},{8,9},{9,8},{10,11... | collective-permute-start | bytes 442376 | tf_op jit(solution)/shard_map/ppermute | solution.py:447
  131.3 10.0 %collective-permute-start.35 = (f32[4,3,24,128]{3,2,1,0:T(8,128)S(1)}, f32[4,3,24,128]{3,2,1,0:T(8,128)S(1)}, u32[]{:S(2)}, u32[]{:S(2)}) collective-permute-start(f32[4,3,24,128]{3,2,1,0:T(8,128)S(1)} %get-tuple-element.68), channel_id=1, source_target_pairs={{0,6},{1,7},{2,4},{3,5},{4,2},{5,3},{6,0},{7,1},{8,14},{9,15},{10,... | collective-permute-start | bytes 442376 | tf_op jit(solution)/shard_map/ppermute | solution.py:447
  136.9 5.1 %collective-permute-start.36 = (f32[4,3,24,128]{3,2,1,0:T(8,128)S(1)}, f32[4,3,24,128]{3,2,1,0:T(8,128)S(1)}, u32[]{:S(2)}, u32[]{:S(2)}) collective-permute-start(f32[4,3,24,128]{3,2,1,0:T(8,128)S(1)} %get-tuple-element.69), channel_id=1, source_target_pairs={{0,2},{1,3},{2,0},{3,1},{4,6},{5,7},{6,4},{7,5},{8,10},{9,11},{10,... | collective-permute-start | bytes 442376 | tf_op jit(solution)/shard_map/ppermute | solution.py:447

commit v2 on v1

--- a/solution.py
+++ b/solution.py
@@ -455,14 +455,14 @@
         return u, yd, yu, za, zb
 
     coefs = [pltpu.VMEM((per, 31, SUB, LANES), jnp.float32)]
-    moving = [pltpu.VMEM((nvec * comps * tiles, LANES), jnp.float32), pltpu.SemaphoreType.DMA((nvec // SUB,))]
+    moving = [pltpu.VMEM(((nvec + 1) * comps * tiles, LANES), jnp.float32), pltpu.SemaphoreType.DMA((nvec // SUB,))]
     place = jnp.stack([h, h // 2, core]).astype(jnp.int32)
     work = total * total * per * comps * LANES
     packed = len(PAIRS) * TILE
     pieces = call(
         functools.partial(spread_kernel, tiles=tiles),
         [piece] * groups,
-        (place, vectors.reshape(nvec * comps * tiles, LANES)),
+        (place, jnp.pad(vectors.reshape(nvec * comps * tiles, LANES), ((0, comps * tiles), (0, 0)))),
         smem=1,
     )
     v, first, last = call(gather_kernel, [shape, edge, edge], [place] + exchange(pieces), smem=1)

time: 145 us -> 145 us (level)
  no operation moved by 1% of the time
where the time goes in v2:
time: 145 us
  starting transfers between devices  68.1 us (47%)
  waiting for transfers between devices  45.6 us (31%)
  Pallas kernels  27.6 us (19%)
  local copies, waits for them, and re-layouts  1.99 us (1%)
    ppermute x14, starting transfers between devices, exchange(): lax.ppermute(a, 'vec', [(i, i ^ k) for i in range(groups)])  30.9 us
    pallas_call x9, Pallas kernels, call(): pl.pallas_call(kernel, out_shape=[jax.ShapeDtypeStruct(dims, jnp.float32)...  27.6 us
    ppermute x14, starting transfers between devices, route(): return lax.ppermute(array, ('space', 'vec'), pairs)  21.6 us
    ppermute x14, waiting for transfers between devices, route(): return lax.ppermute(array, ('space', 'vec'), pairs)  17.4 us
    ppermute x5, waiting for transfers between devices, step_along(): return lax.ppermute(array, axis, pairs)  9.7 us
    ppermute x14, waiting for transfers between devices, exchange(): lax.ppermute(a, 'vec', [(i, i ^ k) for i in range(groups)])  9.51 us
    ppermute x2, waiting for transfers between devices, halo(): lax.ppermute(u, 'space', [(i, i + (1 if i % 2 else -1)) for i in range(1,...  8.99 us
    ppermute x5, starting transfers between devices, step_along(): return lax.ppermute(array, axis, pairs)  8.32 us
  transfers between devices with their start and end apart: 37, of which 22 were waited for; matrix products, arithmetic and copies ran while one was open for 0% of the time, Pallas kernels for 3%

profile of v2, /device:TPU:8, one launch (start us, length us, event | category | flops | bytes accessed | tf_op | source)
XLA Modules:
  0.0 144.7 jit_solution(5977308102075656516)
XLA Ops:
  0.7 1.4 pad.5.x_ref
  2.1 1.3 shard_map.59
  3.4 6.2 %collective-permute-start.1 = (f32[4,3,24,128]{3,2,1,0:T(8,128)S(1)}, f32[4,3,24,128]{3,2,1,0:T(8,128)S(1)}, u32[]{:S(2)}, u32[]{:S(2)}) collective-permute-start(f32[4,3,24,128]{3,2,1,0:T(8,128)S(1)} %get-tuple-element.38), channel_id=1, source_target_pairs={{0,7},{1,6},{2,5},{3,4},{4,3},{5,2},{6,1},{7,0},{8,15},{9,14},{10,... | collective-permute-start | bytes 442376 | tf_op jit(solution)/shard_map/ppermute | solution.py:447
  9.6 0.4 collective-permute-start.2
  9.9 3.4 %collective-permute-start.3 = (f32[4,3,24,128]{3,2,1,0:T(8,128)S(1)}, f32[4,3,24,128]{3,2,1,0:T(8,128)S(1)}, u32[]{:S(2)}, u32[]{:S(2)}) collective-permute-start(f32[4,3,24,128]{3,2,1,0:T(8,128)S(1)} %get-tuple-element.40), channel_id=1, source_target_pairs={{0,3},{1,2},{2,1},{3,0},{4,7},{5,6},{6,5},{7,4},{8,11},{9,10},{10,... | collective-permute-start | bytes 442376 | tf_op jit(solution)/shard_map/ppermute | solution.py:447
  13.3 3.0 %collective-permute-start.4 = (f32[4,3,24,128]{3,2,1,0:T(8,128)S(1)}, f32[4,3,24,128]{3,2,1,0:T(8,128)S(1)}, u32[]{:S(2)}, u32[]{:S(2)}) collective-permute-start(f32[4,3,24,128]{3,2,1,0:T(8,128)S(1)} %get-tuple-element.41), channel_id=1, source_target_pairs={{0,4},{1,5},{2,6},{3,7},{4,0},{5,1},{6,2},{7,3},{8,12},{9,13},{10,... | collective-permute-start | bytes 442376 | tf_op jit(solution)/shard_map/ppermute | solution.py:447
  16.3 0.1 iota.20
  16.5 0.1 iota.23
  16.6 1.3 collective-permute-start.6
  18.0 3.3 %collective-permute-done.2.refs_2_ = f32[4,3,24,128]{3,2,1,0:T(8,128)S(1)} collective-permute-done((f32[4,3,24,128]{3,2,1,0:T(8,128)S(1)}, f32[4,3,24,128]{3,2,1,0:T(8,128)S(1)}, u32[]{:S(2)}, u32[]{:S(2)}) %collective-permute-start.2) | collective-permute-done | bytes 147488 | tf_op jit(solution)/shard_map/ppermute | solution.py:447
  21.5 0.3 collective-permute-done.3.refs_3_
  21.8 1.9 %collective-permute-start = (s32[1,4096]{1,0:T(1,128)S(1)}, s32[1,4096]{1,0:T(1,128)S(1)}, u32[]{:S(2)}, u32[]{:S(2)}) collective-permute-start(s32[1,4096]{1,0:T(1,128)S(1)} %copy-done.1), channel_id=1, source_target_pairs={{0,8},{8,16},{16,24},{24,32},{32,40},{40,48},{48,56},{56,64},{64,7... | collective-permute-start | bytes 49160 | tf_op jit(solution)/shard_map/ppermute | solution.py:51
  23.8 0.1 reshape.126.stiff_ref.refs_0_
  23.9 1.5 %collective-permute-done.4.refs_4_ = f32[4,3,24,128]{3,2,1,0:T(8,128)S(1)} collective-permute-done((f32[4,3,24,128]{3,2,1,0:T(8,128)S(1)}, f32[4,3,24,128]{3,2,1,0:T(8,128)S(1)}, u32[]{:S(2)}, u32[]{:S(2)}) %collective-permute-start.4) | collective-permute-done | bytes 147488 | tf_op jit(solution)/shard_map/ppermute | solution.py:447
  25.4 1.0 collective-permute-done.7.refs_7_
  26.4 0.8 shard_map.60
  27.2 1.9 %collective-permute-start.10 = (f32[8,4,3,24,128]{4,3,2,1,0:T(8,128)S(1)}, f32[8,4,3,24,128]{4,3,2,1,0:T(8,128)S(1)}, u32[]{:S(2)}, u32[]{:S(2)}) collective-permute-start(f32[8,4,3,24,128]{4,3,2,1,0:T(8,128)S(1)} %get-tuple-element.45.u_ref.b_ref), channel_id=1, source_target_pairs={{8,16},{16,8},{24,32},{32,24},{40,48},{48,40},{56,64},{64,56},{72,... | collective-permute-start | bytes 3538952 | tf_op jit(solution)/shard_map/ppermute | solution.py:453
  29.1 1.8 %collective-permute-start.11 = (f32[8,4,3,24,128]{4,3,2,1,0:T(8,128)S(1)}, f32[8,4,3,24,128]{4,3,2,1,0:T(8,128)S(1)}, u32[]{:S(2)}, u32[]{:S(2)}) collective-permute-start(f32[8,4,3,24,128]{4,3,2,1,0:T(8,128)S(1)} %get-tuple-element.45.u_ref.b_ref), channel_id=1, source_target_pairs={{0,8},{8,0},{16,24},{24,16},{32,40},{40,32},{48,56},{56,48},{64,72... | collective-permute-start | bytes 3538952 | tf_op jit(solution)/shard_map/ppermute | solution.py:454
  30.9 1.9 %collective-permute-start.8 = (f32[4,3,24,128]{3,2,1,0:T(8,128)S(1)}, f32[4,3,24,128]{3,2,1,0:T(8,128)S(1)}, u32[]{:S(2)}, u32[]{:S(2)}) collective-permute-start(f32[4,3,24,128]{3,2,1,0:T(8,128)S(1)} %get-tuple-element.46), channel_id=1, source_target_pairs={{0,2},{2,4},{4,6},{6,7},{7,5},{5,3},{3,1},{8,10},{10,12},{12,14},{... | collective-permute-start | bytes 442376 | tf_op jit(solution)/shard_map/ppermute | solution.py:51
  32.8 1.3 collective-permute-start.9
  34.2 1.9 %collective-permute-done.8.yd_ref = f32[4,3,24,128]{3,2,1,0:T(8,128)S(1)} collective-permute-done((f32[4,3,24,128]{3,2,1,0:T(8,128)S(1)}, f32[4,3,24,128]{3,2,1,0:T(8,128)S(1)}, u32[]{:S(2)}, u32[]{:S(2)}) %collective-permute-start.8) | collective-permute-done | bytes 147488 | tf_op jit(solution)/shard_map/ppermute | solution.py:51
  36.1 4.1 %collective-permute-done.9.yu_ref = f32[4,3,24,128]{3,2,1,0:T(8,128)S(1)} collective-permute-done((f32[4,3,24,128]{3,2,1,0:T(8,128)S(1)}, f32[4,3,24,128]{3,2,1,0:T(8,128)S(1)}, u32[]{:S(2)}, u32[]{:S(2)}) %collective-permute-start.9) | collective-permute-done | bytes 147488 | tf_op jit(solution)/shard_map/ppermute | solution.py:51
  40.2 4.5 %collective-permute-done.10.za_ref = f32[8,4,3,24,128]{4,3,2,1,0:T(8,128)S(1)} collective-permute-done((f32[8,4,3,24,128]{4,3,2,1,0:T(8,128)S(1)}, f32[8,4,3,24,128]{4,3,2,1,0:T(8,128)S(1)}, u32[]{:S(2)}, u32[]{:S(2)}) %collective-permute-start.10) | collective-permute-done | bytes 1179680 | tf_op jit(solution)/shard_map/ppermute | solution.py:453
  44.7 3.7 %shard_map.61 = (f32[8,4,3,24,128]{4,3,2,1,0:T(8,128)S(1)}, f32[4,3,24,128]{3,2,1,0:T(8,128)S(1)}, f32[4,3,24,128]{3,2,1,0:T(8,128)S(1)}) custom-call(f32[108]{0:T(128)S(1)} %reshape.126.stiff_ref.refs_0_, f32[4]{0:T(128)S(1)} %copy-done, s32[6,4,128]{2,1,0:T(4,128)S(1)} %constant_dynamic-slice_fusion.3.cls_ref.refs_2_, ...), custom_call_target="tpu_custom_call" | custom-call | flops 20000000 | bytes 3846596 | tf_op jit(solution)/shard_map/pallas_call | solution.py:364
  48.4 1.9 %collective-permute-start.14 = (f32[8,4,3,24,128]{4,3,2,1,0:T(8,128)S(1)}, f32[8,4,3,24,128]{4,3,2,1,0:T(8,128)S(1)}, u32[]{:S(2)}, u32[]{:S(2)}) collective-permute-start(f32[8,4,3,24,128]{4,3,2,1,0:T(8,128)S(1)} %get-tuple-element.48.a_ref.refs_3_), channel_id=1, source_target_pairs={{8,16},{16,8},{24,32},{32,24},{40,48},{48,40},{56,64},{64,56},{72,... | collective-permute-start | bytes 3538952 | tf_op jit(solution)/shard_map/ppermute | solution.py:453
  50.4 1.8 %collective-permute-start.15 = (f32[8,4,3,24,128]{4,3,2,1,0:T(8,128)S(1)}, f32[8,4,3,24,128]{4,3,2,1,0:T(8,128)S(1)}, u32[]{:S(2)}, u32[]{:S(2)}) collective-permute-start(f32[8,4,3,24,128]{4,3,2,1,0:T(8,128)S(1)} %get-tuple-element.48.a_ref.refs_3_), channel_id=1, source_target_pairs={{0,8},{8,0},{16,24},{24,16},{32,40},{40,32},{48,56},{56,48},{64,72... | collective-permute-start | bytes 3538952 | tf_op jit(solution)/shard_map/ppermute | solution.py:454
  52.1 1.9 %collective-permute-start.12 = (f32[4,3,24,128]{3,2,1,0:T(8,128)S(1)}, f32[4,3,24,128]{3,2,1,0:T(8,128)S(1)}, u32[]{:S(2)}, u32[]{:S(2)}) collective-permute-start(f32[4,3,24,128]{3,2,1,0:T(8,128)S(1)} %get-tuple-element.49), channel_id=1, source_target_pairs={{0,2},{2,4},{4,6},{6,7},{7,5},{5,3},{3,1},{8,10},{10,12},{12,14},{... | collective-permute-start | bytes 442376 | tf_op jit(solution)/shard_map/ppermute | solution.py:51
  54.0 1.3 collective-permute-start.13
  55.3 2.4 %shard_map.62.refs_8_ = f32[384,128]{1,0:T(8,128)S(1)} custom-call(f32[8,4,3,24,128]{4,3,2,1,0:T(8,128)S(1)} %get-tuple-element.45.u_ref.b_ref, f32[8,4,3,24,128]{4,3,2,1,0:T(8,128)S(1)} %get-tuple-element.48.a_ref.refs_3_), custom_call_target="tpu_custom_call" | custom-call | flops 1358954496 | bytes 2359300 | tf_op jit(solution)/shard_map/pallas_call | solution.py:364
  57.8 3.6 %collective-permute-done.13.refs_5_ = f32[4,3,24,128]{3,2,1,0:T(8,128)S(1)} collective-permute-done((f32[4,3,24,128]{3,2,1,0:T(8,128)S(1)}, f32[4,3,24,128]{3,2,1,0:T(8,128)S(1)}, u32[]{:S(2)}, u32[]{:S(2)}) %collective-permute-start.13) | collective-permute-done | bytes 147488 | tf_op jit(solution)/shard_map/ppermute | solution.py:51
  61.4 4.5 %collective-permute-done.14.refs_6_ = f32[8,4,3,24,128]{4,3,2,1,0:T(8,128)S(1)} collective-permute-done((f32[8,4,3,24,128]{4,3,2,1,0:T(8,128)S(1)}, f32[8,4,3,24,128]{4,3,2,1,0:T(8,128)S(1)}, u32[]{:S(2)}, u32[]{:S(2)}) %collective-permute-start.14) | collective-permute-done | bytes 1179680 | tf_op jit(solution)/shard_map/ppermute | solution.py:453
  66.0 5.7 %shard_map.63 = (f32[8,4,3,24,128]{4,3,2,1,0:T(8,128)S(1)}, f32[384,128]{1,0:T(8,128)S(1)}, f32[384,128]{1,0:T(8,128)S(1)}) custom-call(s32[3]{0:T(128)S(1)} %pad_add_fusion.place_ref, f32[108]{0:T(128)S(1)} %reshape.126.stiff_ref.refs_0_, f32[4]{0:T(128)S(1)} %copy-done, s32[6,4,128]{2,1,0:T(4,128)S(1)} %constant_dynamic-slice_fusion.3.cls_ref.refs_2_, ...), custom_call_target="tpu_custom_call" | custom-call | flops 1358954496 | bytes 4043216 | tf_op jit(solution)/shard_map/pallas_call | solution.py:364
  71.7 0.2 collective-permute-start.16
  71.9 1.3 collective-permute-done.16
  73.3 5.2 %collective-permute-start.17 = (f32[96,128]{1,0:T(8,128)S(1)}, f32[96,128]{1,0:T(8,128)S(1)}, u32[]{:S(2)}, u32[]{:S(2)}) collective-permute-start(f32[96,128]{1,0:T(8,128)S(1)} %get-tuple-element.76), channel_id=1, source_target_pairs={{0,4},{1,5},{2,6},{3,7},{4,0},{5,1},{6,2},{7,3},{8,12},{9,13},{10,... | collective-permute-start | bytes 147464 | tf_op jit(solution)/shard_map/ppermute | solution.py:45
  78.4 3.4 %collective-permute-start.18 = (f32[96,128]{1,0:T(8,128)S(1)}, f32[96,128]{1,0:T(8,128)S(1)}, u32[]{:S(2)}, u32[]{:S(2)}) collective-permute-start(f32[96,128]{1,0:T(8,128)S(1)} %get-tuple-element.78), channel_id=1, source_target_pairs={{0,2},{1,3},{2,4},{3,5},{4,6},{5,7},{6,0},{7,1},{8,10},{9,11},{10,... | collective-permute-start | bytes 147464 | tf_op jit(solution)/shard_map/ppermute | solution.py:45
  81.8 1.9 %collective-permute-done.18 = f32[96,128]{1,0:T(8,128)S(1)} collective-permute-done((f32[96,128]{1,0:T(8,128)S(1)}, f32[96,128]{1,0:T(8,128)S(1)}, u32[]{:S(2)}, u32[]{:S(2)}) %collective-permute-start.18) | collective-permute-done | bytes 49184 | tf_op jit(solution)/shard_map/ppermute | solution.py:45
  83.7 2.2 %collective-permute-done.19 = f32[96,128]{1,0:T(8,128)S(1)} collective-permute-done((f32[96,128]{1,0:T(8,128)S(1)}, f32[96,128]{1,0:T(8,128)S(1)}, u32[]{:S(2)}, u32[]{:S(2)}) %collective-permute-start.19) | collective-permute-done | bytes 49184 | tf_op jit(solution)/shard_map/ppermute | solution.py:45
  86.0 5.8 %collective-permute-start.21 = (f32[96,128]{1,0:T(8,128)S(1)}, f32[96,128]{1,0:T(8,128)S(1)}, u32[]{:S(2)}, u32[]{:S(2)}) collective-permute-start(f32[96,128]{1,0:T(8,128)S(1)} %add_add_fusion.2), channel_id=1, source_target_pairs={{0,16},{1,17},{2,18},{3,19},{4,20},{5,21},{6,22},{7,23},{8,24},{9,... | collective-permute-start | bytes 147464 | tf_op jit(solution)/shard_map/ppermute | solution.py:45
  91.8 1.7 %collective-permute-done.21 = f32[96,128]{1,0:T(8,128)S(1)} collective-permute-done((f32[96,128]{1,0:T(8,128)S(1)}, f32[96,128]{1,0:T(8,128)S(1)}, u32[]{:S(2)}, u32[]{:S(2)}) %collective-permute-start.21) | collective-permute-done | bytes 49184 | tf_op jit(solution)/shard_map/ppermute | solution.py:45
  93.5 2.3 %collective-permute-done.22 = f32[96,128]{1,0:T(8,128)S(1)} collective-permute-done((f32[96,128]{1,0:T(8,128)S(1)}, f32[96,128]{1,0:T(8,128)S(1)}, u32[]{:S(2)}, u32[]{:S(2)}) %collective-permute-start.22) | collective-permute-done | bytes 49184 | tf_op jit(solution)/shard_map/ppermute | solution.py:45
  95.9 0.3 collective-permute-start.23
  96.2 0.4 collective-permute-start.24
  96.6 2.8 %collective-permute-start.25 = (f32[96,128]{1,0:T(8,128)S(1)}, f32[96,128]{1,0:T(8,128)S(1)}, u32[]{:S(2)}, u32[]{:S(2)}) collective-permute-start(f32[96,128]{1,0:T(8,128)S(1)} %add_add_fusion.1), channel_id=1, source_target_pairs={{0,65},{1,64},{2,67},{3,66},{4,69},{5,68},{6,71},{7,70},{8,73},{9,... | collective-permute-start | bytes 147464 | tf_op jit(solution)/shard_map/ppermute | solution.py:45
  99.4 2.3 %collective-permute-done.23 = f32[96,128]{1,0:T(8,128)S(1)} collective-permute-done((f32[96,128]{1,0:T(8,128)S(1)}, f32[96,128]{1,0:T(8,128)S(1)}, u32[]{:S(2)}, u32[]{:S(2)}) %collective-permute-start.23) | collective-permute-done | bytes 49184 | tf_op jit(solution)/shard_map/ppermute | solution.py:45
  101.7 0.3 collective-permute-done.24
  102.1 2.8 %collective-permute-start.27 = (f32[96,128]{1,0:T(8,128)S(1)}, f32[96,128]{1,0:T(8,128)S(1)}, u32[]{:S(2)}, u32[]{:S(2)}) collective-permute-start(f32[96,128]{1,0:T(8,128)S(1)} %add_add_fusion), channel_id=1, source_target_pairs={{0,4},{1,5},{2,6},{3,7},{4,0},{5,1},{6,2},{7,3},{8,12},{9,13},{10,... | collective-permute-start | bytes 147464 | tf_op jit(solution)/shard_map/ppermute | solution.py:45
  104.9 0.5 collective-permute-start.28
  105.4 2.5 %collective-permute-done.26 = f32[96,128]{1,0:T(8,128)S(1)} collective-permute-done((f32[96,128]{1,0:T(8,128)S(1)}, f32[96,128]{1,0:T(8,128)S(1)}, u32[]{:S(2)}, u32[]{:S(2)}) %collective-permute-start.26) | collective-permute-done | bytes 49184 | tf_op jit(solution)/shard_map/ppermute | solution.py:45
  107.9 1.1 collective-permute-done.28
  109.0 7.8 %shard_map.64.mine_ref = f32[2,192,192]{2,1,0:T(8,128)S(1)} custom-call(s32[3]{0:T(128)S(1)} %pad_add_fusion.place_ref, f32[4,96,128]{2,1,0:T(8,128)S(1)} %pad_maximum_fusion.own_ref), custom_call_target="tpu_custom_call" | custom-call | flops 113246208 | bytes 196624 | tf_op jit(solution)/shard_map/pallas_call | solution.py:364
  117.0 1.7 %collective-permute-done.29.other_ref = f32[2,192,192]{2,1,0:T(8,128)S(1)} collective-permute-done((f32[2,192,192]{2,1,0:T(8,128)S(1)}, f32[2,192,192]{2,1,0:T(8,128)S(1)}, u32[]{:S(2)}, u32[]{:S(2)}) %collective-permute-start.29) | collective-permute-done | bytes 294944 | tf_op jit(solution)/shard_map/ppermute | solution.py:45
  118.7 1.7 %shard_map.65 = (f32[4,3,24,128]{3,2,1,0:T(8,128)S(1)}, f32[4,3,24,128]{3,2,1,0:T(8,128)S(1)}, f32[4,3,24,128]{3,2,1,0:T(8,128)S(1)}, f32[4,3,24,128]{3,2,1,0:T(...) custom-call(s32[3]{0:T(128)S(1)} %pad_add_fusion.place_ref, ...), custom_call_target="tpu_custom_call" | custom-call | flops 679477248 | bytes 1769488 | tf_op jit(solution)/shard_map/pallas_call | solution.py:364
  120.4 3.3 %collective-permute-start.30 = (f32[4,3,24,128]{3,2,1,0:T(8,128)S(1)}, f32[4,3,24,128]{3,2,1,0:T(8,128)S(1)}, u32[]{:S(2)}, u32[]{:S(2)}) collective-permute-start(f32[4,3,24,128]{3,2,1,0:T(8,128)S(1)} %get-tuple-element.63), channel_id=1, source_target_pairs={{0,7},{1,6},{2,5},{3,4},{4,3},{5,2},{6,1},{7,0},{8,15},{9,14},{10,... | collective-permute-start | bytes 442376 | tf_op jit(solution)/shard_map/ppermute | solution.py:447
  123.7 2.4 %collective-permute-start.31 = (f32[4,3,24,128]{3,2,1,0:T(8,128)S(1)}, f32[4,3,24,128]{3,2,1,0:T(8,128)S(1)}, u32[]{:S(2)}, u32[]{:S(2)}) collective-permute-start(f32[4,3,24,128]{3,2,1,0:T(8,128)S(1)} %get-tuple-element.64), channel_id=1, source_target_pairs={{0,5},{1,4},{2,7},{3,6},{4,1},{5,0},{6,3},{7,2},{8,13},{9,12},{10,... | collective-permute-start | bytes 442376 | tf_op jit(solution)/shard_map/ppermute | solution.py:447
  126.1 1.9 %collective-permute-start.32 = (f32[4,3,24,128]{3,2,1,0:T(8,128)S(1)}, f32[4,3,24,128]{3,2,1,0:T(8,128)S(1)}, u32[]{:S(2)}, u32[]{:S(2)}) collective-permute-start(f32[4,3,24,128]{3,2,1,0:T(8,128)S(1)} %get-tuple-element.65), channel_id=1, source_target_pairs={{0,3},{1,2},{2,1},{3,0},{4,7},{5,6},{6,5},{7,4},{8,11},{9,10},{10,... | collective-permute-start | bytes 442376 | tf_op jit(solution)/shard_map/ppermute | solution.py:447
  128.0 1.5 %collective-permute-start.33 = (f32[4,3,24,128]{3,2,1,0:T(8,128)S(1)}, f32[4,3,24,128]{3,2,1,0:T(8,128)S(1)}, u32[]{:S(2)}, u32[]{:S(2)}) collective-permute-start(f32[4,3,24,128]{3,2,1,0:T(8,128)S(1)} %get-tuple-element.66), channel_id=1, source_target_pairs={{0,4},{1,5},{2,6},{3,7},{4,0},{5,1},{6,2},{7,3},{8,12},{9,13},{10,... | collective-permute-start | bytes 442376 | tf_op jit(solution)/shard_map/ppermute | solution.py:447
  129.5 1.9 %collective-permute-start.34 = (f32[4,3,24,128]{3,2,1,0:T(8,128)S(1)}, f32[4,3,24,128]{3,2,1,0:T(8,128)S(1)}, u32[]{:S(2)}, u32[]{:S(2)}) collective-permute-start(f32[4,3,24,128]{3,2,1,0:T(8,128)S(1)} %get-tuple-element.67), channel_id=1, source_target_pairs={{0,1},{1,0},{2,3},{3,2},{4,5},{5,4},{6,7},{7,6},{8,9},{9,8},{10,11... | collective-permute-start | bytes 442376 | tf_op jit(solution)/shard_map/ppermute | solution.py:447
  131.4 5.6 %collective-permute-start.35 = (f32[4,3,24,128]{3,2,1,0:T(8,128)S(1)}, f32[4,3,24,128]{3,2,1,0:T(8,128)S(1)}, u32[]{:S(2)}, u32[]{:S(2)}) collective-permute-start(f32[4,3,24,128]{3,2,1,0:T(8,128)S(1)} %get-tuple-element.68), channel_id=1, source_target_pairs={{0,6},{1,7},{2,4},{3,5},{4,2},{5,3},{6,0},{7,1},{8,14},{9,15},{10,... | collective-permute-start | bytes 442376 | tf_op jit(solution)/shard_map/ppermute | solution.py:447
  137.0 1.8 %shard_map.67 = f32[2,24,192]{2,1,0:T(8,128)} custom-call(s32[3]{0:T(128)S(1)} %pad_add_fusion.place_ref, f32[2,192,192]{2,1,0:T(8,128)S(1)} %shard_map.64.mine_ref, f32[2,192,192]{2,1,0:T(8,128)S(1)} %collective-permute-done.29.other_ref), custom_call_target="tpu_custom_call" | custom-call | flops 113246208 | bytes 589840 | tf_op jit(solution)/shard_map/pallas_call | solution.py:364
  138.8 1.8 %collective-permute-done.33.refs_4_ = f32[4,3,24,128]{3,2,1,0:T(8,128)S(1)} collective-permute-done((f32[4,3,24,128]{3,2,1,0:T(8,128)S(1)}, f32[4,3,24,128]{3,2,1,0:T(8,128)S(1)}, u32[]{:S(2)}, u32[]{:S(2)}) %collective-permute-start.33) | collective-permute-done | bytes 147488 | tf_op jit(solution)/shard_map/ppermute | solution.py:447
  140.6 0.8 collective-permute-done.35.refs_6_
  141.4 0.8 collective-permute-done.36.refs_7_
  142.1 2.4 %shard_map.66 = f32[2304,128]{1,0:T(8,128)} custom-call(s32[3]{0:T(128)S(1)} %pad_add_fusion.place_ref, f32[4,3,24,128]{3,2,1,0:T(8,128)S(1)} %get-tuple-element.62.refs_0_, f32[4,3,24,128]{3,2,1,0:T(8,128)S(1)} %collective-permute-done.30.refs_1_, f32[4,3,24,128]{3,2,1,0:T(8,128)S(1)} %collective-permute-done.31.refs_2_, ...), custom_call_target="tpu_custom_call" | custom-call | bytes 1179664 | tf_op jit(solution)/shard_map/pallas_call | solution.py:364
  (52 shorter events, 0.8 us)
Async XLA Ops:
  2.0 14.6 %copy-start.1 = (s32[1,4096]{1,0:T(1,128)S(1)}, s32[1,4096]{1,0:T(1,128)}, u32[]{:S(2)}) copy-start(s32[1,4096]{1,0:T(1,128)} %param.5) | copy-start | bytes 49156
  2.0 21.7 %copy-start.2 = (f32[4,3,3,3]{3,0,2,1:T(4,128)S(1)}, f32[4,3,3,3]{3,0,2,1:T(4,128)}, u32[]{:S(2)}) copy-start(f32[4,3,3,3]{3,0,2,1:T(4,128)} %param.6) | copy-start | bytes 1300
  3.4 41.3 %copy-start = (f32[4]{0:T(128)S(1)}, f32[4]{0:T(128)}, u32[]{:S(2)}) copy-start(f32[4]{0:T(128)} %refs_1_.1) | copy-start | bytes 52
  3.4 13.2 %collective-permute-start.1 = (f32[4,3,24,128]{3,2,1,0:T(8,128)S(1)}, f32[4,3,24,128]{3,2,1,0:T(8,128)S(1)}, u32[]{:S(2)}, u32[]{:S(2)}) collective-permute-start(f32[4,3,24,128]{3,2,1,0:T(8,128)S(1)} %get-tuple-element.38), channel_id=1, source_target_pairs={{0,7},{1,6},{2,5},{3,4},{4,3},{5,2},{6,1},{7,0},{8,15},{9,14},{10,... | collective-permute-start | bytes 442376 | tf_op jit(solution)/shard_map/ppermute | solution.py:447
  9.6 11.7 %collective-permute-start.2 = (f32[4,3,24,128]{3,2,1,0:T(8,128)S(1)}, f32[4,3,24,128]{3,2,1,0:T(8,128)S(1)}, u32[]{:S(2)}, u32[]{:S(2)}) collective-permute-start(f32[4,3,24,128]{3,2,1,0:T(8,128)S(1)} %get-tuple-element.39), channel_id=1, source_target_pairs={{0,5},{1,4},{2,7},{3,6},{4,1},{5,0},{6,3},{7,2},{8,13},{9,12},{10,... | collective-permute-start | bytes 442376 | tf_op jit(solution)/shard_map/ppermute | solution.py:447
  9.9 11.9 %collective-permute-start.3 = (f32[4,3,24,128]{3,2,1,0:T(8,128)S(1)}, f32[4,3,24,128]{3,2,1,0:T(8,128)S(1)}, u32[]{:S(2)}, u32[]{:S(2)}) collective-permute-start(f32[4,3,24,128]{3,2,1,0:T(8,128)S(1)} %get-tuple-element.40), channel_id=1, source_target_pairs={{0,3},{1,2},{2,1},{3,0},{4,7},{5,6},{6,5},{7,4},{8,11},{9,10},{10,... | collective-permute-start | bytes 442376 | tf_op jit(solution)/shard_map/ppermute | solution.py:447
  13.3 12.1 %collective-permute-start.4 = (f32[4,3,24,128]{3,2,1,0:T(8,128)S(1)}, f32[4,3,24,128]{3,2,1,0:T(8,128)S(1)}, u32[]{:S(2)}, u32[]{:S(2)}) collective-permute-start(f32[4,3,24,128]{3,2,1,0:T(8,128)S(1)} %get-tuple-element.41), channel_id=1, source_target_pairs={{0,4},{1,5},{2,6},{3,7},{4,0},{5,1},{6,2},{7,3},{8,12},{9,13},{10,... | collective-permute-start | bytes 442376 | tf_op jit(solution)/shard_map/ppermute | solution.py:447
  16.3 9.1 %collective-permute-start.5 = (f32[4,3,24,128]{3,2,1,0:T(8,128)S(1)}, f32[4,3,24,128]{3,2,1,0:T(8,128)S(1)}, u32[]{:S(2)}, u32[]{:S(2)}) collective-permute-start(f32[4,3,24,128]{3,2,1,0:T(8,128)S(1)} %get-tuple-element.42), channel_id=1, source_target_pairs={{0,1},{1,0},{2,3},{3,2},{4,5},{5,4},{6,7},{7,6},{8,9},{9,8},{10,11... | collective-permute-start | bytes 442376 | tf_op jit(solution)/shard_map/ppermute | solution.py:447
  16.6 8.8 %collective-permute-start.6 = (f32[4,3,24,128]{3,2,1,0:T(8,128)S(1)}, f32[4,3,24,128]{3,2,1,0:T(8,128)S(1)}, u32[]{:S(2)}, u32[]{:S(2)}) collective-permute-start(f32[4,3,24,128]{3,2,1,0:T(8,128)S(1)} %get-tuple-element.43), channel_id=1, source_target_pairs={{0,6},{1,7},{2,4},{3,5},{4,2},{5,3},{6,0},{7,1},{8,14},{9,15},{10,... | collective-permute-start | bytes 442376 | tf_op jit(solution)/shard_map/ppermute | solution.py:447
  21.3 5.1 %collective-permute-start.7 = (f32[4,3,24,128]{3,2,1,0:T(8,128)S(1)}, f32[4,3,24,128]{3,2,1,0:T(8,128)S(1)}, u32[]{:S(2)}, u32[]{:S(2)}) collective-permute-start(f32[4,3,24,128]{3,2,1,0:T(8,128)S(1)} %get-tuple-element.44), channel_id=1, source_target_pairs={{0,2},{1,3},{2,0},{3,1},{4,6},{5,7},{6,4},{7,5},{8,10},{9,11},{10,... | collective-permute-start | bytes 442376 | tf_op jit(solution)/shard_map/ppermute | solution.py:447
  21.8 9.1 %collective-permute-start = (s32[1,4096]{1,0:T(1,128)S(1)}, s32[1,4096]{1,0:T(1,128)S(1)}, u32[]{:S(2)}, u32[]{:S(2)}) collective-permute-start(s32[1,4096]{1,0:T(1,128)S(1)} %copy-done.1), channel_id=1, source_target_pairs={{0,8},{8,16},{16,24},{24,32},{32,40},{40,48},{48,56},{56,64},{64,7... | collective-permute-start | bytes 49160 | tf_op jit(solution)/shard_map/ppermute | solution.py:51
  27.2 17.5 %collective-permute-start.10 = (f32[8,4,3,24,128]{4,3,2,1,0:T(8,128)S(1)}, f32[8,4,3,24,128]{4,3,2,1,0:T(8,128)S(1)}, u32[]{:S(2)}, u32[]{:S(2)}) collective-permute-start(f32[8,4,3,24,128]{4,3,2,1,0:T(8,128)S(1)} %get-tuple-element.45.u_ref.b_ref), channel_id=1, source_target_pairs={{8,16},{16,8},{24,32},{32,24},{40,48},{48,40},{56,64},{64,56},{72,... | collective-permute-start | bytes 3538952 | tf_op jit(solution)/shard_map/ppermute | solution.py:453
  29.1 15.6 %collective-permute-start.11 = (f32[8,4,3,24,128]{4,3,2,1,0:T(8,128)S(1)}, f32[8,4,3,24,128]{4,3,2,1,0:T(8,128)S(1)}, u32[]{:S(2)}, u32[]{:S(2)}) collective-permute-start(f32[8,4,3,24,128]{4,3,2,1,0:T(8,128)S(1)} %get-tuple-element.45.u_ref.b_ref), channel_id=1, source_target_pairs={{0,8},{8,0},{16,24},{24,16},{32,40},{40,32},{48,56},{56,48},{64,72... | collective-permute-start | bytes 3538952 | tf_op jit(solution)/shard_map/ppermute | solution.py:454
  30.9 5.2 %collective-permute-start.8 = (f32[4,3,24,128]{3,2,1,0:T(8,128)S(1)}, f32[4,3,24,128]{3,2,1,0:T(8,128)S(1)}, u32[]{:S(2)}, u32[]{:S(2)}) collective-permute-start(f32[4,3,24,128]{3,2,1,0:T(8,128)S(1)} %get-tuple-element.46), channel_id=1, source_target_pairs={{0,2},{2,4},{4,6},{6,7},{7,5},{5,3},{3,1},{8,10},{10,12},{12,14},{... | collective-permute-start | bytes 442376 | tf_op jit(solution)/shard_map/ppermute | solution.py:51
  32.8 7.4 %collective-permute-start.9 = (f32[4,3,24,128]{3,2,1,0:T(8,128)S(1)}, f32[4,3,24,128]{3,2,1,0:T(8,128)S(1)}, u32[]{:S(2)}, u32[]{:S(2)}) collective-permute-start(f32[4,3,24,128]{3,2,1,0:T(8,128)S(1)} %get-tuple-element.47), channel_id=1, source_target_pairs={{2,0},{4,2},{6,4},{7,6},{5,7},{3,5},{1,3},{10,8},{12,10},{14,12},{... | collective-permute-start | bytes 442376 | tf_op jit(solution)/shard_map/ppermute | solution.py:51
  48.4 17.5 %collective-permute-start.14 = (f32[8,4,3,24,128]{4,3,2,1,0:T(8,128)S(1)}, f32[8,4,3,24,128]{4,3,2,1,0:T(8,128)S(1)}, u32[]{:S(2)}, u32[]{:S(2)}) collective-permute-start(f32[8,4,3,24,128]{4,3,2,1,0:T(8,128)S(1)} %get-tuple-element.48.a_ref.refs_3_), channel_id=1, source_target_pairs={{8,16},{16,8},{24,32},{32,24},{40,48},{48,40},{56,64},{64,56},{72,... | collective-permute-start | bytes 3538952 | tf_op jit(solution)/shard_map/ppermute | solution.py:453
  50.4 15.6 %collective-permute-start.15 = (f32[8,4,3,24,128]{4,3,2,1,0:T(8,128)S(1)}, f32[8,4,3,24,128]{4,3,2,1,0:T(8,128)S(1)}, u32[]{:S(2)}, u32[]{:S(2)}) collective-permute-start(f32[8,4,3,24,128]{4,3,2,1,0:T(8,128)S(1)} %get-tuple-element.48.a_ref.refs_3_), channel_id=1, source_target_pairs={{0,8},{8,0},{16,24},{24,16},{32,40},{40,32},{48,56},{56,48},{64,72... | collective-permute-start | bytes 3538952 | tf_op jit(solution)/shard_map/ppermute | solution.py:454
  52.1 5.7 %collective-permute-start.12 = (f32[4,3,24,128]{3,2,1,0:T(8,128)S(1)}, f32[4,3,24,128]{3,2,1,0:T(8,128)S(1)}, u32[]{:S(2)}, u32[]{:S(2)}) collective-permute-start(f32[4,3,24,128]{3,2,1,0:T(8,128)S(1)} %get-tuple-element.49), channel_id=1, source_target_pairs={{0,2},{2,4},{4,6},{6,7},{7,5},{5,3},{3,1},{8,10},{10,12},{12,14},{... | collective-permute-start | bytes 442376 | tf_op jit(solution)/shard_map/ppermute | solution.py:51
  54.0 7.4 %collective-permute-start.13 = (f32[4,3,24,128]{3,2,1,0:T(8,128)S(1)}, f32[4,3,24,128]{3,2,1,0:T(8,128)S(1)}, u32[]{:S(2)}, u32[]{:S(2)}) collective-permute-start(f32[4,3,24,128]{3,2,1,0:T(8,128)S(1)} %get-tuple-element.50), channel_id=1, source_target_pairs={{2,0},{4,2},{6,4},{7,6},{5,7},{3,5},{1,3},{10,8},{12,10},{14,12},{... | collective-permute-start | bytes 442376 | tf_op jit(solution)/shard_map/ppermute | solution.py:51
  71.7 1.5 %collective-permute-start.16 = (f32[384,128]{1,0:T(8,128)S(1)}, f32[384,128]{1,0:T(8,128)S(1)}, u32[]{:S(2)}, u32[]{:S(2)}) collective-permute-start(f32[384,128]{1,0:T(8,128)S(1)} %get-tuple-element.52), channel_id=1, source_target_pairs={{0,8},{1,9},{2,10},{3,11},{4,12},{5,13},{6,14},{7,15},{8,0},{9,1},... | collective-permute-start | bytes 589832 | tf_op jit(solution)/shard_map/ppermute | solution.py:45
  73.3 8.6 %collective-permute-start.17 = (f32[96,128]{1,0:T(8,128)S(1)}, f32[96,128]{1,0:T(8,128)S(1)}, u32[]{:S(2)}, u32[]{:S(2)}) collective-permute-start(f32[96,128]{1,0:T(8,128)S(1)} %get-tuple-element.76), channel_id=1, source_target_pairs={{0,4},{1,5},{2,6},{3,7},{4,0},{5,1},{6,2},{7,3},{8,12},{9,13},{10,... | collective-permute-start | bytes 147464 | tf_op jit(solution)/shard_map/ppermute | solution.py:45
  78.4 5.3 %collective-permute-start.18 = (f32[96,128]{1,0:T(8,128)S(1)}, f32[96,128]{1,0:T(8,128)S(1)}, u32[]{:S(2)}, u32[]{:S(2)}) collective-permute-start(f32[96,128]{1,0:T(8,128)S(1)} %get-tuple-element.78), channel_id=1, source_target_pairs={{0,2},{1,3},{2,4},{3,5},{4,6},{5,7},{6,0},{7,1},{8,10},{9,11},{10,... | collective-permute-start | bytes 147464 | tf_op jit(solution)/shard_map/ppermute | solution.py:45
  81.8 4.1 %collective-permute-start.19 = (f32[96,128]{1,0:T(8,128)S(1)}, f32[96,128]{1,0:T(8,128)S(1)}, u32[]{:S(2)}, u32[]{:S(2)}) collective-permute-start(f32[96,128]{1,0:T(8,128)S(1)} %get-tuple-element.77), channel_id=1, source_target_pairs={{0,6},{1,7},{2,0},{3,1},{4,2},{5,3},{6,4},{7,5},{8,14},{9,15},{10,... | collective-permute-start | bytes 147464 | tf_op jit(solution)/shard_map/ppermute | solution.py:45
  85.9 5.9 %collective-permute-start.20 = (f32[96,128]{1,0:T(8,128)S(1)}, f32[96,128]{1,0:T(8,128)S(1)}, u32[]{:S(2)}, u32[]{:S(2)}) collective-permute-start(f32[96,128]{1,0:T(8,128)S(1)} %add_add_fusion.2), channel_id=1, source_target_pairs={{0,32},{1,33},{2,34},{3,35},{4,36},{5,37},{6,38},{7,39},{8,40},{9,... | collective-permute-start | bytes 147464 | tf_op jit(solution)/shard_map/ppermute | solution.py:45
  86.0 7.5 %collective-permute-start.21 = (f32[96,128]{1,0:T(8,128)S(1)}, f32[96,128]{1,0:T(8,128)S(1)}, u32[]{:S(2)}, u32[]{:S(2)}) collective-permute-start(f32[96,128]{1,0:T(8,128)S(1)} %add_add_fusion.2), channel_id=1, source_target_pairs={{0,16},{1,17},{2,18},{3,19},{4,20},{5,21},{6,22},{7,23},{8,24},{9,... | collective-permute-start | bytes 147464 | tf_op jit(solution)/shard_map/ppermute | solution.py:45
  91.8 4.1 %collective-permute-start.22 = (f32[96,128]{1,0:T(8,128)S(1)}, f32[96,128]{1,0:T(8,128)S(1)}, u32[]{:S(2)}, u32[]{:S(2)}) collective-permute-start(f32[96,128]{1,0:T(8,128)S(1)} %add_add_fusion.2), channel_id=1, source_target_pairs={{0,48},{1,49},{2,50},{3,51},{4,52},{5,53},{6,54},{7,55},{8,56},{9,... | collective-permute-start | bytes 147464 | tf_op jit(solution)/shard_map/ppermute | solution.py:45
  95.9 5.8 %collective-permute-start.23 = (f32[96,128]{1,0:T(8,128)S(1)}, f32[96,128]{1,0:T(8,128)S(1)}, u32[]{:S(2)}, u32[]{:S(2)}) collective-permute-start(f32[96,128]{1,0:T(8,128)S(1)} %add_add_fusion.1), channel_id=1, source_target_pairs={{0,1},{1,0},{2,3},{3,2},{4,5},{5,4},{6,7},{7,6},{8,9},{9,8},{10,11... | collective-permute-start | bytes 147464 | tf_op jit(solution)/shard_map/ppermute | solution.py:45
  96.2 5.8 %collective-permute-start.24 = (f32[96,128]{1,0:T(8,128)S(1)}, f32[96,128]{1,0:T(8,128)S(1)}, u32[]{:S(2)}, u32[]{:S(2)}) collective-permute-start(f32[96,128]{1,0:T(8,128)S(1)} %add_add_fusion.1), channel_id=1, source_target_pairs={{0,64},{1,65},{2,66},{3,67},{4,68},{5,69},{6,70},{7,71},{8,72},{9,... | collective-permute-start | bytes 147464 | tf_op jit(solution)/shard_map/ppermute | solution.py:45
  96.6 5.4 %collective-permute-start.25 = (f32[96,128]{1,0:T(8,128)S(1)}, f32[96,128]{1,0:T(8,128)S(1)}, u32[]{:S(2)}, u32[]{:S(2)}) collective-permute-start(f32[96,128]{1,0:T(8,128)S(1)} %add_add_fusion.1), channel_id=1, source_target_pairs={{0,65},{1,64},{2,67},{3,66},{4,69},{5,68},{6,71},{7,70},{8,73},{9,... | collective-permute-start | bytes 147464 | tf_op jit(solution)/shard_map/ppermute | solution.py:45
  102.0 5.9 %collective-permute-start.26 = (f32[96,128]{1,0:T(8,128)S(1)}, f32[96,128]{1,0:T(8,128)S(1)}, u32[]{:S(2)}, u32[]{:S(2)}) collective-permute-start(f32[96,128]{1,0:T(8,128)S(1)} %add_add_fusion), channel_id=1, source_target_pairs={{0,2},{1,3},{2,4},{3,5},{4,6},{5,7},{6,0},{7,1},{8,10},{9,11},{10,... | collective-permute-start | bytes 147464 | tf_op jit(solution)/shard_map/ppermute | solution.py:45
  102.1 5.8 %collective-permute-start.27 = (f32[96,128]{1,0:T(8,128)S(1)}, f32[96,128]{1,0:T(8,128)S(1)}, u32[]{:S(2)}, u32[]{:S(2)}) collective-permute-start(f32[96,128]{1,0:T(8,128)S(1)} %add_add_fusion), channel_id=1, source_target_pairs={{0,4},{1,5},{2,6},{3,7},{4,0},{5,1},{6,2},{7,3},{8,12},{9,13},{10,... | collective-permute-start | bytes 147464 | tf_op jit(solution)/shard_map/ppermute | solution.py:45
  104.9 4.1 %collective-permute-start.28 = (f32[96,128]{1,0:T(8,128)S(1)}, f32[96,128]{1,0:T(8,128)S(1)}, u32[]{:S(2)}, u32[]{:S(2)}) collective-permute-start(f32[96,128]{1,0:T(8,128)S(1)} %add_add_fusion), channel_id=1, source_target_pairs={{0,6},{1,7},{2,0},{3,1},{4,2},{5,3},{6,4},{7,5},{8,14},{9,15},{10,... | collective-permute-start | bytes 147464 | tf_op jit(solution)/shard_map/ppermute | solution.py:45
  116.9 1.8 %collective-permute-start.29 = (f32[2,192,192]{2,1,0:T(8,128)S(1)}, f32[2,192,192]{2,1,0:T(8,128)S(1)}, u32[]{:S(2)}, u32[]{:S(2)}) collective-permute-start(f32[2,192,192]{2,1,0:T(8,128)S(1)} %shard_map.64.mine_ref), channel_id=1, source_target_pairs={{0,8},{1,9},{2,10},{3,11},{4,12},{5,13},{6,14},{7,15},{8,0},{9,1},... | collective-permute-start | bytes 884744 | tf_op jit(solution)/shard_map/ppermute | solution.py:45
  120.4 11.1 %collective-permute-start.30 = (f32[4,3,24,128]{3,2,1,0:T(8,128)S(1)}, f32[4,3,24,128]{3,2,1,0:T(8,128)S(1)}, u32[]{:S(2)}, u32[]{:S(2)}) collective-permute-start(f32[4,3,24,128]{3,2,1,0:T(8,128)S(1)} %get-tuple-element.63), channel_id=1, source_target_pairs={{0,7},{1,6},{2,5},{3,4},{4,3},{5,2},{6,1},{7,0},{8,15},{9,14},{10,... | collective-permute-start | bytes 442376 | tf_op jit(solution)/shard_map/ppermute | solution.py:447
  123.7 13.3 %collective-permute-start.31 = (f32[4,3,24,128]{3,2,1,0:T(8,128)S(1)}, f32[4,3,24,128]{3,2,1,0:T(8,128)S(1)}, u32[]{:S(2)}, u32[]{:S(2)}) collective-permute-start(f32[4,3,24,128]{3,2,1,0:T(8,128)S(1)} %get-tuple-element.64), channel_id=1, source_target_pairs={{0,5},{1,4},{2,7},{3,6},{4,1},{5,0},{6,3},{7,2},{8,13},{9,12},{10,... | collective-permute-start | bytes 442376 | tf_op jit(solution)/shard_map/ppermute | solution.py:447
  126.1 12.6 %collective-permute-start.32 = (f32[4,3,24,128]{3,2,1,0:T(8,128)S(1)}, f32[4,3,24,128]{3,2,1,0:T(8,128)S(1)}, u32[]{:S(2)}, u32[]{:S(2)}) collective-permute-start(f32[4,3,24,128]{3,2,1,0:T(8,128)S(1)} %get-tuple-element.65), channel_id=1, source_target_pairs={{0,3},{1,2},{2,1},{3,0},{4,7},{5,6},{6,5},{7,4},{8,11},{9,10},{10,... | collective-permute-start | bytes 442376 | tf_op jit(solution)/shard_map/ppermute | solution.py:447
  128.0 12.6 %collective-permute-start.33 = (f32[4,3,24,128]{3,2,1,0:T(8,128)S(1)}, f32[4,3,24,128]{3,2,1,0:T(8,128)S(1)}, u32[]{:S(2)}, u32[]{:S(2)}) collective-permute-start(f32[4,3,24,128]{3,2,1,0:T(8,128)S(1)} %get-tuple-element.66), channel_id=1, source_target_pairs={{0,4},{1,5},{2,6},{3,7},{4,0},{5,1},{6,2},{7,3},{8,12},{9,13},{10,... | collective-permute-start | bytes 442376 | tf_op jit(solution)/shard_map/ppermute | solution.py:447
  129.5 11.1 %collective-permute-start.34 = (f32[4,3,24,128]{3,2,1,0:T(8,128)S(1)}, f32[4,3,24,128]{3,2,1,0:T(8,128)S(1)}, u32[]{:S(2)}, u32[]{:S(2)}) collective-permute-start(f32[4,3,24,128]{3,2,1,0:T(8,128)S(1)} %get-tuple-element.67), channel_id=1, source_target_pairs={{0,1},{1,0},{2,3},{3,2},{4,5},{5,4},{6,7},{7,6},{8,9},{9,8},{10,11... | collective-permute-start | bytes 442376 | tf_op jit(solution)/shard_map/ppermute | solution.py:447
  131.4 9.9 %collective-permute-start.35 = (f32[4,3,24,128]{3,2,1,0:T(8,128)S(1)}, f32[4,3,24,128]{3,2,1,0:T(8,128)S(1)}, u32[]{:S(2)}, u32[]{:S(2)}) collective-permute-start(f32[4,3,24,128]{3,2,1,0:T(8,128)S(1)} %get-tuple-element.68), channel_id=1, source_target_pairs={{0,6},{1,7},{2,4},{3,5},{4,2},{5,3},{6,0},{7,1},{8,14},{9,15},{10,... | collective-permute-start | bytes 442376 | tf_op jit(solution)/shard_map/ppermute | solution.py:447
  137.0 5.1 %collective-permute-start.36 = (f32[4,3,24,128]{3,2,1,0:T(8,128)S(1)}, f32[4,3,24,128]{3,2,1,0:T(8,128)S(1)}, u32[]{:S(2)}, u32[]{:S(2)}) collective-permute-start(f32[4,3,24,128]{3,2,1,0:T(8,128)S(1)} %get-tuple-element.69), channel_id=1, source_target_pairs={{0,2},{1,3},{2,0},{3,1},{4,6},{5,7},{6,4},{7,5},{8,10},{9,11},{10,... | collective-permute-start | bytes 442376 | tf_op jit(solution)/shard_map/ppermute | solution.py:447

commit v3 on v2

--- a/solution.py
+++ b/solution.py
@@ -131,8 +131,8 @@
         cls = jnp.broadcast_to(cls_ref[5, t : t + 1, :], (SUB, LANES))
         coef_ref[t, 30] = pick(cls, [mass_ref[level] for level in range(LEVELS)])
 
-    def mix(t, face, d):
-        s = [coef_ref[t, face * 6 + i] for i in range(6)]
+    def mix(coef, face, d):
+        s = coef[face * 6 : face * 6 + 6]
         return [
             s[ENTRY_OF[min(a, 0), max(a, 0)]] * d[0]
             + s[ENTRY_OF[min(a, 1), max(a, 1)]] * d[1]
@@ -146,37 +146,44 @@
     def body(i, carry):
         q = i // steps
         rows = pl.ds(pl.multiple_of((i % steps) * SUB, SUB), SUB)
-        ends = []
+        places = (q, q + half)
+        below = [yd_ref[q, c, rows, :] for c in range(3)]
+        above = [yu_ref[q, c, rows, :] for c in range(3)]
+        window = [[below, None], [[turn(a) for a in below], None]]
+        here = [[u_ref[g, 0, c, rows, :] for c in range(3)] for g in places]
         for part in range(2):
-            g = q + part * half
-            tiles = [[u_ref[g, t, c, rows, :] for c in range(3)] for t in range(per)]
-            below = [yd_ref[q, c, rows, :] for c in range(3)]
-            above = [yu_ref[q, c, rows, :] for c in range(3)]
-            if part == 0:
-                above = [turn(a) for a in above]
-            else:
-                below = [turn(a) for a in below]
-            swaps = [below] + [[turn(a) for a in line] for line in tiles] + [above]
+            window[part][1] = [turn(a) for a in here[part]]
+        for t in range(per):
+            coef = [coef_ref[t, n] for n in range(31)]
             done = []
-            for t in range(per):
-                u = tiles[t]
-                f = mix(t, 0, [pltpu.roll(u[c], LANES - 1, 1) - u[c] for c in range(3)])
-                acc = [coef_ref[t, 30] * u[c] + (pltpu.roll(f[c], 1, 1) - f[c]) for c in range(3)]
-                f = mix(t, 1, [jnp.where(low, swaps[t + 1][c], swaps[t + 2][c]) - u[c] for c in range(3)])
+            for part, g in enumerate(places):
+                u = here[part]
+                if t + 1 < per:
+                    here[part] = [u_ref[g, t + 1, c, rows, :] for c in range(3)]
+                    after = [turn(a) for a in here[part]]
+                else:
+                    after = above if part else [turn(a) for a in above]
+                before, swap = window[part]
+                window[part] = [swap, after]
+                f = mix(coef, 0, [pltpu.roll(u[c], LANES - 1, 1) - u[c] for c in range(3)])
+                acc = [coef[30] * u[c] + (pltpu.roll(f[c], 1, 1) - f[c]) for c in range(3)]
+                f = mix(coef, 1, [jnp.where(low, swap[c], after[c]) - u[c] for c in range(3)])
                 acc = [acc[c] - f[c] for c in range(3)]
-                f = mix(t, 2, [u[c] - jnp.where(low, swaps[t][c], swaps[t + 1][c]) for c in range(3)])
+                f = mix(coef, 2, [u[c] - jnp.where(low, before[c], swap[c]) for c in range(3)])
                 acc = [acc[c] + f[c] for c in range(3)]
-                f = mix(t, 3, [za_ref[g, t, c, rows, :] - u[c] for c in range(3)])
+                f = mix(coef, 3, [za_ref[g, t, c, rows, :] - u[c] for c in range(3)])
                 acc = [acc[c] - f[c] for c in range(3)]
-                f = mix(t, 4, [zb_ref[g, t, c, rows, :] - u[c] for c in range(3)])
+                f = mix(coef, 4, [zb_ref[g, t, c, rows, :] - u[c] for c in range(3)])
                 done.append([acc[c] - f[c] for c in range(3)])
+            for g, line in zip(places, done):
                 for c in range(3):
-                    w_ref[g, t, c, rows, :] = done[t][c]
-            ends.append((done[0], done[-1]))
-        if edges:
-            for c in range(3):
-                near, far = [[end[c] for end in pair] for pair in ends]
-                pack_edges(low, near, far, *edges, (q, c, rows, slice(None)))
+                    w_ref[g, t, c, rows, :] = line[c]
+            if edges and t == 0:
+                for c in range(3):
+                    edges[0][q, c, rows, :] = jnp.where(low, done[0][c], turn(done[1][c]))
+            if edges and t == per - 1:
+                for c in range(3):
+                    edges[1][q, c, rows, :] = jnp.where(low, turn(done[0][c]), done[1][c])
         return carry
 
     lax.fori_loop(0, half * steps, body, 0)

time: 145 us -> 145 us (level)
  no operation moved by 1% of the time
where the time goes in v3:
time: 145 us
  starting transfers between devices  68.1 us (47%)
  waiting for transfers between devices  45.6 us (31%)
  Pallas kernels  27.4 us (19%)
  local copies, waits for them, and re-layouts  1.99 us (1%)
    ppermute x14, starting transfers between devices, exchange(): lax.ppermute(a, 'vec', [(i, i ^ k) for i in range(groups)])  30.9 us
    pallas_call x9, Pallas kernels, call(): pl.pallas_call(kernel, out_shape=[jax.ShapeDtypeStruct(dims, jnp.float32)...  27.4 us
    ppermute x14, starting transfers between devices, route(): return lax.ppermute(array, ('space', 'vec'), pairs)  21.6 us
    ppermute x14, waiting for transfers between devices, route(): return lax.ppermute(array, ('space', 'vec'), pairs)  17.4 us
    ppermute x5, waiting for transfers between devices, step_along(): return lax.ppermute(array, axis, pairs)  9.69 us
    ppermute x14, waiting for transfers between devices, exchange(): lax.ppermute(a, 'vec', [(i, i ^ k) for i in range(groups)])  9.51 us
    ppermute x2, waiting for transfers between devices, halo(): lax.ppermute(u, 'space', [(i, i + (1 if i % 2 else -1)) for i in range(1,...  8.99 us
    ppermute x5, starting transfers between devices, step_along(): return lax.ppermute(array, axis, pairs)  8.32 us
  transfers between devices with their start and end apart: 37, of which 22 were waited for; matrix products, arithmetic and copies ran while one was open for 0% of the time, Pallas kernels for 3%

profile of v3, /device:TPU:8, one launch (start us, length us, event | category | flops | bytes accessed | tf_op | source)
XLA Modules:
  0.0 144.5 jit_solution(9906380508965011047)
XLA Ops:
  0.7 1.4 pad.5.x_ref
  2.1 1.3 shard_map.59
  3.4 6.2 %collective-permute-start.1 = (f32[4,3,24,128]{3,2,1,0:T(8,128)S(1)}, f32[4,3,24,128]{3,2,1,0:T(8,128)S(1)}, u32[]{:S(2)}, u32[]{:S(2)}) collective-permute-start(f32[4,3,24,128]{3,2,1,0:T(8,128)S(1)} %get-tuple-element.38), channel_id=1, source_target_pairs={{0,7},{1,6},{2,5},{3,4},{4,3},{5,2},{6,1},{7,0},{8,15},{9,14},{10,... | collective-permute-start | bytes 442376 | tf_op jit(solution)/shard_map/ppermute | solution.py:454
  9.6 0.4 collective-permute-start.2
  9.9 3.4 %collective-permute-start.3 = (f32[4,3,24,128]{3,2,1,0:T(8,128)S(1)}, f32[4,3,24,128]{3,2,1,0:T(8,128)S(1)}, u32[]{:S(2)}, u32[]{:S(2)}) collective-permute-start(f32[4,3,24,128]{3,2,1,0:T(8,128)S(1)} %get-tuple-element.40), channel_id=1, source_target_pairs={{0,3},{1,2},{2,1},{3,0},{4,7},{5,6},{6,5},{7,4},{8,11},{9,10},{10,... | collective-permute-start | bytes 442376 | tf_op jit(solution)/shard_map/ppermute | solution.py:454
  13.3 3.0 %collective-permute-start.4 = (f32[4,3,24,128]{3,2,1,0:T(8,128)S(1)}, f32[4,3,24,128]{3,2,1,0:T(8,128)S(1)}, u32[]{:S(2)}, u32[]{:S(2)}) collective-permute-start(f32[4,3,24,128]{3,2,1,0:T(8,128)S(1)} %get-tuple-element.41), channel_id=1, source_target_pairs={{0,4},{1,5},{2,6},{3,7},{4,0},{5,1},{6,2},{7,3},{8,12},{9,13},{10,... | collective-permute-start | bytes 442376 | tf_op jit(solution)/shard_map/ppermute | solution.py:454
  16.3 0.1 iota.20
  16.5 0.1 iota.23
  16.6 1.3 collective-permute-start.6
  18.0 3.3 %collective-permute-done.2.refs_2_ = f32[4,3,24,128]{3,2,1,0:T(8,128)S(1)} collective-permute-done((f32[4,3,24,128]{3,2,1,0:T(8,128)S(1)}, f32[4,3,24,128]{3,2,1,0:T(8,128)S(1)}, u32[]{:S(2)}, u32[]{:S(2)}) %collective-permute-start.2) | collective-permute-done | bytes 147488 | tf_op jit(solution)/shard_map/ppermute | solution.py:454
  21.5 0.3 collective-permute-done.3.refs_3_
  21.8 1.9 %collective-permute-start = (s32[1,4096]{1,0:T(1,128)S(1)}, s32[1,4096]{1,0:T(1,128)S(1)}, u32[]{:S(2)}, u32[]{:S(2)}) collective-permute-start(s32[1,4096]{1,0:T(1,128)S(1)} %copy-done.1), channel_id=1, source_target_pairs={{0,8},{8,16},{16,24},{24,32},{32,40},{40,48},{48,56},{56,64},{64,7... | collective-permute-start | bytes 49160 | tf_op jit(solution)/shard_map/ppermute | solution.py:51
  23.8 0.1 reshape.126.stiff_ref.refs_0_
  23.9 1.5 %collective-permute-done.4.refs_4_ = f32[4,3,24,128]{3,2,1,0:T(8,128)S(1)} collective-permute-done((f32[4,3,24,128]{3,2,1,0:T(8,128)S(1)}, f32[4,3,24,128]{3,2,1,0:T(8,128)S(1)}, u32[]{:S(2)}, u32[]{:S(2)}) %collective-permute-start.4) | collective-permute-done | bytes 147488 | tf_op jit(solution)/shard_map/ppermute | solution.py:454
  25.4 1.0 collective-permute-done.7.refs_7_
  26.4 0.8 shard_map.60
  27.2 1.9 %collective-permute-start.10 = (f32[8,4,3,24,128]{4,3,2,1,0:T(8,128)S(1)}, f32[8,4,3,24,128]{4,3,2,1,0:T(8,128)S(1)}, u32[]{:S(2)}, u32[]{:S(2)}) collective-permute-start(f32[8,4,3,24,128]{4,3,2,1,0:T(8,128)S(1)} %get-tuple-element.45.u_ref.b_ref), channel_id=1, source_target_pairs={{8,16},{16,8},{24,32},{32,24},{40,48},{48,40},{56,64},{64,56},{72,... | collective-permute-start | bytes 3538952 | tf_op jit(solution)/shard_map/ppermute | solution.py:460
  29.1 1.8 %collective-permute-start.11 = (f32[8,4,3,24,128]{4,3,2,1,0:T(8,128)S(1)}, f32[8,4,3,24,128]{4,3,2,1,0:T(8,128)S(1)}, u32[]{:S(2)}, u32[]{:S(2)}) collective-permute-start(f32[8,4,3,24,128]{4,3,2,1,0:T(8,128)S(1)} %get-tuple-element.45.u_ref.b_ref), channel_id=1, source_target_pairs={{0,8},{8,0},{16,24},{24,16},{32,40},{40,32},{48,56},{56,48},{64,72... | collective-permute-start | bytes 3538952 | tf_op jit(solution)/shard_map/ppermute | solution.py:461
  30.9 1.9 %collective-permute-start.8 = (f32[4,3,24,128]{3,2,1,0:T(8,128)S(1)}, f32[4,3,24,128]{3,2,1,0:T(8,128)S(1)}, u32[]{:S(2)}, u32[]{:S(2)}) collective-permute-start(f32[4,3,24,128]{3,2,1,0:T(8,128)S(1)} %get-tuple-element.46), channel_id=1, source_target_pairs={{0,2},{2,4},{4,6},{6,7},{7,5},{5,3},{3,1},{8,10},{10,12},{12,14},{... | collective-permute-start | bytes 442376 | tf_op jit(solution)/shard_map/ppermute | solution.py:51
  32.8 1.3 collective-permute-start.9
  34.2 1.9 %collective-permute-done.8.yd_ref = f32[4,3,24,128]{3,2,1,0:T(8,128)S(1)} collective-permute-done((f32[4,3,24,128]{3,2,1,0:T(8,128)S(1)}, f32[4,3,24,128]{3,2,1,0:T(8,128)S(1)}, u32[]{:S(2)}, u32[]{:S(2)}) %collective-permute-start.8) | collective-permute-done | bytes 147488 | tf_op jit(solution)/shard_map/ppermute | solution.py:51
  36.1 4.1 %collective-permute-done.9.yu_ref = f32[4,3,24,128]{3,2,1,0:T(8,128)S(1)} collective-permute-done((f32[4,3,24,128]{3,2,1,0:T(8,128)S(1)}, f32[4,3,24,128]{3,2,1,0:T(8,128)S(1)}, u32[]{:S(2)}, u32[]{:S(2)}) %collective-permute-start.9) | collective-permute-done | bytes 147488 | tf_op jit(solution)/shard_map/ppermute | solution.py:51
  40.2 4.5 %collective-permute-done.10.za_ref = f32[8,4,3,24,128]{4,3,2,1,0:T(8,128)S(1)} collective-permute-done((f32[8,4,3,24,128]{4,3,2,1,0:T(8,128)S(1)}, f32[8,4,3,24,128]{4,3,2,1,0:T(8,128)S(1)}, u32[]{:S(2)}, u32[]{:S(2)}) %collective-permute-start.10) | collective-permute-done | bytes 1179680 | tf_op jit(solution)/shard_map/ppermute | solution.py:460
  44.7 3.6 %shard_map.61 = (f32[8,4,3,24,128]{4,3,2,1,0:T(8,128)S(1)}, f32[4,3,24,128]{3,2,1,0:T(8,128)S(1)}, f32[4,3,24,128]{3,2,1,0:T(8,128)S(1)}) custom-call(f32[108]{0:T(128)S(1)} %reshape.126.stiff_ref.refs_0_, f32[4]{0:T(128)S(1)} %copy-done, s32[6,4,128]{2,1,0:T(4,128)S(1)} %constant_dynamic-slice_fusion.3.cls_ref.refs_2_, ...), custom_call_target="tpu_custom_call" | custom-call | flops 20000000 | bytes 3846596 | tf_op jit(solution)/shard_map/pallas_call | solution.py:371
  48.3 1.9 %collective-permute-start.14 = (f32[8,4,3,24,128]{4,3,2,1,0:T(8,128)S(1)}, f32[8,4,3,24,128]{4,3,2,1,0:T(8,128)S(1)}, u32[]{:S(2)}, u32[]{:S(2)}) collective-permute-start(f32[8,4,3,24,128]{4,3,2,1,0:T(8,128)S(1)} %get-tuple-element.48.a_ref.refs_3_), channel_id=1, source_target_pairs={{8,16},{16,8},{24,32},{32,24},{40,48},{48,40},{56,64},{64,56},{72,... | collective-permute-start | bytes 3538952 | tf_op jit(solution)/shard_map/ppermute | solution.py:460
  50.3 1.8 %collective-permute-start.15 = (f32[8,4,3,24,128]{4,3,2,1,0:T(8,128)S(1)}, f32[8,4,3,24,128]{4,3,2,1,0:T(8,128)S(1)}, u32[]{:S(2)}, u32[]{:S(2)}) collective-permute-start(f32[8,4,3,24,128]{4,3,2,1,0:T(8,128)S(1)} %get-tuple-element.48.a_ref.refs_3_), channel_id=1, source_target_pairs={{0,8},{8,0},{16,24},{24,16},{32,40},{40,32},{48,56},{56,48},{64,72... | collective-permute-start | bytes 3538952 | tf_op jit(solution)/shard_map/ppermute | solution.py:461
  52.0 1.9 %collective-permute-start.12 = (f32[4,3,24,128]{3,2,1,0:T(8,128)S(1)}, f32[4,3,24,128]{3,2,1,0:T(8,128)S(1)}, u32[]{:S(2)}, u32[]{:S(2)}) collective-permute-start(f32[4,3,24,128]{3,2,1,0:T(8,128)S(1)} %get-tuple-element.49), channel_id=1, source_target_pairs={{0,2},{2,4},{4,6},{6,7},{7,5},{5,3},{3,1},{8,10},{10,12},{12,14},{... | collective-permute-start | bytes 442376 | tf_op jit(solution)/shard_map/ppermute | solution.py:51
  53.9 1.3 collective-permute-start.13
  55.2 2.4 %shard_map.62.refs_8_ = f32[384,128]{1,0:T(8,128)S(1)} custom-call(f32[8,4,3,24,128]{4,3,2,1,0:T(8,128)S(1)} %get-tuple-element.45.u_ref.b_ref, f32[8,4,3,24,128]{4,3,2,1,0:T(8,128)S(1)} %get-tuple-element.48.a_ref.refs_3_), custom_call_target="tpu_custom_call" | custom-call | flops 1358954496 | bytes 2359300 | tf_op jit(solution)/shard_map/pallas_call | solution.py:371
  57.7 3.6 %collective-permute-done.13.refs_5_ = f32[4,3,24,128]{3,2,1,0:T(8,128)S(1)} collective-permute-done((f32[4,3,24,128]{3,2,1,0:T(8,128)S(1)}, f32[4,3,24,128]{3,2,1,0:T(8,128)S(1)}, u32[]{:S(2)}, u32[]{:S(2)}) %collective-permute-start.13) | collective-permute-done | bytes 147488 | tf_op jit(solution)/shard_map/ppermute | solution.py:51
  61.3 4.5 %collective-permute-done.14.refs_6_ = f32[8,4,3,24,128]{4,3,2,1,0:T(8,128)S(1)} collective-permute-done((f32[8,4,3,24,128]{4,3,2,1,0:T(8,128)S(1)}, f32[8,4,3,24,128]{4,3,2,1,0:T(8,128)S(1)}, u32[]{:S(2)}, u32[]{:S(2)}) %collective-permute-start.14) | collective-permute-done | bytes 1179680 | tf_op jit(solution)/shard_map/ppermute | solution.py:460
  65.9 5.7 %shard_map.63 = (f32[8,4,3,24,128]{4,3,2,1,0:T(8,128)S(1)}, f32[384,128]{1,0:T(8,128)S(1)}, f32[384,128]{1,0:T(8,128)S(1)}) custom-call(s32[3]{0:T(128)S(1)} %pad_add_fusion.place_ref, f32[108]{0:T(128)S(1)} %reshape.126.stiff_ref.refs_0_, f32[4]{0:T(128)S(1)} %copy-done, s32[6,4,128]{2,1,0:T(4,128)S(1)} %constant_dynamic-slice_fusion.3.cls_ref.refs_2_, ...), custom_call_target="tpu_custom_call" | custom-call | flops 1358954496 | bytes 4043216 | tf_op jit(solution)/shard_map/pallas_call | solution.py:371
  71.5 0.2 collective-permute-start.16
  71.7 1.3 collective-permute-done.16
  73.1 5.2 %collective-permute-start.17 = (f32[96,128]{1,0:T(8,128)S(1)}, f32[96,128]{1,0:T(8,128)S(1)}, u32[]{:S(2)}, u32[]{:S(2)}) collective-permute-start(f32[96,128]{1,0:T(8,128)S(1)} %get-tuple-element.76), channel_id=1, source_target_pairs={{0,4},{1,5},{2,6},{3,7},{4,0},{5,1},{6,2},{7,3},{8,12},{9,13},{10,... | collective-permute-start | bytes 147464 | tf_op jit(solution)/shard_map/ppermute | solution.py:45
  78.3 3.4 %collective-permute-start.18 = (f32[96,128]{1,0:T(8,128)S(1)}, f32[96,128]{1,0:T(8,128)S(1)}, u32[]{:S(2)}, u32[]{:S(2)}) collective-permute-start(f32[96,128]{1,0:T(8,128)S(1)} %get-tuple-element.78), channel_id=1, source_target_pairs={{0,2},{1,3},{2,4},{3,5},{4,6},{5,7},{6,0},{7,1},{8,10},{9,11},{10,... | collective-permute-start | bytes 147464 | tf_op jit(solution)/shard_map/ppermute | solution.py:45
  81.7 1.9 %collective-permute-done.18 = f32[96,128]{1,0:T(8,128)S(1)} collective-permute-done((f32[96,128]{1,0:T(8,128)S(1)}, f32[96,128]{1,0:T(8,128)S(1)}, u32[]{:S(2)}, u32[]{:S(2)}) %collective-permute-start.18) | collective-permute-done | bytes 49184 | tf_op jit(solution)/shard_map/ppermute | solution.py:45
  83.6 2.2 %collective-permute-done.19 = f32[96,128]{1,0:T(8,128)S(1)} collective-permute-done((f32[96,128]{1,0:T(8,128)S(1)}, f32[96,128]{1,0:T(8,128)S(1)}, u32[]{:S(2)}, u32[]{:S(2)}) %collective-permute-start.19) | collective-permute-done | bytes 49184 | tf_op jit(solution)/shard_map/ppermute | solution.py:45
  85.9 5.8 %collective-permute-start.21 = (f32[96,128]{1,0:T(8,128)S(1)}, f32[96,128]{1,0:T(8,128)S(1)}, u32[]{:S(2)}, u32[]{:S(2)}) collective-permute-start(f32[96,128]{1,0:T(8,128)S(1)} %add_add_fusion.2), channel_id=1, source_target_pairs={{0,16},{1,17},{2,18},{3,19},{4,20},{5,21},{6,22},{7,23},{8,24},{9,... | collective-permute-start | bytes 147464 | tf_op jit(solution)/shard_map/ppermute | solution.py:45
  91.6 1.7 %collective-permute-done.21 = f32[96,128]{1,0:T(8,128)S(1)} collective-permute-done((f32[96,128]{1,0:T(8,128)S(1)}, f32[96,128]{1,0:T(8,128)S(1)}, u32[]{:S(2)}, u32[]{:S(2)}) %collective-permute-start.21) | collective-permute-done | bytes 49184 | tf_op jit(solution)/shard_map/ppermute | solution.py:45
  93.4 2.3 %collective-permute-done.22 = f32[96,128]{1,0:T(8,128)S(1)} collective-permute-done((f32[96,128]{1,0:T(8,128)S(1)}, f32[96,128]{1,0:T(8,128)S(1)}, u32[]{:S(2)}, u32[]{:S(2)}) %collective-permute-start.22) | collective-permute-done | bytes 49184 | tf_op jit(solution)/shard_map/ppermute | solution.py:45
  95.7 0.3 collective-permute-start.23
  96.0 0.4 collective-permute-start.24
  96.4 2.8 %collective-permute-start.25 = (f32[96,128]{1,0:T(8,128)S(1)}, f32[96,128]{1,0:T(8,128)S(1)}, u32[]{:S(2)}, u32[]{:S(2)}) collective-permute-start(f32[96,128]{1,0:T(8,128)S(1)} %add_add_fusion.1), channel_id=1, source_target_pairs={{0,65},{1,64},{2,67},{3,66},{4,69},{5,68},{6,71},{7,70},{8,73},{9,... | collective-permute-start | bytes 147464 | tf_op jit(solution)/shard_map/ppermute | solution.py:45
  99.2 2.3 %collective-permute-done.23 = f32[96,128]{1,0:T(8,128)S(1)} collective-permute-done((f32[96,128]{1,0:T(8,128)S(1)}, f32[96,128]{1,0:T(8,128)S(1)}, u32[]{:S(2)}, u32[]{:S(2)}) %collective-permute-start.23) | collective-permute-done | bytes 49184 | tf_op jit(solution)/shard_map/ppermute | solution.py:45
  101.5 0.3 collective-permute-done.24
  101.9 2.8 %collective-permute-start.27 = (f32[96,128]{1,0:T(8,128)S(1)}, f32[96,128]{1,0:T(8,128)S(1)}, u32[]{:S(2)}, u32[]{:S(2)}) collective-permute-start(f32[96,128]{1,0:T(8,128)S(1)} %add_add_fusion), channel_id=1, source_target_pairs={{0,4},{1,5},{2,6},{3,7},{4,0},{5,1},{6,2},{7,3},{8,12},{9,13},{10,... | collective-permute-start | bytes 147464 | tf_op jit(solution)/shard_map/ppermute | solution.py:45
  104.8 0.5 collective-permute-start.28
  105.2 2.5 %collective-permute-done.26 = f32[96,128]{1,0:T(8,128)S(1)} collective-permute-done((f32[96,128]{1,0:T(8,128)S(1)}, f32[96,128]{1,0:T(8,128)S(1)}, u32[]{:S(2)}, u32[]{:S(2)}) %collective-permute-start.26) | collective-permute-done | bytes 49184 | tf_op jit(solution)/shard_map/ppermute | solution.py:45
  107.7 1.1 collective-permute-done.28
  108.9 7.8 %shard_map.64.mine_ref = f32[2,192,192]{2,1,0:T(8,128)S(1)} custom-call(s32[3]{0:T(128)S(1)} %pad_add_fusion.place_ref, f32[4,96,128]{2,1,0:T(8,128)S(1)} %pad_maximum_fusion.own_ref), custom_call_target="tpu_custom_call" | custom-call | flops 113246208 | bytes 196624 | tf_op jit(solution)/shard_map/pallas_call | solution.py:371
  116.8 1.7 %collective-permute-done.29.other_ref = f32[2,192,192]{2,1,0:T(8,128)S(1)} collective-permute-done((f32[2,192,192]{2,1,0:T(8,128)S(1)}, f32[2,192,192]{2,1,0:T(8,128)S(1)}, u32[]{:S(2)}, u32[]{:S(2)}) %collective-permute-start.29) | collective-permute-done | bytes 294944 | tf_op jit(solution)/shard_map/ppermute | solution.py:45
  118.5 1.7 %shard_map.65 = (f32[4,3,24,128]{3,2,1,0:T(8,128)S(1)}, f32[4,3,24,128]{3,2,1,0:T(8,128)S(1)}, f32[4,3,24,128]{3,2,1,0:T(8,128)S(1)}, f32[4,3,24,128]{3,2,1,0:T(...) custom-call(s32[3]{0:T(128)S(1)} %pad_add_fusion.place_ref, ...), custom_call_target="tpu_custom_call" | custom-call | flops 679477248 | bytes 1769488 | tf_op jit(solution)/shard_map/pallas_call | solution.py:371
  120.2 3.3 %collective-permute-start.30 = (f32[4,3,24,128]{3,2,1,0:T(8,128)S(1)}, f32[4,3,24,128]{3,2,1,0:T(8,128)S(1)}, u32[]{:S(2)}, u32[]{:S(2)}) collective-permute-start(f32[4,3,24,128]{3,2,1,0:T(8,128)S(1)} %get-tuple-element.63), channel_id=1, source_target_pairs={{0,7},{1,6},{2,5},{3,4},{4,3},{5,2},{6,1},{7,0},{8,15},{9,14},{10,... | collective-permute-start | bytes 442376 | tf_op jit(solution)/shard_map/ppermute | solution.py:454
  123.5 2.4 %collective-permute-start.31 = (f32[4,3,24,128]{3,2,1,0:T(8,128)S(1)}, f32[4,3,24,128]{3,2,1,0:T(8,128)S(1)}, u32[]{:S(2)}, u32[]{:S(2)}) collective-permute-start(f32[4,3,24,128]{3,2,1,0:T(8,128)S(1)} %get-tuple-element.64), channel_id=1, source_target_pairs={{0,5},{1,4},{2,7},{3,6},{4,1},{5,0},{6,3},{7,2},{8,13},{9,12},{10,... | collective-permute-start | bytes 442376 | tf_op jit(solution)/shard_map/ppermute | solution.py:454
  126.0 1.9 %collective-permute-start.32 = (f32[4,3,24,128]{3,2,1,0:T(8,128)S(1)}, f32[4,3,24,128]{3,2,1,0:T(8,128)S(1)}, u32[]{:S(2)}, u32[]{:S(2)}) collective-permute-start(f32[4,3,24,128]{3,2,1,0:T(8,128)S(1)} %get-tuple-element.65), channel_id=1, source_target_pairs={{0,3},{1,2},{2,1},{3,0},{4,7},{5,6},{6,5},{7,4},{8,11},{9,10},{10,... | collective-permute-start | bytes 442376 | tf_op jit(solution)/shard_map/ppermute | solution.py:454
  127.8 1.5 %collective-permute-start.33 = (f32[4,3,24,128]{3,2,1,0:T(8,128)S(1)}, f32[4,3,24,128]{3,2,1,0:T(8,128)S(1)}, u32[]{:S(2)}, u32[]{:S(2)}) collective-permute-start(f32[4,3,24,128]{3,2,1,0:T(8,128)S(1)} %get-tuple-element.66), channel_id=1, source_target_pairs={{0,4},{1,5},{2,6},{3,7},{4,0},{5,1},{6,2},{7,3},{8,12},{9,13},{10,... | collective-permute-start | bytes 442376 | tf_op jit(solution)/shard_map/ppermute | solution.py:454
  129.3 1.9 %collective-permute-start.34 = (f32[4,3,24,128]{3,2,1,0:T(8,128)S(1)}, f32[4,3,24,128]{3,2,1,0:T(8,128)S(1)}, u32[]{:S(2)}, u32[]{:S(2)}) collective-permute-start(f32[4,3,24,128]{3,2,1,0:T(8,128)S(1)} %get-tuple-element.67), channel_id=1, source_target_pairs={{0,1},{1,0},{2,3},{3,2},{4,5},{5,4},{6,7},{7,6},{8,9},{9,8},{10,11... | collective-permute-start | bytes 442376 | tf_op jit(solution)/shard_map/ppermute | solution.py:454
  131.2 5.6 %collective-permute-start.35 = (f32[4,3,24,128]{3,2,1,0:T(8,128)S(1)}, f32[4,3,24,128]{3,2,1,0:T(8,128)S(1)}, u32[]{:S(2)}, u32[]{:S(2)}) collective-permute-start(f32[4,3,24,128]{3,2,1,0:T(8,128)S(1)} %get-tuple-element.68), channel_id=1, source_target_pairs={{0,6},{1,7},{2,4},{3,5},{4,2},{5,3},{6,0},{7,1},{8,14},{9,15},{10,... | collective-permute-start | bytes 442376 | tf_op jit(solution)/shard_map/ppermute | solution.py:454
  136.8 1.8 %shard_map.67 = f32[2,24,192]{2,1,0:T(8,128)} custom-call(s32[3]{0:T(128)S(1)} %pad_add_fusion.place_ref, f32[2,192,192]{2,1,0:T(8,128)S(1)} %shard_map.64.mine_ref, f32[2,192,192]{2,1,0:T(8,128)S(1)} %collective-permute-done.29.other_ref), custom_call_target="tpu_custom_call" | custom-call | flops 113246208 | bytes 589840 | tf_op jit(solution)/shard_map/pallas_call | solution.py:371
  138.6 1.8 %collective-permute-done.33.refs_4_ = f32[4,3,24,128]{3,2,1,0:T(8,128)S(1)} collective-permute-done((f32[4,3,24,128]{3,2,1,0:T(8,128)S(1)}, f32[4,3,24,128]{3,2,1,0:T(8,128)S(1)}, u32[]{:S(2)}, u32[]{:S(2)}) %collective-permute-start.33) | collective-permute-done | bytes 147488 | tf_op jit(solution)/shard_map/ppermute | solution.py:454
  140.4 0.8 collective-permute-done.35.refs_6_
  141.2 0.8 collective-permute-done.36.refs_7_
  142.0 2.4 %shard_map.66 = f32[2304,128]{1,0:T(8,128)} custom-call(s32[3]{0:T(128)S(1)} %pad_add_fusion.place_ref, f32[4,3,24,128]{3,2,1,0:T(8,128)S(1)} %get-tuple-element.62.refs_0_, f32[4,3,24,128]{3,2,1,0:T(8,128)S(1)} %collective-permute-done.30.refs_1_, f32[4,3,24,128]{3,2,1,0:T(8,128)S(1)} %collective-permute-done.31.refs_2_, ...), custom_call_target="tpu_custom_call" | custom-call | bytes 1179664 | tf_op jit(solution)/shard_map/pallas_call | solution.py:371
  (52 shorter events, 0.8 us)
Async XLA Ops:
  2.0 14.6 %copy-start.1 = (s32[1,4096]{1,0:T(1,128)S(1)}, s32[1,4096]{1,0:T(1,128)}, u32[]{:S(2)}) copy-start(s32[1,4096]{1,0:T(1,128)} %param.5) | copy-start | bytes 49156
  2.0 21.7 %copy-start.2 = (f32[4,3,3,3]{3,0,2,1:T(4,128)S(1)}, f32[4,3,3,3]{3,0,2,1:T(4,128)}, u32[]{:S(2)}) copy-start(f32[4,3,3,3]{3,0,2,1:T(4,128)} %param.6) | copy-start | bytes 1300
  3.4 41.3 %copy-start = (f32[4]{0:T(128)S(1)}, f32[4]{0:T(128)}, u32[]{:S(2)}) copy-start(f32[4]{0:T(128)} %refs_1_.1) | copy-start | bytes 52
  3.4 13.2 %collective-permute-start.1 = (f32[4,3,24,128]{3,2,1,0:T(8,128)S(1)}, f32[4,3,24,128]{3,2,1,0:T(8,128)S(1)}, u32[]{:S(2)}, u32[]{:S(2)}) collective-permute-start(f32[4,3,24,128]{3,2,1,0:T(8,128)S(1)} %get-tuple-element.38), channel_id=1, source_target_pairs={{0,7},{1,6},{2,5},{3,4},{4,3},{5,2},{6,1},{7,0},{8,15},{9,14},{10,... | collective-permute-start | bytes 442376 | tf_op jit(solution)/shard_map/ppermute | solution.py:454
  9.6 11.7 %collective-permute-start.2 = (f32[4,3,24,128]{3,2,1,0:T(8,128)S(1)}, f32[4,3,24,128]{3,2,1,0:T(8,128)S(1)}, u32[]{:S(2)}, u32[]{:S(2)}) collective-permute-start(f32[4,3,24,128]{3,2,1,0:T(8,128)S(1)} %get-tuple-element.39), channel_id=1, source_target_pairs={{0,5},{1,4},{2,7},{3,6},{4,1},{5,0},{6,3},{7,2},{8,13},{9,12},{10,... | collective-permute-start | bytes 442376 | tf_op jit(solution)/shard_map/ppermute | solution.py:454
  9.9 11.9 %collective-permute-start.3 = (f32[4,3,24,128]{3,2,1,0:T(8,128)S(1)}, f32[4,3,24,128]{3,2,1,0:T(8,128)S(1)}, u32[]{:S(2)}, u32[]{:S(2)}) collective-permute-start(f32[4,3,24,128]{3,2,1,0:T(8,128)S(1)} %get-tuple-element.40), channel_id=1, source_target_pairs={{0,3},{1,2},{2,1},{3,0},{4,7},{5,6},{6,5},{7,4},{8,11},{9,10},{10,... | collective-permute-start | bytes 442376 | tf_op jit(solution)/shard_map/ppermute | solution.py:454
  13.3 12.1 %collective-permute-start.4 = (f32[4,3,24,128]{3,2,1,0:T(8,128)S(1)}, f32[4,3,24,128]{3,2,1,0:T(8,128)S(1)}, u32[]{:S(2)}, u32[]{:S(2)}) collective-permute-start(f32[4,3,24,128]{3,2,1,0:T(8,128)S(1)} %get-tuple-element.41), channel_id=1, source_target_pairs={{0,4},{1,5},{2,6},{3,7},{4,0},{5,1},{6,2},{7,3},{8,12},{9,13},{10,... | collective-permute-start | bytes 442376 | tf_op jit(solution)/shard_map/ppermute | solution.py:454
  16.3 9.1 %collective-permute-start.5 = (f32[4,3,24,128]{3,2,1,0:T(8,128)S(1)}, f32[4,3,24,128]{3,2,1,0:T(8,128)S(1)}, u32[]{:S(2)}, u32[]{:S(2)}) collective-permute-start(f32[4,3,24,128]{3,2,1,0:T(8,128)S(1)} %get-tuple-element.42), channel_id=1, source_target_pairs={{0,1},{1,0},{2,3},{3,2},{4,5},{5,4},{6,7},{7,6},{8,9},{9,8},{10,11... | collective-permute-start | bytes 442376 | tf_op jit(solution)/shard_map/ppermute | solution.py:454
  16.6 8.8 %collective-permute-start.6 = (f32[4,3,24,128]{3,2,1,0:T(8,128)S(1)}, f32[4,3,24,128]{3,2,1,0:T(8,128)S(1)}, u32[]{:S(2)}, u32[]{:S(2)}) collective-permute-start(f32[4,3,24,128]{3,2,1,0:T(8,128)S(1)} %get-tuple-element.43), channel_id=1, source_target_pairs={{0,6},{1,7},{2,4},{3,5},{4,2},{5,3},{6,0},{7,1},{8,14},{9,15},{10,... | collective-permute-start | bytes 442376 | tf_op jit(solution)/shard_map/ppermute | solution.py:454
  21.3 5.1 %collective-permute-start.7 = (f32[4,3,24,128]{3,2,1,0:T(8,128)S(1)}, f32[4,3,24,128]{3,2,1,0:T(8,128)S(1)}, u32[]{:S(2)}, u32[]{:S(2)}) collective-permute-start(f32[4,3,24,128]{3,2,1,0:T(8,128)S(1)} %get-tuple-element.44), channel_id=1, source_target_pairs={{0,2},{1,3},{2,0},{3,1},{4,6},{5,7},{6,4},{7,5},{8,10},{9,11},{10,... | collective-permute-start | bytes 442376 | tf_op jit(solution)/shard_map/ppermute | solution.py:454
  21.8 9.1 %collective-permute-start = (s32[1,4096]{1,0:T(1,128)S(1)}, s32[1,4096]{1,0:T(1,128)S(1)}, u32[]{:S(2)}, u32[]{:S(2)}) collective-permute-start(s32[1,4096]{1,0:T(1,128)S(1)} %copy-done.1), channel_id=1, source_target_pairs={{0,8},{8,16},{16,24},{24,32},{32,40},{40,48},{48,56},{56,64},{64,7... | collective-permute-start | bytes 49160 | tf_op jit(solution)/shard_map/ppermute | solution.py:51
  27.2 17.5 %collective-permute-start.10 = (f32[8,4,3,24,128]{4,3,2,1,0:T(8,128)S(1)}, f32[8,4,3,24,128]{4,3,2,1,0:T(8,128)S(1)}, u32[]{:S(2)}, u32[]{:S(2)}) collective-permute-start(f32[8,4,3,24,128]{4,3,2,1,0:T(8,128)S(1)} %get-tuple-element.45.u_ref.b_ref), channel_id=1, source_target_pairs={{8,16},{16,8},{24,32},{32,24},{40,48},{48,40},{56,64},{64,56},{72,... | collective-permute-start | bytes 3538952 | tf_op jit(solution)/shard_map/ppermute | solution.py:460
  29.1 15.6 %collective-permute-start.11 = (f32[8,4,3,24,128]{4,3,2,1,0:T(8,128)S(1)}, f32[8,4,3,24,128]{4,3,2,1,0:T(8,128)S(1)}, u32[]{:S(2)}, u32[]{:S(2)}) collective-permute-start(f32[8,4,3,24,128]{4,3,2,1,0:T(8,128)S(1)} %get-tuple-element.45.u_ref.b_ref), channel_id=1, source_target_pairs={{0,8},{8,0},{16,24},{24,16},{32,40},{40,32},{48,56},{56,48},{64,72... | collective-permute-start | bytes 3538952 | tf_op jit(solution)/shard_map/ppermute | solution.py:461
  30.9 5.2 %collective-permute-start.8 = (f32[4,3,24,128]{3,2,1,0:T(8,128)S(1)}, f32[4,3,24,128]{3,2,1,0:T(8,128)S(1)}, u32[]{:S(2)}, u32[]{:S(2)}) collective-permute-start(f32[4,3,24,128]{3,2,1,0:T(8,128)S(1)} %get-tuple-element.46), channel_id=1, source_target_pairs={{0,2},{2,4},{4,6},{6,7},{7,5},{5,3},{3,1},{8,10},{10,12},{12,14},{... | collective-permute-start | bytes 442376 | tf_op jit(solution)/shard_map/ppermute | solution.py:51
  32.8 7.4 %collective-permute-start.9 = (f32[4,3,24,128]{3,2,1,0:T(8,128)S(1)}, f32[4,3,24,128]{3,2,1,0:T(8,128)S(1)}, u32[]{:S(2)}, u32[]{:S(2)}) collective-permute-start(f32[4,3,24,128]{3,2,1,0:T(8,128)S(1)} %get-tuple-element.47), channel_id=1, source_target_pairs={{2,0},{4,2},{6,4},{7,6},{5,7},{3,5},{1,3},{10,8},{12,10},{14,12},{... | collective-permute-start | bytes 442376 | tf_op jit(solution)/shard_map/ppermute | solution.py:51
  48.3 17.5 %collective-permute-start.14 = (f32[8,4,3,24,128]{4,3,2,1,0:T(8,128)S(1)}, f32[8,4,3,24,128]{4,3,2,1,0:T(8,128)S(1)}, u32[]{:S(2)}, u32[]{:S(2)}) collective-permute-start(f32[8,4,3,24,128]{4,3,2,1,0:T(8,128)S(1)} %get-tuple-element.48.a_ref.refs_3_), channel_id=1, source_target_pairs={{8,16},{16,8},{24,32},{32,24},{40,48},{48,40},{56,64},{64,56},{72,... | collective-permute-start | bytes 3538952 | tf_op jit(solution)/shard_map/ppermute | solution.py:460
  50.3 15.6 %collective-permute-start.15 = (f32[8,4,3,24,128]{4,3,2,1,0:T(8,128)S(1)}, f32[8,4,3,24,128]{4,3,2,1,0:T(8,128)S(1)}, u32[]{:S(2)}, u32[]{:S(2)}) collective-permute-start(f32[8,4,3,24,128]{4,3,2,1,0:T(8,128)S(1)} %get-tuple-element.48.a_ref.refs_3_), channel_id=1, source_target_pairs={{0,8},{8,0},{16,24},{24,16},{32,40},{40,32},{48,56},{56,48},{64,72... | collective-permute-start | bytes 3538952 | tf_op jit(solution)/shard_map/ppermute | solution.py:461
  52.0 5.7 %collective-permute-start.12 = (f32[4,3,24,128]{3,2,1,0:T(8,128)S(1)}, f32[4,3,24,128]{3,2,1,0:T(8,128)S(1)}, u32[]{:S(2)}, u32[]{:S(2)}) collective-permute-start(f32[4,3,24,128]{3,2,1,0:T(8,128)S(1)} %get-tuple-element.49), channel_id=1, source_target_pairs={{0,2},{2,4},{4,6},{6,7},{7,5},{5,3},{3,1},{8,10},{10,12},{12,14},{... | collective-permute-start | bytes 442376 | tf_op jit(solution)/shard_map/ppermute | solution.py:51
  53.9 7.4 %collective-permute-start.13 = (f32[4,3,24,128]{3,2,1,0:T(8,128)S(1)}, f32[4,3,24,128]{3,2,1,0:T(8,128)S(1)}, u32[]{:S(2)}, u32[]{:S(2)}) collective-permute-start(f32[4,3,24,128]{3,2,1,0:T(8,128)S(1)} %get-tuple-element.50), channel_id=1, source_target_pairs={{2,0},{4,2},{6,4},{7,6},{5,7},{3,5},{1,3},{10,8},{12,10},{14,12},{... | collective-permute-start | bytes 442376 | tf_op jit(solution)/shard_map/ppermute | solution.py:51
  71.5 1.5 %collective-permute-start.16 = (f32[384,128]{1,0:T(8,128)S(1)}, f32[384,128]{1,0:T(8,128)S(1)}, u32[]{:S(2)}, u32[]{:S(2)}) collective-permute-start(f32[384,128]{1,0:T(8,128)S(1)} %get-tuple-element.52), channel_id=1, source_target_pairs={{0,8},{1,9},{2,10},{3,11},{4,12},{5,13},{6,14},{7,15},{8,0},{9,1},... | collective-permute-start | bytes 589832 | tf_op jit(solution)/shard_map/ppermute | solution.py:45
  73.1 8.6 %collective-permute-start.17 = (f32[96,128]{1,0:T(8,128)S(1)}, f32[96,128]{1,0:T(8,128)S(1)}, u32[]{:S(2)}, u32[]{:S(2)}) collective-permute-start(f32[96,128]{1,0:T(8,128)S(1)} %get-tuple-element.76), channel_id=1, source_target_pairs={{0,4},{1,5},{2,6},{3,7},{4,0},{5,1},{6,2},{7,3},{8,12},{9,13},{10,... | collective-permute-start | bytes 147464 | tf_op jit(solution)/shard_map/ppermute | solution.py:45
  78.3 5.3 %collective-permute-start.18 = (f32[96,128]{1,0:T(8,128)S(1)}, f32[96,128]{1,0:T(8,128)S(1)}, u32[]{:S(2)}, u32[]{:S(2)}) collective-permute-start(f32[96,128]{1,0:T(8,128)S(1)} %get-tuple-element.78), channel_id=1, source_target_pairs={{0,2},{1,3},{2,4},{3,5},{4,6},{5,7},{6,0},{7,1},{8,10},{9,11},{10,... | collective-permute-start | bytes 147464 | tf_op jit(solution)/shard_map/ppermute | solution.py:45
  81.7 4.1 %collective-permute-start.19 = (f32[96,128]{1,0:T(8,128)S(1)}, f32[96,128]{1,0:T(8,128)S(1)}, u32[]{:S(2)}, u32[]{:S(2)}) collective-permute-start(f32[96,128]{1,0:T(8,128)S(1)} %get-tuple-element.77), channel_id=1, source_target_pairs={{0,6},{1,7},{2,0},{3,1},{4,2},{5,3},{6,4},{7,5},{8,14},{9,15},{10,... | collective-permute-start | bytes 147464 | tf_op jit(solution)/shard_map/ppermute | solution.py:45
  85.8 5.9 %collective-permute-start.20 = (f32[96,128]{1,0:T(8,128)S(1)}, f32[96,128]{1,0:T(8,128)S(1)}, u32[]{:S(2)}, u32[]{:S(2)}) collective-permute-start(f32[96,128]{1,0:T(8,128)S(1)} %add_add_fusion.2), channel_id=1, source_target_pairs={{0,32},{1,33},{2,34},{3,35},{4,36},{5,37},{6,38},{7,39},{8,40},{9,... | collective-permute-start | bytes 147464 | tf_op jit(solution)/shard_map/ppermute | solution.py:45
  85.9 7.5 %collective-permute-start.21 = (f32[96,128]{1,0:T(8,128)S(1)}, f32[96,128]{1,0:T(8,128)S(1)}, u32[]{:S(2)}, u32[]{:S(2)}) collective-permute-start(f32[96,128]{1,0:T(8,128)S(1)} %add_add_fusion.2), channel_id=1, source_target_pairs={{0,16},{1,17},{2,18},{3,19},{4,20},{5,21},{6,22},{7,23},{8,24},{9,... | collective-permute-start | bytes 147464 | tf_op jit(solution)/shard_map/ppermute | solution.py:45
  91.6 4.1 %collective-permute-start.22 = (f32[96,128]{1,0:T(8,128)S(1)}, f32[96,128]{1,0:T(8,128)S(1)}, u32[]{:S(2)}, u32[]{:S(2)}) collective-permute-start(f32[96,128]{1,0:T(8,128)S(1)} %add_add_fusion.2), channel_id=1, source_target_pairs={{0,48},{1,49},{2,50},{3,51},{4,52},{5,53},{6,54},{7,55},{8,56},{9,... | collective-permute-start | bytes 147464 | tf_op jit(solution)/shard_map/ppermute | solution.py:45
  95.7 5.8 %collective-permute-start.23 = (f32[96,128]{1,0:T(8,128)S(1)}, f32[96,128]{1,0:T(8,128)S(1)}, u32[]{:S(2)}, u32[]{:S(2)}) collective-permute-start(f32[96,128]{1,0:T(8,128)S(1)} %add_add_fusion.1), channel_id=1, source_target_pairs={{0,1},{1,0},{2,3},{3,2},{4,5},{5,4},{6,7},{7,6},{8,9},{9,8},{10,11... | collective-permute-start | bytes 147464 | tf_op jit(solution)/shard_map/ppermute | solution.py:45
  96.0 5.8 %collective-permute-start.24 = (f32[96,128]{1,0:T(8,128)S(1)}, f32[96,128]{1,0:T(8,128)S(1)}, u32[]{:S(2)}, u32[]{:S(2)}) collective-permute-start(f32[96,128]{1,0:T(8,128)S(1)} %add_add_fusion.1), channel_id=1, source_target_pairs={{0,64},{1,65},{2,66},{3,67},{4,68},{5,69},{6,70},{7,71},{8,72},{9,... | collective-permute-start | bytes 147464 | tf_op jit(solution)/shard_map/ppermute | solution.py:45
  96.4 5.4 %collective-permute-start.25 = (f32[96,128]{1,0:T(8,128)S(1)}, f32[96,128]{1,0:T(8,128)S(1)}, u32[]{:S(2)}, u32[]{:S(2)}) collective-permute-start(f32[96,128]{1,0:T(8,128)S(1)} %add_add_fusion.1), channel_id=1, source_target_pairs={{0,65},{1,64},{2,67},{3,66},{4,69},{5,68},{6,71},{7,70},{8,73},{9,... | collective-permute-start | bytes 147464 | tf_op jit(solution)/shard_map/ppermute | solution.py:45
  101.8 5.9 %collective-permute-start.26 = (f32[96,128]{1,0:T(8,128)S(1)}, f32[96,128]{1,0:T(8,128)S(1)}, u32[]{:S(2)}, u32[]{:S(2)}) collective-permute-start(f32[96,128]{1,0:T(8,128)S(1)} %add_add_fusion), channel_id=1, source_target_pairs={{0,2},{1,3},{2,4},{3,5},{4,6},{5,7},{6,0},{7,1},{8,10},{9,11},{10,... | collective-permute-start | bytes 147464 | tf_op jit(solution)/shard_map/ppermute | solution.py:45
  101.9 5.8 %collective-permute-start.27 = (f32[96,128]{1,0:T(8,128)S(1)}, f32[96,128]{1,0:T(8,128)S(1)}, u32[]{:S(2)}, u32[]{:S(2)}) collective-permute-start(f32[96,128]{1,0:T(8,128)S(1)} %add_add_fusion), channel_id=1, source_target_pairs={{0,4},{1,5},{2,6},{3,7},{4,0},{5,1},{6,2},{7,3},{8,12},{9,13},{10,... | collective-permute-start | bytes 147464 | tf_op jit(solution)/shard_map/ppermute | solution.py:45
  104.8 4.1 %collective-permute-start.28 = (f32[96,128]{1,0:T(8,128)S(1)}, f32[96,128]{1,0:T(8,128)S(1)}, u32[]{:S(2)}, u32[]{:S(2)}) collective-permute-start(f32[96,128]{1,0:T(8,128)S(1)} %add_add_fusion), channel_id=1, source_target_pairs={{0,6},{1,7},{2,0},{3,1},{4,2},{5,3},{6,4},{7,5},{8,14},{9,15},{10,... | collective-permute-start | bytes 147464 | tf_op jit(solution)/shard_map/ppermute | solution.py:45
  116.7 1.8 %collective-permute-start.29 = (f32[2,192,192]{2,1,0:T(8,128)S(1)}, f32[2,192,192]{2,1,0:T(8,128)S(1)}, u32[]{:S(2)}, u32[]{:S(2)}) collective-permute-start(f32[2,192,192]{2,1,0:T(8,128)S(1)} %shard_map.64.mine_ref), channel_id=1, source_target_pairs={{0,8},{1,9},{2,10},{3,11},{4,12},{5,13},{6,14},{7,15},{8,0},{9,1},... | collective-permute-start | bytes 884744 | tf_op jit(solution)/shard_map/ppermute | solution.py:45
  120.2 11.1 %collective-permute-start.30 = (f32[4,3,24,128]{3,2,1,0:T(8,128)S(1)}, f32[4,3,24,128]{3,2,1,0:T(8,128)S(1)}, u32[]{:S(2)}, u32[]{:S(2)}) collective-permute-start(f32[4,3,24,128]{3,2,1,0:T(8,128)S(1)} %get-tuple-element.63), channel_id=1, source_target_pairs={{0,7},{1,6},{2,5},{3,4},{4,3},{5,2},{6,1},{7,0},{8,15},{9,14},{10,... | collective-permute-start | bytes 442376 | tf_op jit(solution)/shard_map/ppermute | solution.py:454
  123.5 13.3 %collective-permute-start.31 = (f32[4,3,24,128]{3,2,1,0:T(8,128)S(1)}, f32[4,3,24,128]{3,2,1,0:T(8,128)S(1)}, u32[]{:S(2)}, u32[]{:S(2)}) collective-permute-start(f32[4,3,24,128]{3,2,1,0:T(8,128)S(1)} %get-tuple-element.64), channel_id=1, source_target_pairs={{0,5},{1,4},{2,7},{3,6},{4,1},{5,0},{6,3},{7,2},{8,13},{9,12},{10,... | collective-permute-start | bytes 442376 | tf_op jit(solution)/shard_map/ppermute | solution.py:454
  126.0 12.6 %collective-permute-start.32 = (f32[4,3,24,128]{3,2,1,0:T(8,128)S(1)}, f32[4,3,24,128]{3,2,1,0:T(8,128)S(1)}, u32[]{:S(2)}, u32[]{:S(2)}) collective-permute-start(f32[4,3,24,128]{3,2,1,0:T(8,128)S(1)} %get-tuple-element.65), channel_id=1, source_target_pairs={{0,3},{1,2},{2,1},{3,0},{4,7},{5,6},{6,5},{7,4},{8,11},{9,10},{10,... | collective-permute-start | bytes 442376 | tf_op jit(solution)/shard_map/ppermute | solution.py:454
  127.8 12.6 %collective-permute-start.33 = (f32[4,3,24,128]{3,2,1,0:T(8,128)S(1)}, f32[4,3,24,128]{3,2,1,0:T(8,128)S(1)}, u32[]{:S(2)}, u32[]{:S(2)}) collective-permute-start(f32[4,3,24,128]{3,2,1,0:T(8,128)S(1)} %get-tuple-element.66), channel_id=1, source_target_pairs={{0,4},{1,5},{2,6},{3,7},{4,0},{5,1},{6,2},{7,3},{8,12},{9,13},{10,... | collective-permute-start | bytes 442376 | tf_op jit(solution)/shard_map/ppermute | solution.py:454
  129.3 11.1 %collective-permute-start.34 = (f32[4,3,24,128]{3,2,1,0:T(8,128)S(1)}, f32[4,3,24,128]{3,2,1,0:T(8,128)S(1)}, u32[]{:S(2)}, u32[]{:S(2)}) collective-permute-start(f32[4,3,24,128]{3,2,1,0:T(8,128)S(1)} %get-tuple-element.67), channel_id=1, source_target_pairs={{0,1},{1,0},{2,3},{3,2},{4,5},{5,4},{6,7},{7,6},{8,9},{9,8},{10,11... | collective-permute-start | bytes 442376 | tf_op jit(solution)/shard_map/ppermute | solution.py:454
  131.2 10.0 %collective-permute-start.35 = (f32[4,3,24,128]{3,2,1,0:T(8,128)S(1)}, f32[4,3,24,128]{3,2,1,0:T(8,128)S(1)}, u32[]{:S(2)}, u32[]{:S(2)}) collective-permute-start(f32[4,3,24,128]{3,2,1,0:T(8,128)S(1)} %get-tuple-element.68), channel_id=1, source_target_pairs={{0,6},{1,7},{2,4},{3,5},{4,2},{5,3},{6,0},{7,1},{8,14},{9,15},{10,... | collective-permute-start | bytes 442376 | tf_op jit(solution)/shard_map/ppermute | solution.py:454
  136.8 5.1 %collective-permute-start.36 = (f32[4,3,24,128]{3,2,1,0:T(8,128)S(1)}, f32[4,3,24,128]{3,2,1,0:T(8,128)S(1)}, u32[]{:S(2)}, u32[]{:S(2)}) collective-permute-start(f32[4,3,24,128]{3,2,1,0:T(8,128)S(1)} %get-tuple-element.69), channel_id=1, source_target_pairs={{0,2},{1,3},{2,0},{3,1},{4,6},{5,7},{6,4},{7,5},{8,10},{9,11},{10,... | collective-permute-start | bytes 442376 | tf_op jit(solution)/shard_map/ppermute | solution.py:454
